TPU v7x, 32 devices: a whole 2x2x4 slice. The times are simulated.
32 devices in a mesh: dp: 8 (over z, y), seq: 4 (over x, core).
Axes of the slice: x: 2, y: 2, z: 4, core: 2. Of those that a mesh axis runs over, the one named last changes fastest.
Arguments:
- token_ids: int32 [8192], replicated, may hold values from 0 to 50687
- targets: int32 [8192], P('dp'), may hold values from 0 to 50687
- loss_mask: int32 [8192], P('dp'), may hold values from 0 to 1
- square_weights: float32 [2, 5, 768, 768], P(None, None, ('dp', 'seq')), may hold values from -0.21875 to 0.21875
- expand_weights: float32 [2, 768, 3072], P(None, ('dp', 'seq')), may hold values from -0.21875 to 0.21875
- shrink_weights: float32 [2, 3072, 768], P(None, ('dp', 'seq')), may hold values from -0.109375 to 0.109375
- vector_params: float32 [26, 768], P(None, ('dp', 'seq')), as said below
- embed_table: float32 [768, 50688], P(('dp', 'seq')), may hold values from -6 to 6
- head_table: float32 [768, 50688], P('dp', 'seq')
- square_first: float32 [2, 5, 768, 768], P(None, None, ('dp', 'seq')), may hold values from -3.5762787e-07 to 3.5762787e-07
- expand_first: float32 [2, 768, 3072], P(None, ('dp', 'seq')), may hold values from -3.5762787e-07 to 3.5762787e-07
- shrink_first: float32 [2, 3072, 768], P(None, ('dp', 'seq')), may hold values from -3.5762787e-07 to 3.5762787e-07
- vector_first: float32 [26, 768], P(None, ('dp', 'seq')), may hold values from -1.4305115e-06 to 1.4305115e-06
- embed_first: float32 [768, 50688], P(('dp', 'seq')), may hold values from -1.8626451e-08 to 1.8626451e-08
- head_first: float32 [768, 50688], P('dp', 'seq'), may hold values from -3.5762787e-07 to 3.5762787e-07
- square_second: float32 [2, 5, 768, 768], P(None, None, ('dp', 'seq')), may hold values from 1.6369956e-16 to 2.619193e-15
- expand_second: float32 [2, 768, 3072], P(None, ('dp', 'seq')), may hold values from 1.6369956e-16 to 2.619193e-15
- shrink_second: float32 [2, 3072, 768], P(None, ('dp', 'seq')), may hold values from 1.6369956e-16 to 2.619193e-15
- vector_second: float32 [26, 768], P(None, ('dp', 'seq')), may hold values from 2.619193e-15 to 4.1907087e-14
- embed_second: float32 [768, 50688], P(('dp', 'seq')), may hold values from 8.184978e-18 to 1.3095964e-16
- head_second: float32 [768, 50688], P('dp', 'seq'), may hold values from 1.6369956e-16 to 2.619193e-15
Outputs:
- loss_sum: float32 [], replicated
- grad_norm: float32 [], replicated
- square_out: float32 [2, 5, 768, 768], P(None, None, ('dp', 'seq'))
- expand_out: float32 [2, 768, 3072], P(None, ('dp', 'seq'))
- shrink_out: float32 [2, 3072, 768], P(None, ('dp', 'seq'))
- vector_out: float32 [26, 768], P(None, ('dp', 'seq'))
- embed_out: float32 [768, 50688], P(('dp', 'seq'))
- head_out: float32 [768, 50688], P('dp', 'seq')
- square_first_out: float32 [2, 5, 768, 768], P(None, None, ('dp', 'seq'))
- expand_first_out: float32 [2, 768, 3072], P(None, ('dp', 'seq'))
- shrink_first_out: float32 [2, 3072, 768], P(None, ('dp', 'seq'))
- vector_first_out: float32 [26, 768], P(None, ('dp', 'seq'))
- embed_first_out: float32 [768, 50688], P(('dp', 'seq'))
- head_first_out: float32 [768, 50688], P('dp', 'seq')
- square_second_out: float32 [2, 5, 768, 768], P(None, None, ('dp', 'seq'))
- expand_second_out: float32 [2, 768, 3072], P(None, ('dp', 'seq'))
- shrink_second_out: float32 [2, 3072, 768], P(None, ('dp', 'seq'))
- vector_second_out: float32 [26, 768], P(None, ('dp', 'seq'))
- embed_second_out: float32 [768, 50688], P(('dp', 'seq'))
- head_second_out: float32 [768, 50688], P('dp', 'seq')
Inputs may be any that keep to these rules, and one draw needn't show every extreme that they name: `vector_params`: time decays lie between log(0.25 / 1024) and log(1 / 24); mixing shares between 0.1 and 0.9.
All inputs are finite; a program needn't handle non-finite values.
Results may differ from a plain program's by a relative error of at most 0.018.
Values may be sent and summed in bfloat16 or wider, within the bound.
A program may use at most 448 MiB of HBM per device.

v0:
```python
import math

import jax
import jax.numpy as jnp
from jax import lax
from jax.sharding import PartitionSpec as P

STEP = 10


EXACT_MATMUL = lax.Precision.HIGHEST
BETA_ONE = 0.9
BETA_TWO = 0.999
ADAM_EPS = 1e-08
WEIGHT_DECAY = 0.01
LEARN_RATES = (0.03, 0.03, 0.015, 0.5, 2.0, 0.05)
DECAY_FLAGS = (True, True, True, False, True, True)
param_stride = 11
logit_block = 512
scan_block = 256


def from_behind(value, axis, steps):
    count = lax.axis_size(axis)
    leading, last = (max(0, -steps), min(count, count - steps))
    return lax.ppermute(value, axis, [(source, source + steps) for source in range(leading, last)])


def carried_in(value, axis, join, neutral, backward):
    count, mine = (lax.axis_size(axis), lax.axis_index(axis))
    pieces = jax.tree.map(lambda part: lax.all_gather(part, axis), value)
    if backward:
        pieces = jax.tree.map(lambda part: part[::-1], pieces)
        mine = count - 1 - mine
    running = jax.tree.map(
        lambda part, zero: jnp.full_like(part, 0) + jnp.asarray(zero, part.dtype), value, neutral
    )

    def carried_turn(position, running):
        longer = join(running, jax.tree.map(lambda part: part[position], pieces))
        return jax.tree.map(lambda new, old: jnp.where(position < mine, new, old), longer, running)

    return lax.fori_loop(0, count - 1, carried_turn, running)


def combined_all(shard, axis, combine):
    everything = jax.tree.map(lambda part: lax.all_gather(part, axis), shard)
    leading = jax.tree.map(lambda part: part[0], everything)

    def combined_turn(k, so_far):
        return combine(so_far, jax.tree.map(lambda part: part[k], everything))

    return lax.fori_loop(1, lax.axis_size(axis), combined_turn, leading)


def layer_norm(values, gain, bias):
    centre = values - jnp.mean(values, axis=-1, keepdims=True)
    spread = jnp.mean(centre * centre, axis=-1, keepdims=True)
    return centre * lax.rsqrt(spread + 1e-05) * gain + bias


def matmul(left, right):
    return jnp.dot(left, right, preferred_element_type=jnp.float32)


def matmul_tn(left, right):
    return lax.dot_general(
        left, right, (((0,), (0,)), ((), ())), preferred_element_type=jnp.float32
    )


def matmul_nt(left, right):
    return lax.dot_general(
        left, right, (((1,), (1,)), ((), ())), preferred_element_type=jnp.float32
    )


def blend_all(normed, incoming, shares):
    earlier = jnp.concatenate([incoming, normed[:-1]], axis=0)
    return tuple(
        (
            normed * shares[member] + earlier * (1.0 - shares[member])
            for member in range(shares.shape[0])
        )
    )


def take_previous(normed):
    return from_behind(normed[-1:], "seq", 1)


def give_back(grad_first):
    return from_behind(grad_first, "seq", -1)


def block_ends(arriving_lookups, arriving_contents, logarithmic_fading_speed):
    decay_rate = jnp.exp(logarithmic_fading_speed)
    length = arriving_lookups.shape[0]
    ages = (length - 1.0 - jnp.arange(length, dtype=jnp.float32))[:, None]
    weight = jnp.exp(arriving_lookups - decay_rate * ages)
    return (jnp.sum(weight * arriving_contents, axis=0), jnp.sum(weight, axis=0))


def block_factor(logarithmic_fading_speed, length):
    return jnp.exp(-jnp.exp(logarithmic_fading_speed) * length)


def chain_combine(earlier, later):
    return (
        earlier[0] * later[2] + later[0],
        earlier[1] * later[2] + later[1],
        earlier[2] * later[2],
    )


def token_mixer_block(
    arriving_lookups,
    arriving_contents,
    logarithmic_fading_speed,
    present_reward,
    initial_numerator,
    initial_denominator,
):
    decay_rate = jnp.exp(logarithmic_fading_speed)
    length, channels = arriving_lookups.shape
    block_size = min(scan_block, length)
    block_count = length // block_size
    offsets = jnp.arange(block_size, dtype=jnp.float32)[:, None]
    lower_mask = (offsets > offsets.T).astype(jnp.float32)
    diagonal_amplifier = jnp.exp(present_reward)
    back_decay = jnp.exp(-decay_rate * (offsets - 1.0))
    carry_decay = jnp.exp(-decay_rate * offsets)
    tail_decay = jnp.exp(-decay_rate * (block_size - 1.0))
    full_decay = jnp.exp(-decay_rate * block_size)

    def sub_block(state, step_item):
        numerator, denominator = state
        key_block, value_block = step_item
        lifted = jnp.exp(key_block + decay_rate * offsets)
        prefix_sums = jnp.dot(
            lower_mask,
            jnp.concatenate([lifted * value_block, lifted], axis=1),
            precision=EXACT_MATMUL,
        )
        own_term = diagonal_amplifier * jnp.exp(key_block)
        top_part = (
            back_decay * prefix_sums[:, :channels]
            + carry_decay * numerator
            + own_term * value_block
        )
        low_part = back_decay * prefix_sums[:, channels:] + carry_decay * denominator + own_term
        next_num = tail_decay * jnp.sum(lifted * value_block, axis=0) + full_decay * numerator
        next_den = tail_decay * jnp.sum(lifted, axis=0) + full_decay * denominator
        return ((next_num, next_den), (top_part / low_part, low_part))

    shaped = (
        arriving_lookups.reshape(block_count, block_size, channels),
        arriving_contents.reshape(block_count, block_size, channels),
    )
    (end_num, end_den), (block_outs, denoms) = lax.scan(
        sub_block, (initial_numerator, initial_denominator), shaped
    )
    return (
        (block_outs.reshape(length, channels), end_num, end_den),
        denoms.reshape(length, channels),
    )


def layer_forward(stream, gathered):
    square, expand, shrink, params = gathered
    normed = layer_norm(stream, params[0], params[1])
    incoming_one = take_previous(normed)
    blended = blend_all(normed, incoming_one, params[2:5])
    mixed_key = blended[0].astype(jnp.bfloat16)
    mixed_value = blended[1].astype(jnp.bfloat16)
    mixed_gate = blended[2].astype(jnp.bfloat16)
    arriving_lookups = matmul(mixed_key, square[0])
    arriving_contents = matmul(mixed_value, square[1])
    gates_in = matmul(mixed_gate, square[2])
    length = arriving_lookups.shape[0]
    end_sums = block_ends(arriving_lookups, arriving_contents, params[5])
    zero_state = jnp.zeros_like(end_sums[0])
    one_state = jnp.ones_like(end_sums[0])
    factor = block_factor(params[5], length)
    initial_numerator, initial_denominator, spare_factor = carried_in(
        (end_sums[0], end_sums[1], factor),
        "seq",
        chain_combine,
        (zero_state, zero_state, one_state),
        False,
    )
    (mixed_out, spare_placeholder, spare_placeholder), spare_placeholder = token_mixer_block(
        arriving_lookups,
        arriving_contents,
        params[5],
        params[6],
        initial_numerator,
        initial_denominator,
    )
    gated = (jax.nn.sigmoid(gates_in) * mixed_out).astype(jnp.bfloat16)
    middle = stream + matmul(gated, square[3])
    normed_two = layer_norm(middle, params[7], params[8])
    incoming_two = take_previous(normed_two)
    blended_two = blend_all(normed_two, incoming_two, params[9:11])
    chan_key = blended_two[0].astype(jnp.bfloat16)
    chan_gate = blended_two[1].astype(jnp.bfloat16)
    pre_act = matmul(chan_key, expand)
    activated = jnp.square(jnp.maximum(pre_act, 0.0)).astype(jnp.bfloat16)
    chan_value = matmul(activated, shrink)
    gate_pre = matmul(chan_gate, square[4])
    result = middle + jax.nn.sigmoid(gate_pre) * chan_value
    saved = (
        stream,
        incoming_one,
        mixed_key,
        mixed_value,
        mixed_gate,
        arriving_lookups,
        arriving_contents,
        gates_in,
        initial_numerator,
        initial_denominator,
        gated,
        middle,
        incoming_two,
        chan_key,
        chan_gate,
        pre_act,
        activated,
        chan_value,
        gate_pre,
    )
    return (result, saved)


def norm_back(stream, incoming, params, first_row, share_rows, grads):
    normed, norm_pull = jax.vjp(layer_norm, stream, params[first_row], params[first_row + 1])
    shares = params[share_rows[0] : share_rows[1]]
    spare_placeholder, blend_pull = jax.vjp(blend_all, normed, incoming, shares)
    d_normed, d_incoming, d_shares = blend_pull(grads)
    from_next = give_back(d_incoming)
    d_normed = d_normed.at[-1].add(from_next[0])
    d_stream, d_gain, d_bias = norm_pull(d_normed)
    return (d_stream, jnp.stack([d_gain, d_bias]), d_shares)


def layer_backward(gradient, saved, gathered):
    square, expand, shrink, params = gathered
    (
        stream,
        incoming_one,
        mixed_key,
        mixed_value,
        mixed_gate,
        arriving_lookups,
        arriving_contents,
        gates_in,
        initial_numerator,
        initial_denominator,
        gated,
        middle,
        incoming_two,
        chan_key,
        chan_gate,
        pre_act,
        activated,
        chan_value,
        gate_pre,
    ) = saved
    gate_sig = jax.nn.sigmoid(gate_pre)
    d_value = (gradient * gate_sig).astype(jnp.bfloat16)
    d_gate_pre = (gradient * chan_value * gate_sig * (1.0 - gate_sig)).astype(jnp.bfloat16)
    g_shrink = matmul_tn(activated, d_value)
    d_active = matmul_nt(d_value, shrink)
    d_pre = (d_active * 2.0 * jnp.maximum(pre_act, 0.0)).astype(jnp.bfloat16)
    g_expand = matmul_tn(chan_key, d_pre)
    g_chan_gate = matmul_tn(chan_gate, d_gate_pre)
    d_chan_key = matmul_nt(d_pre, expand)
    d_chan_gate = matmul_nt(d_gate_pre, square[4])
    d_middle, second_norm_gradient, second_share_gradient = norm_back(
        middle, incoming_two, params, 7, (9, 11), (d_chan_key, d_chan_gate)
    )
    d_middle = d_middle + gradient
    d_output = d_middle.astype(jnp.bfloat16)
    g_output = matmul_tn(gated, d_output)
    d_gated = matmul_nt(d_output, square[3])
    (mixed_out, spare_placeholder, spare_placeholder), token_mixer_backward, denoms = jax.vjp(
        token_mixer_block,
        arriving_lookups,
        arriving_contents,
        params[5],
        params[6],
        initial_numerator,
        initial_denominator,
        has_aux=True,
    )
    gate_sig_one = jax.nn.sigmoid(gates_in)
    mixed_gradient = d_gated * gate_sig_one
    d_gates_in = (d_gated * mixed_out * gate_sig_one * (1.0 - gate_sig_one)).astype(jnp.bfloat16)
    length = arriving_lookups.shape[0]
    decay_rate = jnp.exp(params[5])
    carried = (
        jnp.exp(-decay_rate * jnp.arange(length, dtype=jnp.float32)[:, None])
        * mixed_gradient
        / denoms
    )
    zero_state = jnp.zeros_like(decay_rate)
    one_state = jnp.ones_like(decay_rate)
    factor = block_factor(params[5], length)
    following_numerator, following_denominator, spare_factor = carried_in(
        (jnp.sum(carried, axis=0), -jnp.sum(carried * mixed_out, axis=0), factor),
        "seq",
        chain_combine,
        (zero_state, zero_state, one_state),
        True,
    )
    (
        lookup_sensitivity,
        content_sensitivity,
        fading_sensitivity,
        reward_sensitivity,
        spare_placeholder,
        spare_placeholder,
    ) = token_mixer_backward((mixed_gradient, following_numerator, following_denominator))
    lookup_sensitivity = lookup_sensitivity.astype(jnp.bfloat16)
    content_sensitivity = content_sensitivity.astype(jnp.bfloat16)
    g_key = matmul_tn(mixed_key, lookup_sensitivity)
    g_value = matmul_tn(mixed_value, content_sensitivity)
    g_gate = matmul_tn(mixed_gate, d_gates_in)
    d_mixed_key = matmul_nt(lookup_sensitivity, square[0])
    d_mixed_value = matmul_nt(content_sensitivity, square[1])
    d_mixed_gate = matmul_nt(d_gates_in, square[2])
    d_stream, first_norm_gradient, first_share_gradient = norm_back(
        stream, incoming_one, params, 0, (2, 5), (d_mixed_key, d_mixed_value, d_mixed_gate)
    )
    d_stream = d_stream + d_middle
    g_square = jnp.stack([g_key, g_value, g_gate, g_output, g_chan_gate])
    g_params = jnp.concatenate(
        [
            first_norm_gradient,
            first_share_gradient,
            fading_sensitivity[None],
            reward_sensitivity[None],
            second_norm_gradient,
            second_share_gradient,
        ],
        axis=0,
    )
    return (d_stream, (g_square, g_expand, g_shrink, g_params))


def merge_soft(first_part, second_part):
    row_top = jnp.maximum(first_part[0], second_part[0])
    spread = first_part[1] * jnp.exp(first_part[0] - row_top) + second_part[1] * jnp.exp(
        second_part[0] - row_top
    )
    return (row_top, spread, first_part[2] + second_part[2])


def adam_update(weights, gradient, first, second, step_rate, decay_on):
    first_new = BETA_ONE * first + (1.0 - BETA_ONE) * gradient
    second_new = BETA_TWO * second + (1.0 - BETA_TWO) * gradient * gradient
    first_hat = first_new / (1.0 - BETA_ONE**STEP)
    second_hat = second_new / (1.0 - BETA_TWO**STEP)
    moved = first_hat / (jnp.sqrt(second_hat) + ADAM_EPS)
    if decay_on:
        moved = moved + WEIGHT_DECAY * weights
    return (weights - step_rate * moved, first_new, second_new)


def per_device(
    token_ids,
    targets,
    loss_mask,
    square_weights,
    expand_weights,
    shrink_weights,
    vector_params,
    embed_table,
    head_table,
    square_first,
    expand_first,
    shrink_first,
    vector_first,
    embed_first,
    head_first,
    square_second,
    expand_second,
    shrink_second,
    vector_second,
    embed_second,
    head_second,
):
    layers = square_weights.shape[0]
    global_rows = param_stride * layers
    total_tokens = token_ids.shape[0]

    def fetch_layer(layer_id):
        vector_rows = vector_params[layer_id * param_stride : (layer_id + 1) * param_stride]
        if layer_id == 0:
            vector_rows = jnp.concatenate([vector_rows, vector_params[global_rows:]], axis=0)
        fetched = (
            lax.all_gather(
                square_weights[layer_id].astype(jnp.bfloat16), ("dp", "seq"), axis=1, tiled=True
            ),
            lax.all_gather(
                expand_weights[layer_id].astype(jnp.bfloat16), ("dp", "seq"), axis=0, tiled=True
            ),
            lax.all_gather(
                shrink_weights[layer_id].astype(jnp.bfloat16), ("dp", "seq"), axis=0, tiled=True
            ),
            lax.all_gather(vector_rows.astype(jnp.bfloat16), ("dp", "seq"), axis=1, tiled=True),
        )
        return (fetched[0], fetched[1], fetched[2], fetched[3].astype(jnp.float32))

    columns = jnp.take(embed_table.astype(jnp.bfloat16), token_ids, axis=1)
    embedded = lax.all_to_all(
        columns, ("dp", "seq"), split_axis=1, concat_axis=0, tiled=True
    ).T.astype(jnp.float32)
    first_block = fetch_layer(0)
    global_params = first_block[3][param_stride:]
    stream, norm_pull_zero = jax.vjp(layer_norm, embedded, global_params[0], global_params[1])
    kept_blocks = []
    saved_layers = []
    gathered = first_block
    for layer_id in range(layers):
        if layer_id > 0:
            gathered = fetch_layer(layer_id)
        kept_blocks.append(gathered)
        stream, saved = layer_forward(stream, gathered)
        saved_layers.append(saved)
    normed, norm_pull_last = jax.vjp(layer_norm, stream, global_params[2], global_params[3])
    head_full = lax.all_gather(head_table.astype(jnp.bfloat16), "dp", axis=0, tiled=True)
    vocab_part = head_full.shape[1]
    own_rows = normed.shape[0]
    rows_all = lax.all_gather(normed.astype(jnp.bfloat16), "seq", axis=0, tiled=True)
    seq_len = rows_all.shape[0]
    seq_place = lax.axis_index("seq")
    local_ids = targets - seq_place * vocab_part
    rows_per_block = min(logit_block, seq_len)
    block_count = seq_len // rows_per_block
    row_blocks = rows_all.reshape(block_count, rows_per_block, rows_all.shape[1])
    id_blocks = local_ids.reshape(block_count, rows_per_block)
    column_ids = jnp.arange(vocab_part, dtype=jnp.int32)[None, :]

    def block_stats(step_item):
        rows_now, ids_now = step_item
        logits = matmul(rows_now, head_full)
        row_top = jnp.max(logits, axis=1)
        spread = jnp.sum(jnp.exp(logits - row_top[:, None]), axis=1)
        picked = jnp.sum(jnp.where(column_ids == ids_now[:, None], logits, 0.0), axis=1)
        return (row_top, spread, picked)

    row_tops, spreads, picks = lax.map(block_stats, (row_blocks, id_blocks))
    row_tops, spreads, picks = combined_all(
        (row_tops.reshape(seq_len), spreads.reshape(seq_len), picks.reshape(seq_len)),
        "seq",
        merge_soft,
    )
    log_total = row_tops + jnp.log(spreads)
    counted = loss_mask.astype(jnp.float32)
    losses = counted * (log_total - picks)
    loss_part = jnp.sum(lax.dynamic_slice_in_dim(losses, seq_place * own_rows, own_rows))
    weight_rows = counted / total_tokens

    def block_back(grad_head, step_item):
        rows_now, ids_now, log_now, weight_now = step_item
        logits = matmul(rows_now, head_full)
        softmax_rows = jnp.exp(logits - log_now[:, None])
        hits = (column_ids == ids_now[:, None]).astype(jnp.float32)
        d_logits = ((softmax_rows - hits) * weight_now[:, None]).astype(jnp.bfloat16)
        return (grad_head + matmul_tn(rows_now, d_logits), matmul_nt(d_logits, head_full))

    grad_head, d_rows = lax.scan(
        block_back,
        jnp.zeros(head_full.shape, jnp.float32),
        (
            row_blocks,
            id_blocks,
            log_total.reshape(block_count, rows_per_block),
            weight_rows.reshape(block_count, rows_per_block),
        ),
    )
    d_normed = lax.psum_scatter(
        d_rows.reshape(seq_len, rows_all.shape[1]).astype(jnp.bfloat16),
        "seq",
        scatter_dimension=0,
        tiled=True,
    ).astype(jnp.float32)
    g_head = lax.psum_scatter(
        grad_head.astype(jnp.bfloat16), "dp", scatter_dimension=0, tiled=True
    ).astype(jnp.float32)
    d_stream, d_gain_last, d_bias_last = norm_pull_last(d_normed)
    layer_grads = [None] * layers
    d_embedded = d_stream
    for layer_id in reversed(range(layers)):
        gathered = fetch_layer(layer_id)
        d_stream, grads = layer_backward(d_stream, saved_layers[layer_id], gathered)
        g_params = grads[3]
        if layer_id == 0:
            d_embedded, d_gain_zero, d_bias_zero = norm_pull_zero(d_stream)
            g_params = jnp.concatenate(
                [g_params, jnp.stack([d_gain_zero, d_bias_zero, d_gain_last, d_bias_last])], axis=0
            )
        layer_grads[layer_id] = (
            lax.psum_scatter(grads[0], ("dp", "seq"), scatter_dimension=1, tiled=True),
            lax.psum_scatter(grads[1], ("dp", "seq"), scatter_dimension=0, tiled=True),
            lax.psum_scatter(grads[2], ("dp", "seq"), scatter_dimension=0, tiled=True),
            lax.psum_scatter(g_params, ("dp", "seq"), scatter_dimension=1, tiled=True),
        )
    back_columns = lax.all_to_all(
        d_embedded.T.astype(jnp.bfloat16), ("dp", "seq"), split_axis=0, concat_axis=1, tiled=True
    )
    g_embed = jax.ops.segment_sum(
        back_columns.T.astype(jnp.float32), token_ids, num_segments=embed_table.shape[1]
    ).T
    g_square = jnp.stack([layer_grads[layer_id][0] for layer_id in range(layers)])
    g_expand = jnp.stack([layer_grads[layer_id][1] for layer_id in range(layers)])
    g_shrink = jnp.stack([layer_grads[layer_id][2] for layer_id in range(layers)])
    vector_parts = (
        [layer_grads[0][3][:param_stride]]
        + [layer_grads[1][3]]
        + [layer_grads[0][3][param_stride:]]
    )
    g_vector = jnp.concatenate(vector_parts, axis=0)
    gradients = (g_square, g_expand, g_shrink, g_vector, g_embed, g_head)
    square_part = jnp.zeros((), jnp.float32)
    for gradient in gradients:
        square_part = square_part + jnp.sum(gradient * gradient)
    loss_sum, square_sum = lax.psum((loss_part, square_part), ("dp", "seq"))
    grad_norm = jnp.sqrt(square_sum)
    scale = jnp.minimum(1.0, 0.5 / math.sqrt(total_tokens) / (grad_norm + 1e-06))
    weights = (
        square_weights,
        expand_weights,
        shrink_weights,
        vector_params,
        embed_table,
        head_table,
    )
    firsts = (square_first, expand_first, shrink_first, vector_first, embed_first, head_first)
    seconds = (
        square_second,
        expand_second,
        shrink_second,
        vector_second,
        embed_second,
        head_second,
    )
    updated = [
        adam_update(
            weights[slot],
            gradients[slot] * scale,
            firsts[slot],
            seconds[slot],
            LEARN_RATES[slot],
            DECAY_FLAGS[slot],
        )
        for slot in range(6)
    ]
    return (
        loss_sum,
        grad_norm,
        updated[0][0],
        updated[1][0],
        updated[2][0],
        updated[3][0],
        updated[4][0],
        updated[5][0],
        updated[0][1],
        updated[1][1],
        updated[2][1],
        updated[3][1],
        updated[4][1],
        updated[5][1],
        updated[0][2],
        updated[1][2],
        updated[2][2],
        updated[3][2],
        updated[4][2],
        updated[5][2],
    )


def solution(mesh):
    placed = (
        P(),
        P("dp"),
        P("dp"),
        P(None, None, ("dp", "seq"), None),
        P(None, ("dp", "seq"), None),
        P(None, ("dp", "seq"), None),
        P(None, ("dp", "seq")),
        P(("dp", "seq"), None),
        P("dp", "seq"),
        P(None, None, ("dp", "seq"), None),
        P(None, ("dp", "seq"), None),
        P(None, ("dp", "seq"), None),
        P(None, ("dp", "seq")),
        P(("dp", "seq"), None),
        P("dp", "seq"),
        P(None, None, ("dp", "seq"), None),
        P(None, ("dp", "seq"), None),
        P(None, ("dp", "seq"), None),
        P(None, ("dp", "seq")),
        P(("dp", "seq"), None),
        P("dp", "seq"),
    )
    return jax.shard_map(
        per_device,
        mesh=mesh,
        in_specs=placed,
        out_specs=(
            P(),
            P(),
            P(None, None, ("dp", "seq"), None),
            P(None, ("dp", "seq"), None),
            P(None, ("dp", "seq"), None),
            P(None, ("dp", "seq")),
            P(("dp", "seq"), None),
            P("dp", "seq"),
            P(None, None, ("dp", "seq"), None),
            P(None, ("dp", "seq"), None),
            P(None, ("dp", "seq"), None),
            P(None, ("dp", "seq")),
            P(("dp", "seq"), None),
            P("dp", "seq"),
            P(None, None, ("dp", "seq"), None),
            P(None, ("dp", "seq"), None),
            P(None, ("dp", "seq"), None),
            P(None, ("dp", "seq")),
            P(("dp", "seq"), None),
            P("dp", "seq"),
        ),
        check_vma=False,
    )
```

profile of v0, /device:TPU:0, one launch (start us, length us, event | category | flops | bytes accessed | tf_op | source)
XLA Modules:
  0.0 2625.6 jit_solution(184032377298681552)
XLA Ops:
  25.4 28.3 %gather_fusion = bf16[8192,24]{1,0:T(8,128)(2,1)S(1)} fusion(bf16[24,50688]{0,1:T(8,128)(2,1)} %copy.122, s32[8192]{0:T(1024)S(1)} %fusion.130), kind=kCustom, calls=%fused_computation | custom fusion | bytes 819200 | tf_op jit(solution)/shard_map/jit(_take)/gather | solution.py:416
  64.0 47.0 %all-gather.14 = bf16[32,24,15]{1,2,0:T(8,128)(2,1)S(1)} all-gather(bf16[1,24,15]{1,2,0:T(8,128)(2,1)S(1)} %maximum_bitcast_fusion), channel_id=1, replica_groups=mesh['dp'=8,'seq'=4] {'dp','seq'}, dimensions={0}, use_global_device_ids=true | all-gather | bytes 23760 | tf_op jit(solution)/shard_map/all_gather | solution.py:412
  111.4 39.5 %all-gather.18 = bf16[32,24,11]{1,2,0:T(8,128)(2,1)S(1)} all-gather(bf16[1,24,11]{1,2,0:T(8,128)(2,1)S(1)} %get-tuple-element.1881), channel_id=1, replica_groups=mesh['dp'=8,'seq'=4] {'dp','seq'}, dimensions={0}, use_global_device_ids=true | all-gather | bytes 17424 | tf_op jit(solution)/shard_map/all_gather | solution.py:412
  237.3 54.0 %all-gather.48.cloned.1.call-done = bf16[1,5,768,768]{3,2,1,0:T(8,128)(2,1)} async-done(((bf16[1,5,24,768]{3,2,1,0:T(8,128)(2,1)}), bf16[1,5,768,768]{3,2,1,0:T(8,128)(2,1)}) %all-gather.48.cloned.1.call-update) | async-done | bytes 5898256 | tf_op jit(solution)/shard_map/all_gather | solution.py:403
  328.6 28.2 %all-gather.50.cloned.1.call-done = bf16[1,768,3072]{2,1,0:T(8,128)(2,1)} async-done(((bf16[1,24,3072]{2,1,0:T(8,128)(2,1)}), bf16[1,768,3072]{2,1,0:T(8,128)(2,1)}) %all-gather.50.cloned.1.call-update) | async-done | bytes 4718608 | tf_op jit(solution)/shard_map/all_gather | solution.py:406
  360.6 62.1 %all-gather.52.cloned.1.call-done = bf16[1,3072,768]{2,1,0:T(8,128)(2,1)} async-done(((bf16[1,96,768]{2,1,0:T(8,128)(2,1)}), bf16[1,3072,768]{2,1,0:T(8,128)(2,1)}) %all-gather.52.cloned.1.call-update) | async-done | bytes 4718608 | tf_op jit(solution)/shard_map/all_gather | solution.py:409
  450.6 375.7 %all-gather.40.cloned.1.call-done = bf16[768,12672]{1,0:T(8,128)(2,1)} async-done(((bf16[96,12672]{1,0:T(8,128)(2,1)}), bf16[768,12672]{1,0:T(8,128)(2,1)}) %all-gather.40.cloned.1.call-update) | async-done | bytes 19464208 | tf_op jit(solution)/shard_map/all_gather | solution.py:433
  826.2 69.9 %while.74 = (s32[]{:T(128)}, f32[2,512]{1,0:T(2,128)S(1)}, f32[2,512]{1,0:T(2,128)S(1)}, f32[2,512]{1,0:T(2,128)S(1)}, bf16[2,512,768]{2,1,0:T(8,128)(2,1)}, /*i...) while((s32[]{:T(128)}, f32[2,512]{1,0:T(2,128)S(1)}, ...), condition=%wide.region_24.25_spmd.clone, body=%wide.region_20.24_spmd.clone.sunk | while | flops 10004593664 | bytes 72181872 | solution.py:454
  826.2 22.0 fusion.245
  861.2 22.0 fusion.245
  912.9 125.1 %while.77 = (s32[]{:T(128)}, f32[768,12672]{1,0:T(8,128)}, bf16[2,512,768]{2,1,0:T(8,128)(2,1)}, bf16[2,512,768]{2,1,0:T(8,128)(2,1)}, bf16[768,12672]{1,0:T(8,1...) while((s32[]{:T(128)}, f32[768,12672]{1,0:T(8,128)}, ...), condition=%wide.region_30.31_spmd.clone, body=%wide.region_29.30_spmd.clone.sunk | while | flops 29955391488 | bytes 165169328 | solution.py:474
  932.0 22.4 select_add_fusion.2
  990.6 30.2 %select_add_fusion.2 = f32[768,12672]{1,0:T(8,128)} fusion(f32[768,12672]{1,0:T(8,128)} %get-tuple-element.2389, bf16[512,12672]{1,0:T(8,128)(2,1)} %multiply_convert_fusion.16, pred[]{:T(512)S(6)} %compare.65, bf16[2,512,768]{2,1,0:T(8,128)(2,1)S(1)} %copy-done.30, s32[]{:T(128)S(6)} %copy.233), kind=kOutput, calls=%fused_computation.16.clone.1 | convolution fusion | flops 9985130496 | bytes 91619336 | tf_op jit(solution)/shard_map/while/body/eval_jaxpr/dot_general | solution.py:67
  1042.0 24.3 reduce-scatter.11.cloned.1.call-done
  1293.4 38.3 %all-reduce.34.cloned.1.call-done = (f32[15,768]{1,0:T(8,128)}, f32[11,768]{1,0:T(8,128)}) async-done(((f32[15,768]{1,0:T(8,128)}, f32[11,768]{1,0:T(8,128)}), (f32[15,768]{1,0:T(8,128)}, f32[11,768]{1,0:T(8,128)})) %all-reduce.34.cloned.1.call-update) | async-done | bytes 79888
  1337.5 55.3 %scatter_custom_fusion = f32[50688,24]{1,0:T(8,128)} fusion(s32[8192]{0:T(1024)} %param.43, f32[8192,24]{1,0:T(8,128)} %copy.132, f32[]{:T(128)} %constant.500.clone.1), kind=kCustom, calls=%fused_computation.50 | custom fusion | flops 196608 | bytes 4866560 | tf_op jit(solution)/shard_map/scatter-add | solution.py:514
  1403.1 71.8 %reduce-scatter.19.cloned.1.call-done = f32[24,3072]{1,0:T(8,128)} async-done(((f32[768,3072]{1,0:T(8,128)}), f32[24,3072]{1,0:T(8,128)}) %reduce-scatter.19.cloned.1.call-update) | async-done | bytes 294928 | tf_op jit(solution)/shard_map/reduce_scatter | solution.py:507
  1474.9 140.5 %reduce-scatter.17.cloned.1.call-done = f32[24,3072]{1,0:T(8,128)} async-done(((f32[768,3072]{1,0:T(8,128)}), f32[24,3072]{1,0:T(8,128)}) %reduce-scatter.17.cloned.1.call-update) | async-done | bytes 294928 | tf_op jit(solution)/shard_map/reduce_scatter | solution.py:507
  1617.2 139.7 %reduce-scatter.23.cloned.1.call-done = f32[96,768]{1,0:T(8,128)} async-done(((f32[3072,768]{1,0:T(8,128)}), f32[96,768]{1,0:T(8,128)}) %reduce-scatter.23.cloned.1.call-update) | async-done | bytes 294928 | tf_op jit(solution)/shard_map/reduce_scatter | solution.py:508
  1756.9 140.6 %reduce-scatter.21.cloned.1.call-done = f32[96,768]{1,0:T(8,128)} async-done(((f32[3072,768]{1,0:T(8,128)}), f32[96,768]{1,0:T(8,128)}) %reduce-scatter.21.cloned.1.call-update) | async-done | bytes 294928 | tf_op jit(solution)/shard_map/reduce_scatter | solution.py:508
  1899.3 151.9 %reduce-scatter.15.cloned.1.call-done = f32[5,24,768]{2,1,0:T(8,128)} async-done(((f32[5,768,768]{2,1,0:T(8,128)}), f32[5,24,768]{2,1,0:T(8,128)}) %reduce-scatter.15.cloned.1.call-update) | async-done | bytes 368656 | tf_op jit(solution)/shard_map/reduce_scatter | solution.py:506
  2051.1 152.6 %reduce-scatter.13.cloned.1.call-done = f32[5,24,768]{2,1,0:T(8,128)} async-done(((f32[5,768,768]{2,1,0:T(8,128)}), f32[5,24,768]{2,1,0:T(8,128)}) %reduce-scatter.13.cloned.1.call-update) | async-done | bytes 368656 | tf_op jit(solution)/shard_map/reduce_scatter | solution.py:506
  2208.8 318.1 %reduce-scatter.25.cloned.1.call-done = bf16[96,12672]{1,0:T(8,128)(2,1)} async-done(((bf16[768,12672]{1,0:T(8,128)(2,1)}), bf16[96,12672]{1,0:T(8,128)(2,1)}) %reduce-scatter.25.cloned.1.call-update) | async-done | bytes 2433040 | tf_op jit(solution)/shard_map/reduce_scatter | solution.py:490
  2546.7 39.8 %all-reduce.30 = (f32[]{:T(128)}, f32[]{:T(128)}) all-reduce(f32[]{:T(128)} %dynamic-slice_reduce_fusion.12, f32[]{:T(128)S(6)} %add.813), channel_id=1, replica_groups=mesh['dp'=8,'seq'=4] {'dp','seq'}, use_global_device_ids=true, to_apply=%region_28.29 | all-reduce | flops 2 | bytes 16 | tf_op jit(solution)/shard_map/psum | solution.py:530
  (971 shorter events, 622.4 us)
Async XLA Ops:
  7.2 158.8 %all-gather.42.cloned.1.call-start = ((), (), s32[]{:S(2)}) async-start(), calls=%async_computation.20 | async-start | bytes 6082560 | tf_op jit(solution)/shard_map/all_gather | solution.py:403
  9.2 188.8 %all-gather.44.cloned.1.call-start = ((), (), s32[]{:S(2)}) async-start(), calls=%async_computation.21 | async-start | bytes 4866048 | tf_op jit(solution)/shard_map/all_gather | solution.py:406
  11.1 209.8 %all-gather.46.cloned.1.call-start = ((), (), s32[]{:S(2)}) async-start(), calls=%async_computation.22 | async-start | bytes 4866048 | tf_op jit(solution)/shard_map/all_gather | solution.py:409
  13.0 278.4 %all-gather.48.cloned.1.call-start = ((), (), s32[]{:S(2)}) async-start(), calls=%async_computation.23 | async-start | bytes 6082560 | tf_op jit(solution)/shard_map/all_gather | solution.py:403
  13.6 343.3 %all-gather.50.cloned.1.call-start = ((), (), s32[]{:S(2)}) async-start(), calls=%async_computation.24 | async-start | bytes 4866048 | tf_op jit(solution)/shard_map/all_gather | solution.py:406
  55.3 97.6 %all-to-all-start = ((bf16[24,32,256]{2,0,1:T(8,128)(2,1)}), bf16[24,32,256]{2,0,1:T(8,128)(2,1)S(1)}, u32[]{:S(2)}, u32[]{:S(2)}) async-start(bf16[24,32,256]{2,0,1:T(8,128)(2,1)} %broadcast_select_fusion), calls=%async_computation | async-start | bytes 786432 | tf_op jit(solution)/shard_map/all_to_all | solution.py:417
  62.6 360.0 %all-gather.52.cloned.1.call-start = ((), (), s32[]{:S(2)}) async-start(), calls=%async_computation.25 | async-start | bytes 4866048 | tf_op jit(solution)/shard_map/all_gather | solution.py:409
  63.2 387.3 %all-gather.38.cloned.1.call-start = ((), (), s32[]{:S(2)}) async-start(), calls=%async_computation.10 | async-start | bytes 1966080 | tf_op jit(solution)/shard_map/all_gather | solution.py:436
  154.6 9.1 collective-permute-start
  228.4 8.2 collective-permute-start.2
  431.9 394.3 %all-gather.40.cloned.1.call-start = ((), (), s32[]{:S(2)}) async-start(), calls=%async_computation.11 | async-start | bytes 21897216 | tf_op jit(solution)/shard_map/all_gather | solution.py:433
  436.1 630.2 %reduce-scatter.11.cloned.1.call-start = ((), (), s32[]{:S(2)}) async-start(), calls=%async_computation.12 | async-start | bytes 1966080 | tf_op jit(solution)/shard_map/reduce_scatter | solution.py:484
  1038.0 293.7 %all-reduce.34.cloned.1.call-start = ((), (), s32[]{:S(2)}) async-start(), calls=%async_computation.26 | async-start | bytes 196608
  1124.5 5.6 collective-permute-start.5
  1144.4 6.0 collective-permute-start.6
  1192.8 4.3 collective-permute-start.7
  1207.9 266.9 %reduce-scatter.19.cloned.1.call-start = ((), (), s32[]{:S(2)}) async-start(), calls=%async_computation.16 | async-start | bytes 9732096 | tf_op jit(solution)/shard_map/reduce_scatter | solution.py:507
  1214.6 400.8 %reduce-scatter.17.cloned.1.call-start = ((), (), s32[]{:S(2)}) async-start(), calls=%async_computation.15 | async-start | bytes 9732096 | tf_op jit(solution)/shard_map/reduce_scatter | solution.py:507
  1222.0 534.8 %reduce-scatter.23.cloned.1.call-start = ((), (), s32[]{:S(2)}) async-start(), calls=%async_computation.18 | async-start | bytes 9732096 | tf_op jit(solution)/shard_map/reduce_scatter | solution.py:508
  1230.0 667.4 %reduce-scatter.21.cloned.1.call-start = ((), (), s32[]{:S(2)}) async-start(), calls=%async_computation.17 | async-start | bytes 9732096 | tf_op jit(solution)/shard_map/reduce_scatter | solution.py:508
  1237.9 813.2 %reduce-scatter.15.cloned.1.call-start = ((), (), s32[]{:S(2)}) async-start(), calls=%async_computation.14 | async-start | bytes 12165120 | tf_op jit(solution)/shard_map/reduce_scatter | solution.py:506
  1250.8 952.9 %reduce-scatter.13.cloned.1.call-start = ((), (), s32[]{:S(2)}) async-start(), calls=%async_computation.13 | async-start | bytes 12165120 | tf_op jit(solution)/shard_map/reduce_scatter | solution.py:506
  1261.6 1265.3 %reduce-scatter.25.cloned.1.call-start = ((), (), s32[]{:S(2)}) async-start(), calls=%async_computation.19 | async-start | bytes 21897216 | tf_op jit(solution)/shard_map/reduce_scatter | solution.py:490
  1285.3 49.4 %all-to-all-start.1 = ((bf16[32,24,256]{2,1,0:T(8,128)(2,1)}), bf16[32,24,256]{2,1,0:T(8,128)(2,1)S(1)}, u32[]{:S(2)}, u32[]{:S(2)}) async-start(bf16[32,24,256]{2,1,0:T(8,128)(2,1)} %bitcast.52), calls=%async_computation.8 | async-start | bytes 786432 | tf_op jit(solution)/shard_map/all_to_all | solution.py:511
  (263 other events, 3645.7 us)
Sparse Core Ops, SparseCore 0:
  11.5 76.8 all-gather.41
  92.0 62.8 all-gather.43
  158.3 62.5 all-gather.45
  224.3 67.0 all-gather.47
  294.7 62.0 all-gather.49
  360.2 62.4 all-gather.51
  432.1 18.4 all-gather.37
  452.7 373.5 all-gather.39
  1038.1 28.1 reduce-scatter.10
  1208.1 123.5 all-reduce.33
  1338.6 136.2 reduce-scatter.18
  1480.6 134.7 reduce-scatter.16
  1622.3 134.5 reduce-scatter.22
  1762.6 134.7 reduce-scatter.20
  1904.4 146.6 reduce-scatter.14
  2057.1 146.5 reduce-scatter.12
  2208.0 318.9 reduce-scatter.24
where the time goes:
time: 2640 us; the launch traced here: 2630 us
  waiting for transfers between devices  1730 us (66%)
  matrix products  291 us (11%)
  other arithmetic  228 us (9%)
  blocking collectives  197 us (7%)
  local copies, waits for them, and re-layouts  122 us (5%)
  starting transfers between devices  29.3 us (1%)
    all_gather x1, waiting for transfers between devices, per_device(): lax.all_gather(head_table.astype(jnp.bfloat16), 'dp', axis=0, tiled=True)  376 us
    reduce_scatter x1, waiting for transfers between devices, per_device(): lax.psum_scatter(grad_head.astype(jnp.bfloat16), 'dp', scatter_dimension=...  318 us
    reduce_scatter x2, waiting for transfers between devices, per_device(): lax.psum_scatter(grads[0], ('dp', 'seq'), scatter_dimension=1, tiled=True)  304 us
    reduce_scatter x2, waiting for transfers between devices, per_device(): lax.psum_scatter(grads[2], ('dp', 'seq'), scatter_dimension=0, tiled=True)  280 us
    reduce_scatter x2, waiting for transfers between devices, per_device(): lax.psum_scatter(grads[1], ('dp', 'seq'), scatter_dimension=0, tiled=True)  212 us
    dot_general x18, matrix products, matmul(): return jnp.dot(left, right, preferred_element_type=jnp.float32)  125 us
    dot_general x16, matrix products, matmul_tn(): lax.dot_general(left, right, (((0,), (0,)), ((), ())), preferred_element_...  101 us
    all_gather x2, blocking collectives, fetch_layer(): lax.all_gather(vector_rows.astype(jnp.bfloat16), ('dp', 'seq'), axis=1, t...  86.4 us
  transfers between devices with their start and end apart: 27, of which 16 were waited for; matrix products, arithmetic and copies ran while one was open for 11% of the time, Pallas kernels for 0%

commit v1 on v0

--- a/solution.py
+++ b/solution.py
@@ -3,10 +3,562 @@
 import jax
 import jax.numpy as jnp
 from jax import lax
+from jax.experimental import pallas as pl
+from jax.experimental.pallas import tpu as pltpu
 from jax.sharding import PartitionSpec as P
 
 STEP = 10
-
+ON_MESH = pl.DeviceIdType.MESH
+
+
+def place():
+    dp, seq = lax.axis_index("dp"), lax.axis_index("seq")
+    return dp, seq, dp // 2, lax.rem(dp, 2), seq // 2, lax.rem(seq, 2)
+
+
+def greet(partners, extra):
+    barrier = pltpu.get_barrier_semaphore()
+    for partner in partners:
+        pl.semaphore_signal(barrier, inc=1, device_id=partner, device_id_type=ON_MESH)
+    for exists, partner in extra:
+        @pl.when(exists)
+        def _():
+            pl.semaphore_signal(barrier, inc=1, device_id=partner, device_id_type=ON_MESH)
+    peers = len(partners)
+    for exists, partner in extra:
+        peers = peers + exists.astype(jnp.int32)
+    pl.semaphore_wait(barrier, peers)
+
+
+class Sems:
+    def __init__(self, send, recv, local):
+        self.send, self.recv, self.local = send, recv, local
+        self.ns = self.nr = self.nl = 0
+
+    def pair(self):
+        self.ns += 1
+        return self.send.at[self.ns - 1], self.recv.at[self.ns - 1]
+
+    def own(self):
+        self.nl += 1
+        return self.local.at[self.nl - 1]
+
+
+def gather_blocks(tensors, portions, collective_id):
+    count = len(tensors)
+    dims = [t.shape for t in tensors]
+    hops = 3
+    pieces_total = sum(len(p) for p in portions)
+    n_send = count + count + pieces_total * (1 + 2 * hops + 7)
+
+    def kernel(*refs):
+        ins, outs = refs[:count], refs[count : 2 * count]
+        wide = refs[2 * count : 3 * count]
+        half = refs[3 * count : 4 * count]
+        send, recv, local = refs[4 * count :]
+        dp, seq, z, y, x, c = place()
+        core = (dp, seq + 1 - 2 * c)
+        xway = (dp, seq + 2 - 4 * x)
+        yway = (dp + 1 - 2 * y, seq)
+        up, down = (dp + 2, seq), (dp - 2, seq)
+        has_up, has_down = z < hops, z > 0
+        greet([core, xway, yway], [(has_up, up), (has_down, down)])
+        sems = Sems(send, recv, local)
+
+        def cols(t, side):
+            width = dims[t][2] // 2
+            return pl.ds(pl.multiple_of(side * width, 128), width)
+
+        first = []
+        for t in range(count):
+            rows = pl.ds(pl.multiple_of(c * dims[t][1], 8), dims[t][1])
+            mine = pltpu.make_async_copy(ins[t].at[:, :, cols(t, c)], wide[t].at[:, rows, :], sems.own())
+            ss, rs = sems.pair()
+            other = pltpu.make_async_remote_copy(
+                src_ref=ins[t].at[:, :, cols(t, 1 - c)], dst_ref=wide[t].at[:, rows, :],
+                send_sem=ss, recv_sem=rs, device_id=core, device_id_type=ON_MESH)
+            other.start()
+            mine.start()
+            first.append((mine, other))
+        core_sems = [sems.pair() for t in range(count)]
+        stay = []
+        for t in range(count):
+            first[t][0].wait()
+            first[t][1].wait()
+            half[t][...] = wide[t][...].astype(jnp.bfloat16)
+            own = pltpu.make_async_copy(half[t], outs[t].at[:, z, y, x, :, cols(t, c)], sems.own())
+            own.start()
+            stay.append(own)
+
+        def block(piece, zz, yy, xx):
+            t, m0, m1, r0, r1 = piece
+            return outs[t].at[m0:m1, zz, yy, xx, r0:r1, cols(t, c)]
+
+        def to_core(p, zz, yy, xx, source=None):
+            for piece in portions[p]:
+                t = piece[0]
+                region = block(piece, zz, yy, xx)
+                pltpu.make_async_remote_copy(
+                    src_ref=region if source is None else source(piece), dst_ref=region,
+                    send_sem=core_sems[t][0], recv_sem=core_sems[t][1], device_id=core, device_id_type=ON_MESH).start()
+
+        def message(p, where, device, source=None):
+            copies = []
+            for piece in portions[p]:
+                ss, rs = sems.pair()
+                region = block(piece, *where)
+                copies.append(pltpu.make_async_remote_copy(
+                    src_ref=region if source is None else source(piece), dst_ref=region,
+                    send_sem=ss, recv_sem=rs, device_id=device, device_id_type=ON_MESH))
+            return copies
+
+        def start(copies):
+            for copy in copies:
+                copy.start()
+
+        def arrive(copies):
+            for copy in copies:
+                copy.wait_recv()
+
+        def sent(copies):
+            for copy in copies:
+                copy.wait_send()
+
+        def from_half(piece):
+            t, m0, m1, r0, r1 = piece
+            return half[t].at[m0:m1, r0:r1, :]
+
+        both = slice(0, 2)
+        a_way, b_way = (yway, xway), (xway, yway)
+        a_msgs = []
+        for p in range(2):
+            msg = message(p, (z, y, x), a_way[p], from_half)
+            start(msg)
+            a_msgs.append(msg)
+        for own in stay:
+            own.wait()
+        for p in range(2):
+            to_core(p, z, y, x, from_half)
+
+        def pair_of(p, zz):
+            return (zz, both, x) if p == 0 else (zz, y, both)
+
+        def other_of(p, zz):
+            return (zz, 1 - y, x) if p == 0 else (zz, y, 1 - x)
+
+        def far_of(p, zz):
+            return (zz, both, 1 - x) if p == 0 else (zz, 1 - y, both)
+
+        zmsg = [[[message(p, pair_of(p, z - k), up) for k in range(hops)],
+                 [message(p, pair_of(p, z + k), down) for k in range(hops)]] for p in range(2)]
+        b_msgs = []
+        for p in range(2):
+            own = message(p, pair_of(p, z), b_way[p])
+            ups = [message(p, pair_of(p, z - 1 - k), b_way[p]) for k in range(hops)]
+            downs = [message(p, pair_of(p, z + 1 + k), b_way[p]) for k in range(hops)]
+            b_msgs.append((own, ups, downs))
+
+        for p in range(2):
+            arrive(a_msgs[p])
+
+            @pl.when(has_up)
+            def _():
+                start(zmsg[p][0][0])
+
+            @pl.when(has_down)
+            def _():
+                start(zmsg[p][1][0])
+            start(b_msgs[p][0])
+            to_core(p, *other_of(p, z))
+
+        def far_own(p):
+            arrive(b_msgs[p][0])
+            to_core(p, *far_of(p, z))
+
+        def far_hop(p, k):
+            @pl.when(z - 1 - k >= 0)
+            def _():
+                arrive(b_msgs[p][1][k])
+                to_core(p, *far_of(p, z - 1 - k))
+
+            @pl.when(z + 1 + k <= hops)
+            def _():
+                arrive(b_msgs[p][2][k])
+                to_core(p, *far_of(p, z + 1 + k))
+
+        for k in range(hops):
+            for p in range(2):
+                @pl.when(z - 1 - k >= 0)
+                def _():
+                    arrive(zmsg[p][0][k])
+                    if k + 1 < hops:
+                        @pl.when(has_up)
+                        def _():
+                            start(zmsg[p][0][k + 1])
+                    start(b_msgs[p][1][k])
+                    to_core(p, *pair_of(p, z - 1 - k))
+
+                @pl.when(z + 1 + k <= hops)
+                def _():
+                    arrive(zmsg[p][1][k])
+                    if k + 1 < hops:
+                        @pl.when(has_down)
+                        def _():
+                            start(zmsg[p][1][k + 1])
+                    start(b_msgs[p][2][k])
+                    to_core(p, *pair_of(p, z + 1 + k))
+            for p in range(2):
+                if k == 0:
+                    far_own(p)
+                else:
+                    far_hop(p, k - 1)
+        for p in range(2):
+            far_hop(p, hops - 1)
+
+        for p in range(2):
+            sent(a_msgs[p])
+            sent(b_msgs[p][0])
+            for k in range(hops):
+                @pl.when((z - k >= 0) & has_up)
+                def _():
+                    sent(zmsg[p][0][k])
+
+                @pl.when((z + k <= hops) & has_down)
+                def _():
+                    sent(zmsg[p][1][k])
+
+                @pl.when(z - 1 - k >= 0)
+                def _():
+                    sent(b_msgs[p][1][k])
+
+                @pl.when(z + 1 + k <= hops)
+                def _():
+                    sent(b_msgs[p][2][k])
+        for t in range(count):
+            whole = pltpu.make_async_remote_copy(
+                src_ref=outs[t].at[:, :, :, :, :, cols(t, c)], dst_ref=outs[t].at[:, :, :, :, :, cols(t, 1 - c)],
+                send_sem=core_sems[t][0], recv_sem=core_sems[t][1], device_id=core, device_id_type=ON_MESH)
+            whole.wait_send()
+            whole.wait_recv()
+
+    outs = pl.pallas_call(
+        kernel,
+        out_shape=[jax.ShapeDtypeStruct((m, hops + 1, 2, 2, 2 * r, w), jnp.bfloat16) for m, r, w in dims],
+        in_specs=[pl.BlockSpec(memory_space=pl.ANY)] * count,
+        out_specs=[pl.BlockSpec(memory_space=pl.ANY)] * count,
+        scratch_shapes=[pltpu.VMEM((m, 2 * r, w // 2), jnp.float32) for m, r, w in dims]
+        + [pltpu.VMEM((m, 2 * r, w // 2), jnp.bfloat16) for m, r, w in dims]
+        + [pltpu.SemaphoreType.DMA((n_send,)), pltpu.SemaphoreType.DMA((n_send,)), pltpu.SemaphoreType.DMA((2 * count,))],
+        compiler_params=pltpu.CompilerParams(collective_id=collective_id, has_side_effects=True, vmem_limit_bytes=40 << 20),
+    )(*tensors)
+    return [o.reshape(m, (hops + 1) * 8 * r, w) for o, (m, r, w) in zip(outs, dims)]
+
+
+def scatter_blocks(tensors, portions, rows_own, collective_id):
+    count = len(tensors)
+    hops = 3
+    dims = [(t.shape[0], r, t.shape[2]) for t, r in zip(tensors, rows_own)]
+    views = [t.reshape(m, hops + 1, 2, 2, 2 * r, w) for t, (m, r, w) in zip(tensors, dims)]
+    pieces_total = sum(len(p) for p in portions)
+    n_send = pieces_total * (2 + 4 + 2 * hops + 1) + count
+    n_local = pieces_total * 2 + count
+    flat = [(p, piece) for p in range(2) for piece in portions[p]]
+    flat_dims = [(piece[2] - piece[1], piece[4] - piece[3], dims[piece[0]][2] // 2) for _, piece in flat]
+
+    def kernel(*refs):
+        ins, outs = refs[:count], refs[count : 2 * count]
+        k0 = 2 * count
+        acc = refs[k0 : k0 + count]
+        crecv = refs[k0 + count : k0 + 2 * count]
+        fin = refs[k0 + 2 * count : k0 + 3 * count]
+        k0 += 3 * count
+        n = len(flat)
+        b_all, u_all, d_all, a_all = (refs[k0 + i * n : k0 + (i + 1) * n] for i in range(4))
+        send, recv, local = refs[k0 + 4 * n :]
+        index = {}
+        for i, (p, piece) in enumerate(flat):
+            index.setdefault(p, []).append((i, piece))
+        dp, seq, z, y, x, c = place()
+        core = (dp, seq + 1 - 2 * c)
+        xway = (dp, seq + 2 - 4 * x)
+        yway = (dp + 1 - 2 * y, seq)
+        up, down = (dp + 2, seq), (dp - 2, seq)
+        has_up, has_down = z < hops, z > 0
+        greet([core, xway, yway], [(has_up, up), (has_down, down)])
+        sems = Sems(send, recv, local)
+        a_way, b_way = (yway, xway), (xway, yway)
+
+        def cols(t, side):
+            width = dims[t][2] // 2
+            return pl.ds(pl.multiple_of(side * width, 128), width)
+
+        def remote(src, dst, device):
+            ss, rs = sems.pair()
+            return pltpu.make_async_remote_copy(src_ref=src, dst_ref=dst, send_sem=ss, recv_sem=rs,
+                                                device_id=device, device_id_type=ON_MESH)
+
+        def place_of(p, zz, a, b):
+            return (zz, a, b) if p == 0 else (zz, b, a)
+
+        own_a, own_b = (y, x), (x, y)
+
+        def add(dst, src, lead):
+            def turn(i, _):
+                where, rest = [], i
+                for size in reversed(lead):
+                    where.append(lax.rem(rest, size))
+                    rest = rest // size
+                where = tuple(reversed(where))
+                dst[where] = (dst[where].astype(jnp.float32) + src[where].astype(jnp.float32)).astype(dst.dtype)
+                return 0
+            total = 1
+            for size in lead:
+                total *= size
+            lax.fori_loop(0, total, turn, 0)
+
+        everyz, both = slice(0, hops + 1), slice(0, 2)
+        chunks = {}
+        for far in (1, 0):
+            for p in range(2):
+                b = own_b[p] if far == 0 else 1 - own_b[p]
+                made = []
+                for i, piece in index[p]:
+                    t, m0, m1, r0, r1 = piece
+                    where = (slice(m0, m1),) + place_of(p, everyz, both, b) + (slice(r0, r1),)
+                    there = remote(ins[t].at[where + (cols(t, 1 - c),)], crecv[t].at[where], core)
+                    here = pltpu.make_async_copy(ins[t].at[where + (cols(t, c),)], acc[t].at[where], sems.own())
+                    there.start()
+                    here.start()
+                    made.append((there, here, piece, where))
+                chunks[far, p] = made
+
+        def core_add(far, p):
+            for there, here, piece, where in chunks[far, p]:
+                t, m0, m1, r0, r1 = piece
+                there.wait_recv()
+                here.wait()
+                add(acc[t].at[where], crecv[t].at[where], (m1 - m0, hops + 1, 2))
+
+        zorder = (3, 0, 2, 1)
+        b_msgs = {}
+        for p in range(2):
+            core_add(1, p)
+            for zz in zorder:
+                msgs = []
+                for i, (t, m0, m1, r0, r1) in index[p]:
+                    src = acc[t].at[(slice(m0, m1),) + place_of(p, zz, both, 1 - own_b[p]) + (slice(r0, r1),)]
+                    msgs.append(remote(src, b_all[i].at[:, zz], b_way[p]))
+                for msg in msgs:
+                    msg.start()
+                b_msgs[p, zz] = msgs
+        for p in range(2):
+            core_add(0, p)
+
+        def b_add(p, zz):
+            for msg in b_msgs[p, zz]:
+                msg.wait_recv()
+            for i, (t, m0, m1, r0, r1) in index[p]:
+                dst = acc[t].at[(slice(m0, m1),) + place_of(p, zz, both, own_b[p]) + (slice(r0, r1),)]
+                add(dst, b_all[i].at[:, zz], (m1 - m0, 2))
+
+        def mine(p, i, piece, zz):
+            t, m0, m1, r0, r1 = piece
+            return acc[t].at[(slice(m0, m1),) + place_of(p, zz, both, own_b[p]) + (slice(r0, r1),)]
+
+        up_msgs, down_msgs = {}, {}
+        for p in range(2):
+            for zz in range(hops + 1):
+                up_msgs[p, zz] = [remote(mine(p, i, piece, zz), u_all[i].at[:, zz], up) for i, piece in index[p]] if zz > 0 else None
+                down_msgs[p, zz] = [remote(mine(p, i, piece, zz), d_all[i].at[:, zz], down) for i, piece in index[p]] if zz < hops else None
+
+        def z_add(p, zz, msgs, land):
+            for msg in msgs[p, zz]:
+                msg.wait_recv()
+            for i, piece in index[p]:
+                add(mine(p, i, piece, zz), land[i].at[:, zz], (piece[2] - piece[1], 2))
+
+        def up_send(p, zz):
+            @pl.when(z < zz)
+            def _():
+                @pl.when(z > 0)
+                def _():
+                    z_add(p, zz, up_msgs, u_all)
+                for msg in up_msgs[p, zz]:
+                    msg.start()
+
+        def down_send(p, zz):
+            @pl.when(z > zz)
+            def _():
+                @pl.when(z < hops)
+                def _():
+                    z_add(p, zz, down_msgs, d_all)
+                for msg in down_msgs[p, zz]:
+                    msg.start()
+
+        for p in range(2):
+            b_add(p, 3)
+            up_send(p, 3)
+            b_add(p, 0)
+            down_send(p, 0)
+        for p in range(2):
+            b_add(p, 2)
+            up_send(p, 2)
+            b_add(p, 1)
+            down_send(p, 1)
+        for p in range(2):
+            up_send(p, 1)
+            down_send(p, 2)
+        a_msgs = {}
+        for p in range(2):
+            for zz in range(hops + 1):
+                @pl.when(z == zz)
+                def _():
+                    if zz > 0:
+                        z_add(p, zz, up_msgs, u_all)
+                    if zz < hops:
+                        z_add(p, zz, down_msgs, d_all)
+            msgs = []
+            for i, (t, m0, m1, r0, r1) in index[p]:
+                src = acc[t].at[(slice(m0, m1),) + place_of(p, z, 1 - own_a[p], own_b[p]) + (slice(r0, r1),)]
+                msgs.append(remote(src, a_all[i], a_way[p]))
+            for msg in msgs:
+                msg.start()
+            a_msgs[p] = msgs
+        for p in range(2):
+            for msg in a_msgs[p]:
+                msg.wait_recv()
+            for i, (t, m0, m1, r0, r1) in index[p]:
+                for m in range(m0, m1):
+                    part = acc[t][(m,) + place_of(p, z, own_a[p], own_b[p]) + (slice(r0, r1),)]
+                    fin[t][m, r0:r1, :] = part.astype(jnp.float32) + a_all[i][m - m0].astype(jnp.float32)
+        last = []
+        for t in range(count):
+            r = dims[t][1]
+            other = remote(fin[t].at[:, pl.ds(pl.multiple_of((1 - c) * r, 8), r), :], outs[t].at[:, :, cols(t, c)], core)
+            keep = pltpu.make_async_copy(fin[t].at[:, pl.ds(pl.multiple_of(c * r, 8), r), :], outs[t].at[:, :, cols(t, c)], sems.own())
+            other.start()
+            keep.start()
+            last.append((other, keep))
+        for made in chunks.values():
+            for there, here, piece, where in made:
+                there.wait_send()
+        for msgs in list(b_msgs.values()) + list(a_msgs.values()):
+            for msg in msgs:
+                msg.wait_send()
+        for p in range(2):
+            for zz in range(hops + 1):
+                if zz > 0:
+                    @pl.when(z < zz)
+                    def _():
+                        for msg in up_msgs[p, zz]:
+                            msg.wait_send()
+                if zz < hops:
+                    @pl.when(z > zz)
+                    def _():
+                        for msg in down_msgs[p, zz]:
+                            msg.wait_send()
+        for other, keep in last:
+            keep.wait()
+            other.wait()
+
+    bf = jnp.bfloat16
+    outs = pl.pallas_call(
+        kernel,
+        out_shape=[jax.ShapeDtypeStruct((m, r, w), jnp.float32) for m, r, w in dims],
+        in_specs=[pl.BlockSpec(memory_space=pl.ANY)] * count,
+        out_specs=[pl.BlockSpec(memory_space=pl.ANY)] * count,
+        scratch_shapes=[pltpu.VMEM((m, hops + 1, 2, 2, 2 * r, w // 2), bf) for m, r, w in dims]
+        + [pltpu.VMEM((m, hops + 1, 2, 2, 2 * r, w // 2), bf) for m, r, w in dims]
+        + [pltpu.VMEM((m, 2 * r, w // 2), jnp.float32) for m, r, w in dims]
+        + [pltpu.VMEM((m, hops + 1, 2, r, w), bf) for m, r, w in flat_dims] * 3
+        + [pltpu.VMEM((m, r, w), bf) for m, r, w in flat_dims]
+        + [pltpu.SemaphoreType.DMA((n_send,)), pltpu.SemaphoreType.DMA((n_send,)), pltpu.SemaphoreType.DMA((n_local,))],
+        compiler_params=pltpu.CompilerParams(collective_id=collective_id, has_side_effects=True, vmem_limit_bytes=50 << 20),
+    )(*views)
+    return list(lax.optimization_barrier(outs))
+
+
+def sum_everywhere(value, collective_id):
+    sizes = (("dp", lax.axis_size("dp")), ("seq", lax.axis_size("seq")))
+    steps = [(axis, 1 << bit) for axis, size in reversed(sizes) for bit in range(size.bit_length() - 1)]
+
+    def kernel(in_ref, out_ref, land, send, recv):
+        dp, seq = lax.axis_index("dp"), lax.axis_index("seq")
+        partners = []
+        for axis, step in steps:
+            mine = dp if axis == "dp" else seq
+            other = mine + step - 2 * step * lax.rem(mine // step, 2)
+            partners.append((other, seq) if axis == "dp" else (dp, other))
+        greet(partners, [])
+        out_ref[...] = in_ref[...]
+        for k, partner in enumerate(partners):
+            land[0, k] = out_ref[...]
+            copy = pltpu.make_async_remote_copy(
+                src_ref=land.at[0, k],
+                dst_ref=land.at[1, k],
+                send_sem=send.at[k],
+                recv_sem=recv.at[k],
+                device_id=partner,
+                device_id_type=ON_MESH,
+            )
+            copy.start()
+            copy.wait()
+            out_ref[...] = out_ref[...] + land[1, k]
+
+    n = len(steps)
+    out = pl.pallas_call(
+        kernel,
+        out_shape=jax.ShapeDtypeStruct((8, 128), jnp.float32),
+        in_specs=[pl.BlockSpec(memory_space=pltpu.VMEM)],
+        out_specs=pl.BlockSpec(memory_space=pltpu.VMEM),
+        scratch_shapes=[
+            pltpu.VMEM((2, n, 8, 128), jnp.float32),
+            pltpu.SemaphoreType.DMA((n,)),
+            pltpu.SemaphoreType.DMA((n,)),
+        ],
+        compiler_params=pltpu.CompilerParams(collective_id=collective_id, has_side_effects=True),
+    )(jnp.broadcast_to(value, (8, 128)))
+    return out[0, 0]
+
+
+BOTH = ("dp", "seq")
+
+
+def on_box():
+    return lax.axis_size("dp") == 8 and lax.axis_size("seq") == 4
+
+
+def gather_rows(tensors, portions, collective_id):
+    if on_box():
+        return gather_blocks(tensors, portions, collective_id)
+    return [lax.all_gather(t.astype(jnp.bfloat16), BOTH, axis=1, tiled=True) for t in tensors]
+
+
+def scatter_rows(tensors, portions, collective_id):
+    if on_box():
+        devices = lax.axis_size("dp") * lax.axis_size("seq")
+        rows = [t.shape[1] // devices for t in tensors]
+        return scatter_blocks(tensors, portions, rows, collective_id)
+    return [
+        lax.psum_scatter(t, BOTH, scatter_dimension=1, tiled=True).astype(jnp.float32) for t in tensors
+    ]
+
+
+def weight_portions(square, expand, shrink, vectors):
+    first = [(1, 0, 1, 0, 2 * expand), (0, 0, 3, 0, 2 * square)]
+    second = [(2, 0, 1, 0, 2 * shrink), (0, 3, 5, 0, 2 * square)]
+    if vectors:
+        second.append((3, 0, 1, 0, 2 * vectors))
+    return [first, second]
+
+
+def row_portions(rows):
+    return [[(0, 0, 1, 0, rows)], [(0, 0, 1, rows, 2 * rows)]]
+
+
+def as_rows(vectors):
+    lanes = -(-vectors.shape[0] // 256) * 256
+    return jnp.pad(vectors.T, ((0, 0), (0, lanes - vectors.shape[0])))[None]
 
 EXACT_MATMUL = lax.Precision.HIGHEST
 BETA_ONE = 0.9
@@ -28,29 +580,17 @@
 
 def carried_in(value, axis, join, neutral, backward):
     count, mine = (lax.axis_size(axis), lax.axis_index(axis))
-    pieces = jax.tree.map(lambda part: lax.all_gather(part, axis), value)
+    pieces = lax.all_gather(jnp.stack(value), axis)
     if backward:
-        pieces = jax.tree.map(lambda part: part[::-1], pieces)
+        pieces = pieces[::-1]
         mine = count - 1 - mine
-    running = jax.tree.map(
-        lambda part, zero: jnp.full_like(part, 0) + jnp.asarray(zero, part.dtype), value, neutral
-    )
-
-    def carried_turn(position, running):
-        longer = join(running, jax.tree.map(lambda part: part[position], pieces))
-        return jax.tree.map(lambda new, old: jnp.where(position < mine, new, old), longer, running)
-
-    return lax.fori_loop(0, count - 1, carried_turn, running)
-
-
-def combined_all(shard, axis, combine):
-    everything = jax.tree.map(lambda part: lax.all_gather(part, axis), shard)
-    leading = jax.tree.map(lambda part: part[0], everything)
-
-    def combined_turn(k, so_far):
-        return combine(so_far, jax.tree.map(lambda part: part[k], everything))
-
-    return lax.fori_loop(1, lax.axis_size(axis), combined_turn, leading)
+    running = neutral
+    for position in range(count - 1):
+        longer = join(running, tuple(pieces[position]))
+        running = tuple(
+            jnp.where(position < mine, new, old) for new, old in zip(longer, running)
+        )
+    return running
 
 
 def layer_norm(values, gain, bias):
@@ -349,14 +889,6 @@
     return (d_stream, (g_square, g_expand, g_shrink, g_params))
 
 
-def merge_soft(first_part, second_part):
-    row_top = jnp.maximum(first_part[0], second_part[0])
-    spread = first_part[1] * jnp.exp(first_part[0] - row_top) + second_part[1] * jnp.exp(
-        second_part[0] - row_top
-    )
-    return (row_top, spread, first_part[2] + second_part[2])
-
-
 def adam_update(weights, gradient, first, second, step_rate, decay_on):
     first_new = BETA_ONE * first + (1.0 - BETA_ONE) * gradient
     second_new = BETA_TWO * second + (1.0 - BETA_TWO) * gradient * gradient
@@ -395,85 +927,98 @@
     global_rows = param_stride * layers
     total_tokens = token_ids.shape[0]
 
+    vector_rows = vector_params.shape[0]
+    square_own, expand_own, shrink_own = (
+        square_weights.shape[2],
+        expand_weights.shape[1],
+        shrink_weights.shape[1],
+    )
+
     def fetch_layer(layer_id):
-        vector_rows = vector_params[layer_id * param_stride : (layer_id + 1) * param_stride]
-        if layer_id == 0:
-            vector_rows = jnp.concatenate([vector_rows, vector_params[global_rows:]], axis=0)
-        fetched = (
-            lax.all_gather(
-                square_weights[layer_id].astype(jnp.bfloat16), ("dp", "seq"), axis=1, tiled=True
-            ),
-            lax.all_gather(
-                expand_weights[layer_id].astype(jnp.bfloat16), ("dp", "seq"), axis=0, tiled=True
-            ),
-            lax.all_gather(
-                shrink_weights[layer_id].astype(jnp.bfloat16), ("dp", "seq"), axis=0, tiled=True
-            ),
-            lax.all_gather(vector_rows.astype(jnp.bfloat16), ("dp", "seq"), axis=1, tiled=True),
+        with_vectors = layer_id == 0
+        shards = [
+            square_weights[layer_id],
+            expand_weights[layer_id][None],
+            shrink_weights[layer_id][None],
+        ]
+        if with_vectors:
+            shards.append(as_rows(vector_params))
+        return gather_rows(
+            shards,
+            weight_portions(square_own, expand_own, shrink_own, with_vectors * square_own),
+            layer_id,
         )
-        return (fetched[0], fetched[1], fetched[2], fetched[3].astype(jnp.float32))
+
+    fetched = [fetch_layer(layer_id) for layer_id in range(layers)]
+    vectors_all = fetched[0][3][0, :, :vector_rows].T.astype(jnp.float32)
+    global_params = vectors_all[global_rows:]
+    blocks = [
+        (
+            fetched[layer_id][0],
+            fetched[layer_id][1][0],
+            fetched[layer_id][2][0],
+            vectors_all[layer_id * param_stride : (layer_id + 1) * param_stride],
+        )
+        for layer_id in range(layers)
+    ]
 
     columns = jnp.take(embed_table.astype(jnp.bfloat16), token_ids, axis=1)
     embedded = lax.all_to_all(
         columns, ("dp", "seq"), split_axis=1, concat_axis=0, tiled=True
     ).T.astype(jnp.float32)
-    first_block = fetch_layer(0)
-    global_params = first_block[3][param_stride:]
     stream, norm_pull_zero = jax.vjp(layer_norm, embedded, global_params[0], global_params[1])
-    kept_blocks = []
     saved_layers = []
-    gathered = first_block
     for layer_id in range(layers):
-        if layer_id > 0:
-            gathered = fetch_layer(layer_id)
-        kept_blocks.append(gathered)
-        stream, saved = layer_forward(stream, gathered)
+        stream, saved = layer_forward(stream, blocks[layer_id])
         saved_layers.append(saved)
     normed, norm_pull_last = jax.vjp(layer_norm, stream, global_params[2], global_params[3])
-    head_full = lax.all_gather(head_table.astype(jnp.bfloat16), "dp", axis=0, tiled=True)
-    vocab_part = head_full.shape[1]
+    dp_count = lax.axis_size("dp")
+    features, vocab_own = head_table.shape
+    vocab_part = vocab_own // dp_count
+    head_cut = head_table.astype(jnp.bfloat16).reshape(features, dp_count, vocab_part)
+    head_cols = lax.all_to_all(
+        head_cut.transpose(1, 0, 2), "dp", split_axis=0, concat_axis=0, tiled=True
+    ).reshape(dp_count * features, vocab_part)
     own_rows = normed.shape[0]
-    rows_all = lax.all_gather(normed.astype(jnp.bfloat16), "seq", axis=0, tiled=True)
-    seq_len = rows_all.shape[0]
-    seq_place = lax.axis_index("seq")
-    local_ids = targets - seq_place * vocab_part
-    rows_per_block = min(logit_block, seq_len)
-    block_count = seq_len // rows_per_block
+    rows_all = gather_rows([normed[None]], row_portions(own_rows), 10)[0][0]
+    marks = lax.all_gather(jnp.stack([targets, loss_mask]), "dp", axis=1, tiled=True)
+    first_column = lax.axis_index("seq") * vocab_own + lax.axis_index("dp") * vocab_part
+    local_ids = marks[0] - first_column
+    rows_per_block = min(logit_block, total_tokens)
+    block_count = total_tokens // rows_per_block
     row_blocks = rows_all.reshape(block_count, rows_per_block, rows_all.shape[1])
     id_blocks = local_ids.reshape(block_count, rows_per_block)
     column_ids = jnp.arange(vocab_part, dtype=jnp.int32)[None, :]
 
     def block_stats(step_item):
         rows_now, ids_now = step_item
-        logits = matmul(rows_now, head_full)
+        logits = matmul(rows_now, head_cols)
         row_top = jnp.max(logits, axis=1)
         spread = jnp.sum(jnp.exp(logits - row_top[:, None]), axis=1)
         picked = jnp.sum(jnp.where(column_ids == ids_now[:, None], logits, 0.0), axis=1)
         return (row_top, spread, picked)
 
-    row_tops, spreads, picks = lax.map(block_stats, (row_blocks, id_blocks))
-    row_tops, spreads, picks = combined_all(
-        (row_tops.reshape(seq_len), spreads.reshape(seq_len), picks.reshape(seq_len)),
-        "seq",
-        merge_soft,
-    )
-    log_total = row_tops + jnp.log(spreads)
-    counted = loss_mask.astype(jnp.float32)
-    losses = counted * (log_total - picks)
-    loss_part = jnp.sum(lax.dynamic_slice_in_dim(losses, seq_place * own_rows, own_rows))
+    stats = jnp.stack(lax.map(block_stats, (row_blocks, id_blocks))).reshape(3, total_tokens)
+    stats_all = lax.all_gather(stats, ("dp", "seq"))
+    row_top = jnp.max(stats_all[:, 0], axis=0)
+    spread = jnp.sum(stats_all[:, 1] * jnp.exp(stats_all[:, 0] - row_top), axis=0)
+    log_total = row_top + jnp.log(spread)
+    counted = marks[1].astype(jnp.float32)
+    losses = counted * (log_total - jnp.sum(stats_all[:, 2], axis=0))
+    loss_all = jnp.sum(losses)
     weight_rows = counted / total_tokens
 
     def block_back(grad_head, step_item):
         rows_now, ids_now, log_now, weight_now = step_item
-        logits = matmul(rows_now, head_full)
+        logits = matmul(rows_now, head_cols)
         softmax_rows = jnp.exp(logits - log_now[:, None])
         hits = (column_ids == ids_now[:, None]).astype(jnp.float32)
         d_logits = ((softmax_rows - hits) * weight_now[:, None]).astype(jnp.bfloat16)
-        return (grad_head + matmul_tn(rows_now, d_logits), matmul_nt(d_logits, head_full))
+        return (grad_head + matmul_tn(rows_now, d_logits), matmul_nt(d_logits, head_cols).astype(jnp.bfloat16))
 
     grad_head, d_rows = lax.scan(
         block_back,
-        jnp.zeros(head_full.shape, jnp.float32),
+        jnp.zeros(head_cols.shape, jnp.float32),
         (
             row_blocks,
             id_blocks,
@@ -481,32 +1026,45 @@
             weight_rows.reshape(block_count, rows_per_block),
         ),
     )
-    d_normed = lax.psum_scatter(
-        d_rows.reshape(seq_len, rows_all.shape[1]).astype(jnp.bfloat16),
-        "seq",
-        scatter_dimension=0,
-        tiled=True,
-    ).astype(jnp.float32)
-    g_head = lax.psum_scatter(
-        grad_head.astype(jnp.bfloat16), "dp", scatter_dimension=0, tiled=True
-    ).astype(jnp.float32)
+    d_normed = scatter_rows(
+        [d_rows.reshape(1, total_tokens, rows_all.shape[1])], row_portions(own_rows), 11
+    )[0][0]
+    g_head = (
+        lax.all_to_all(
+            grad_head.astype(jnp.bfloat16).reshape(dp_count, features, vocab_part),
+            "dp",
+            split_axis=0,
+            concat_axis=0,
+            tiled=True,
+        )
+        .transpose(1, 0, 2)
+        .reshape(features, vocab_own)
+        .astype(jnp.float32)
+    )
     d_stream, d_gain_last, d_bias_last = norm_pull_last(d_normed)
     layer_grads = [None] * layers
+    vector_grads = [None] * layers
     d_embedded = d_stream
     for layer_id in reversed(range(layers)):
-        gathered = fetch_layer(layer_id)
-        d_stream, grads = layer_backward(d_stream, saved_layers[layer_id], gathered)
-        g_params = grads[3]
+        d_stream, grads = layer_backward(d_stream, saved_layers[layer_id], blocks[layer_id])
+        vector_grads[layer_id] = grads[3]
+        low_grads = [
+            grads[0].astype(jnp.bfloat16),
+            grads[1].astype(jnp.bfloat16)[None],
+            grads[2].astype(jnp.bfloat16)[None],
+        ]
         if layer_id == 0:
             d_embedded, d_gain_zero, d_bias_zero = norm_pull_zero(d_stream)
-            g_params = jnp.concatenate(
-                [g_params, jnp.stack([d_gain_zero, d_bias_zero, d_gain_last, d_bias_last])], axis=0
+            all_vectors = jnp.concatenate(
+                vector_grads
+                + [jnp.stack([d_gain_zero, d_bias_zero, d_gain_last, d_bias_last])],
+                axis=0,
             )
-        layer_grads[layer_id] = (
-            lax.psum_scatter(grads[0], ("dp", "seq"), scatter_dimension=1, tiled=True),
-            lax.psum_scatter(grads[1], ("dp", "seq"), scatter_dimension=0, tiled=True),
-            lax.psum_scatter(grads[2], ("dp", "seq"), scatter_dimension=0, tiled=True),
-            lax.psum_scatter(g_params, ("dp", "seq"), scatter_dimension=1, tiled=True),
+            low_grads.append(as_rows(all_vectors).astype(jnp.bfloat16))
+        layer_grads[layer_id] = scatter_rows(
+            low_grads,
+            weight_portions(square_own, expand_own, shrink_own, (layer_id == 0) * square_own),
+            layers + layer_id,
         )
     back_columns = lax.all_to_all(
         d_embedded.T.astype(jnp.bfloat16), ("dp", "seq"), split_axis=0, concat_axis=1, tiled=True
@@ -515,19 +1073,15 @@
         back_columns.T.astype(jnp.float32), token_ids, num_segments=embed_table.shape[1]
     ).T
     g_square = jnp.stack([layer_grads[layer_id][0] for layer_id in range(layers)])
-    g_expand = jnp.stack([layer_grads[layer_id][1] for layer_id in range(layers)])
-    g_shrink = jnp.stack([layer_grads[layer_id][2] for layer_id in range(layers)])
-    vector_parts = (
-        [layer_grads[0][3][:param_stride]]
-        + [layer_grads[1][3]]
-        + [layer_grads[0][3][param_stride:]]
-    )
-    g_vector = jnp.concatenate(vector_parts, axis=0)
+    g_expand = jnp.concatenate([layer_grads[layer_id][1] for layer_id in range(layers)])
+    g_shrink = jnp.concatenate([layer_grads[layer_id][2] for layer_id in range(layers)])
+    g_vector = layer_grads[0][3][0, :, :vector_rows].T
     gradients = (g_square, g_expand, g_shrink, g_vector, g_embed, g_head)
     square_part = jnp.zeros((), jnp.float32)
     for gradient in gradients:
         square_part = square_part + jnp.sum(gradient * gradient)
-    loss_sum, square_sum = lax.psum((loss_part, square_part), ("dp", "seq"))
+    loss_sum = loss_all
+    square_sum = sum_everywhere(square_part, 12)
     grad_norm = jnp.sqrt(square_sum)
     scale = jnp.minimum(1.0, 0.5 / math.sqrt(total_tokens) / (grad_norm + 1e-06))
     weights = (

time: 2640 us -> 1480 us (0.56)
  waiting for transfers between devices: 1730 us -> 76.2 us
  Pallas kernels: 0 us -> 571 us
  blocking collectives: 197 us -> 68 us
  other arithmetic: 228 us -> 161 us
  matrix products: 291 us -> 350 us
  local copies, waits for them, and re-layouts: 122 us -> 172 us
    reduce_scatter x8 -> x0, waiting for transfers between devices: 1140 us -> none  [the longest x1 318 us: per_device(): lax.psum_scatter(grad_head.astype(jnp.bfloat16), 'dp', scatter_dimension=...]
    pallas_call x0 -> x7, Pallas kernels: none -> 571 us  [the longest x3 293 us: scatter_blocks(): pl.pallas_call(kernel, out_shape=[jax.ShapeDtypeStruct((m, r, w), jnp.flo...]
    all_gather x8 -> x1, waiting for transfers between devices: 553 us -> 62.8 us  [per_device(): stats_all = lax.all_gather(stats, ('dp', 'seq'))]
    all_gather x15 -> x5, blocking collectives: 157 us -> 68 us  [the longest x1 41.5 us: per_device(): lax.all_gather(jnp.stack([targets, loss_mask]), 'dp', axis=1, tiled=True)]
    dynamic_update_slice x6 -> x48, local copies, waits for them, and re-layouts: 0.24 us -> 43.5 us  [per_device(): lax.map(block_stats, (row_blocks, id_blocks))]
    unnamed x18 -> x1, waiting for transfers between devices: 40.1 us -> 0.02 us
    psum x1 -> x0, blocking collectives: 39.8 us -> none  [per_device(): loss_sum, square_sum = lax.psum((loss_part, square_part), ('dp', 'seq'))]
    dot_general x16 -> x30, matrix products: 58.4 us -> 82.6 us  [matmul_nt(): lax.dot_general(left, right, (((1,), (1,)), ((), ())), preferred_element_...]
  transfers between devices with their start and end apart: 27 -> 13, of which waited for: 16 -> 6; matrix products, arithmetic and copies ran while one was open for 11% -> 11% of each run, Pallas kernels for 0% -> 32%
where the time goes in v1:
time: 1480 us; the launch traced here: 1470 us
  Pallas kernels  571 us (39%)
  matrix products  350 us (24%)
  local copies, waits for them, and re-layouts  172 us (12%)
  other arithmetic  161 us (11%)
  waiting for transfers between devices  76.2 us (5%)
  blocking collectives  68 us (5%)
  starting transfers between devices  46 us (3%)
  between operations  24.8 us (2%)
    pallas_call x3, Pallas kernels, scatter_blocks(): pl.pallas_call(kernel, out_shape=[jax.ShapeDtypeStruct((m, r, w), jnp.flo...  293 us
    pallas_call x3, Pallas kernels, gather_blocks(): pl.pallas_call(kernel, out_shape=[jax.ShapeDtypeStruct((m, hops + 1, 2, 2...  254 us
    dot_general x46, matrix products, matmul(): return jnp.dot(left, right, preferred_element_type=jnp.float32)  141 us
    dot_general x30, matrix products, matmul_tn(): lax.dot_general(left, right, (((0,), (0,)), ((), ())), preferred_element_...  122 us
    dot_general x30, matrix products, matmul_nt(): lax.dot_general(left, right, (((1,), (1,)), ((), ())), preferred_element_...  82.6 us
    all_gather x1, waiting for transfers between devices, per_device(): stats_all = lax.all_gather(stats, ('dp', 'seq'))  62.8 us
    scatter-add x1, other arithmetic, per_device(): jax.ops.segment_sum(back_columns.T.astype(jnp.float32), token_ids, num_se...  54.7 us
    dynamic_update_slice x48, local copies, waits for them, and re-layouts, per_device(): lax.map(block_stats, (row_blocks, id_blocks))  43.5 us
  transfers between devices with their start and end apart: 13, of which 6 were waited for; matrix products, arithmetic and copies ran while one was open for 11% of the time, Pallas kernels for 32%

profile of v1, /device:TPU:0, one launch (start us, length us, event | category | flops | bytes accessed | tf_op | source)
XLA Modules:
  0.0 1468.9 jit_solution(3146271541260696158)
XLA Ops:
  11.4 8.6 copy.108
  20.0 28.3 %gather_fusion = bf16[8192,24]{1,0:T(8,128)(2,1)S(1)} fusion(bf16[24,50688]{0,1:T(8,128)(2,1)} %copy.108, s32[8192]{0:T(1024)S(1)} %fusion.85), kind=kCustom, calls=%fused_computation | custom fusion | bytes 819200 | tf_op jit(solution)/shard_map/jit(_take)/gather | solution.py:965
  51.7 7.4 all-to-all-start
  59.3 92.9 %shard_map.356 = (bf16[5,4,2,2,48,768]{5,4,3,2,1,0:T(8,128)(2,1)}, bf16[1,4,2,2,48,3072]{5,4,3,2,1,0:T(8,128)(2,1)S(1)}, bf16[1,4,2,2,192,768]{5,4,3,2,1,0:T(8,128)(2,1)S(1)}, bf16[1,4,2,2,48,256]{5,4,3,2,1,0:T(8,128)(2,1)S(1)}) custom-call(f32[5,24,768]{2,1,0:T(8,128)S(1)} %get-tuple-element.1031.refs_0_, f32[1,24,3072]{2,1,0:T(8,128)S(1)} %get-tuple-element.1035.refs_1_, ...), custom_call_target="tpu_custom_call" | custom-call | tf_op jit(solution)/shard_map/pallas_call | solution.py:244
  170.0 87.2 %shard_map.357 = (bf16[5,4,2,2,48,768]{5,4,3,2,1,0:T(8,128)(2,1)}, bf16[1,4,2,2,48,3072]{5,4,3,2,1,0:T(8,128)(2,1)S(1)}, bf16[1,4,2,2,192,768]{5,4,3,2,1,0:T(8,128)(2,1)S(1)}) custom-call(f32[5,24,768]{2,1,0:T(8,128)S(1)} %get-tuple-element.1030.refs_0_, f32[1,24,3072]{2,1,0:T(8,128)S(1)} %get-tuple-element.1034.refs_1_, ...), custom_call_target="tpu_custom_call" | custom-call | tf_op jit(solution)/shard_map/pallas_call | solution.py:244
  257.2 8.5 fusion.153
  284.5 6.7 all-gather.4
  310.9 41.5 %all_gather.30 = s32[2,8192]{1,0:T(2,128)S(1)} all-gather(s32[2,1024]{1,0:T(2,128)S(1)} %pad_add_fusion.4), channel_id=1, replica_groups=mesh['dp'=8,'seq'=4] {'dp'}, dimensions={1}, use_global_device_ids=true | all-gather | bytes 73728 | tf_op jit(solution)/shard_map/all_gather | solution.py:984
  378.6 73.8 %shard_map.358 = bf16[1,4,2,2,512,768]{5,4,3,2,1,0:T(8,128)(2,1)} custom-call(f32[1,256,768]{2,1,0:T(8,128)S(1)} %add_bitcast_fusion.refs_0_), custom_call_target="tpu_custom_call" | custom-call | tf_op jit(solution)/shard_map/pallas_call | solution.py:244
  452.4 113.8 %while.10 = (s32[]{:T(128)}, f32[16,512]{1,0:T(8,128)S(1)}, f32[16,512]{1,0:T(8,128)}, f32[16,512]{1,0:T(8,128)}, bf16[16,512,768]{2,1,0:T(8,128)(2,1)}, /*index...) while((s32[]{:T(128)}, f32[16,512]{1,0:T(8,128)S(1)}, ...), condition=%wide.region_20.21_spmd.clone, body=%wide.region_16.20_spmd.clone.sunk | while | flops 1250572800 | bytes 9857145 | solution.py:1001
  568.8 62.8 %all-gather.10.cloned.1.call-done = f32[32,3,8192]{2,1,0:T(4,128)} async-done(((f32[1,3,8192]{2,1,0:T(4,128)}), f32[32,3,8192]{2,1,0:T(4,128)}) %all-gather.10.cloned.1.call-update) | async-done | bytes 3145744 | tf_op jit(solution)/shard_map/all_gather | solution.py:1002
  640.4 232.5 %while.22 = (s32[]{:T(128)}, f32[768,1584]{0,1:T(8,128)}, bf16[16,512,768]{2,1,0:T(8,128)(2,1)}, bf16[16,512,768]{2,1,0:T(8,128)(2,1)}, bf16[768,1584]{1,0:T(8,1...) while((s32[]{:T(128)}, f32[768,1584]{0,1:T(8,128)}, ...), condition=%wide.region_26.27_spmd.clone, body=%wide.region_25.26_spmd.clone.sunk | while | flops 3744817152 | bytes 22087820 | solution.py:1019
  872.9 78.7 %shard_map.359 = f32[1,256,768]{2,1,0:T(8,128)S(1)} custom-call(bf16[1,4,2,2,512,768]{5,4,3,2,1,0:T(8,128)(2,1)} %bitcast.565), custom_call_target="tpu_custom_call" | custom-call | tf_op jit(solution)/shard_map/pallas_call | solution.py:465
  996.0 99.0 %shard_map.361 = (f32[5,24,768]{2,1,0:T(8,128)S(1)}, f32[1,24,3072]{2,1,0:T(8,128)S(1)}, f32[1,96,768]{2,1,0:T(8,128)S(1)}) custom-call(bf16[5,4,2,2,48,768]{5,4,3,2,1,0:T(8,128)(2,1)} %copy-done.42, bf16[1,4,2,2,48,3072]{5,4,3,2,1,0:T(8,128)(2,1)} %bitcast.549, bf16[1,4,2,2,192,768]{5,4,3,2,1,0:T(8,128)(2,1)} %bitcast.547), custom_call_target="tpu_custom_call" | custom-call | tf_op jit(solution)/shard_map/pallas_call | solution.py:465
  1119.8 8.4 all-gather.7
  1141.6 13.6 all-to-all-start.2
  1158.5 9.9 all-to-all-done.2
  1181.9 115.7 %shard_map.360 = (f32[5,24,768]{2,1,0:T(8,128)S(1)}, f32[1,24,3072]{2,1,0:T(8,128)S(1)}, f32[1,96,768]{2,1,0:T(8,128)S(1)}, f32[1,24,256]{2,1,0:T(8,128)S(1)}) custom-call(bf16[5,4,2,2,48,768]{5,4,3,2,1,0:T(8,128)(2,1)} %constant_dynamic-update-slice_fusion.refs_0_, bf16[1,4,2,2,48,3072]{5,4,3,2,1,0:T(8,128)(2,1)} %bitcast.548, ...), custom_call_target="tpu_custom_call" | custom-call | tf_op jit(solution)/shard_map/pallas_call | solution.py:465
  1308.8 54.7 %scatter_custom_fusion = f32[50688,24]{1,0:T(8,128)} fusion(s32[8192]{0:T(1024)} %param.33, f32[8192,24]{1,0:T(8,128)} %copy.117, f32[]{:T(128)} %constant.383.clone.1), kind=kCustom, calls=%fused_computation.28 | custom fusion | flops 196608 | bytes 4866560 | tf_op jit(solution)/shard_map/scatter-add | solution.py:1072
  1363.5 15.4 %copy.119 = f32[50688,24]{0,1:T(8,128)} copy(f32[50688,24]{1,0:T(8,128)} %scatter_custom_fusion) | data formatting | bytes 9732096 | tf_op jit(solution)/shard_map/scatter-add | solution.py:1072
  1378.9 10.3 multiply_reduce_fusion
  1394.8 23.3 %shard_map.362 = f32[8,128]{1,0:T(8,128)} custom-call(f32[8,128]{1,0:T(8,128)} %broadcast_in_dim.324.in_ref), custom_call_target="tpu_custom_call" | custom-call | tf_op jit(solution)/shard_map/pallas_call | solution.py:509
  1441.6 10.6 multiply_subtract_fusion.1
  1452.2 8.2 multiply_subtract_fusion
  (1008 shorter events, 577.9 us)
Async XLA Ops:
  51.7 217.5 %all-to-all-start = ((bf16[24,32,256]{2,0,1:T(8,128)(2,1)}), bf16[24,32,256]{2,0,1:T(8,128)(2,1)}, u32[]{:S(2)}, u32[]{:S(2)}) async-start(bf16[24,32,256]{2,0,1:T(8,128)(2,1)} %broadcast_select_fusion), calls=%async_computation | async-start | bytes 786432 | tf_op jit(solution)/shard_map/all_to_all | solution.py:966
  158.8 123.0 %copy-start.130 = (f32[768]{0:T(1024)}, f32[768]{0:T(1024)S(1)}, u32[]{:S(2)}) copy-start(f32[768]{0:T(1024)S(1)} %get-tuple-element.859) | copy-start | bytes 9220
  158.8 123.0 %copy-start.132 = (f32[768]{0:T(1024)}, f32[768]{0:T(1024)S(1)}, u32[]{:S(2)}) copy-start(f32[768]{0:T(1024)S(1)} %get-tuple-element.860) | copy-start | bytes 9220
  158.8 123.0 %copy-start.134 = (f32[768]{0:T(1024)}, f32[768]{0:T(1024)S(1)}, u32[]{:S(2)}) copy-start(f32[768]{0:T(1024)S(1)} %get-tuple-element.862) | copy-start | bytes 9220
  158.8 141.9 %copy-start.124 = (f32[768]{0:T(1024)}, f32[768]{0:T(1024)S(1)}, u32[]{:S(2)}) copy-start(f32[768]{0:T(1024)S(1)} %get-tuple-element.857) | copy-start | bytes 9220
  158.9 122.9 %copy-start.126 = (f32[768]{0:T(1024)}, f32[768]{0:T(1024)S(1)}, u32[]{:S(2)}) copy-start(f32[768]{0:T(1024)S(1)} %get-tuple-element.865) | copy-start | bytes 9220
  158.9 137.3 %copy-start.114 = (f32[768]{0:T(1024)}, f32[768]{0:T(1024)S(1)}, u32[]{:S(2)}) copy-start(f32[768]{0:T(1024)S(1)} %get-tuple-element.864) | copy-start | bytes 9220
  158.9 137.3 %copy-start.116 = (f32[768]{0:T(1024)}, f32[768]{0:T(1024)S(1)}, u32[]{:S(2)}) copy-start(f32[768]{0:T(1024)S(1)} %get-tuple-element.866) | copy-start | bytes 9220
  269.2 183.3 %all-to-all-start.1 = ((bf16[8,96,1584]{2,1,0:T(8,128)(2,1)}), bf16[8,96,1584]{2,1,0:T(8,128)(2,1)}, u32[]{:S(2)}, u32[]{:S(2)}) async-start(bf16[8,96,1584]{2,1,0:T(8,128)(2,1)} %bitcast.579), calls=%async_computation.1 | async-start | bytes 5111808 | tf_op jit(solution)/shard_map/all_to_all | solution.py:979
  273.8 357.9 %all-gather.10.cloned.1.call-start = ((), (), s32[]{:S(2)}) async-start(), calls=%async_computation.4 | async-start | bytes 4325376 | tf_op jit(solution)/shard_map/all_gather | solution.py:1002
  278.9 2.9 collective-permute-start
  281.2 80.4 %copy-start.185 = (f32[256]{0:T(256)}, f32[256]{0:T(256)S(1)}, u32[]{:S(2)}) copy-start(f32[256]{0:T(256)S(1)} %iota_add_fusion) | copy-start | bytes 3076
  297.7 3.0 collective-permute-start.1
  307.1 45.3 %collective-permute-start.2 = (f32[1,768]{1,0:T(1,128)S(1)}, f32[1,768]{1,0:T(1,128)S(1)}, u32[]{:S(2)}, u32[]{:S(2)}) collective-permute-start(f32[1,768]{1,0:T(1,128)S(1)} %slice.564), channel_id=1, source_target_pairs={{0,1},{1,2},{2,3},{4,5},{5,6},{6,7},{8,9},{9,10},{10,11},{12,13},{... | collective-permute-start | bytes 9224 | tf_op jit(solution)/shard_map/ppermute | solution.py:578
  365.9 3.0 collective-permute-start.3
  872.9 80.4 %slice-start.4 = ((s8[4718592]{0:T(1024)(128)(4,1)}), s8[4194304]{0:T(1024)(128)(4,1)S(1)}, s32[]{:S(2)}) async-start(s8[4718592]{0:T(1024)(128)(4,1)} %bitcast.527), calls=%async_computation.9 | async-start | bytes 8388608
  966.9 6.7 collective-permute-start.4
  990.7 104.4 %collective-permute-start.5 = (f32[1,768]{1,0:T(1,128)S(1)}, f32[1,768]{1,0:T(1,128)S(1)}, u32[]{:S(2)}, u32[]{:S(2)}) collective-permute-start(f32[1,768]{1,0:T(1,128)S(1)} %split.57), channel_id=1, source_target_pairs={{1,0},{2,1},{3,2},{5,4},{6,5},{7,6},{9,8},{10,9},{11,10},{13,12},{... | collective-permute-start | bytes 9224 | tf_op jit(solution)/shard_map/ppermute | solution.py:578
  996.0 99.2 %copy-start.13 = (f32[256,768]{1,0:T(8,128)S(1)}, f32[256,768]{1,0:T(8,128)}, u32[]{:S(2)}) copy-start(f32[256,768]{1,0:T(8,128)} %copy-done.12) | copy-start | bytes 2359300
  996.0 99.6 %copy-start.223 = (f32[256]{0:T(256)S(1)}, f32[256]{0:T(256)}, u32[]{:S(2)}) copy-start(f32[256]{0:T(256)} %copy-done.222) | copy-start | bytes 3076
  1111.8 3.2 collective-permute-start.6
  1133.5 3.2 collective-permute-start.7
  1141.6 26.7 %all-to-all-start.2 = ((bf16[32,24,256]{2,1,0:T(8,128)(2,1)}), bf16[32,24,256]{2,1,0:T(8,128)(2,1)}, u32[]{:S(2)}, u32[]{:S(2)}) async-start(bf16[32,24,256]{2,1,0:T(8,128)(2,1)} %bitcast.605), calls=%async_computation.2 | async-start | bytes 786432 | tf_op jit(solution)/shard_map/all_to_all | solution.py:1069
  1168.4 221.5 %all-to-all-start.3 = ((bf16[8,96,1584]{2,1,0:T(8,128)(2,1)}), bf16[8,96,1584]{2,1,0:T(8,128)(2,1)}, u32[]{:S(2)}, u32[]{:S(2)}) async-start(bf16[8,96,1584]{2,1,0:T(8,128)(2,1)} %bitcast.578), calls=%async_computation.3 | async-start | bytes 5111808 | tf_op jit(solution)/shard_map/all_to_all | solution.py:1033
  (242 other events, 2183.7 us)
Sparse Core Ops, SparseCore 0:
  568.8 62.7 all-gather.9

commit v2 on v1

--- a/solution.py
+++ b/solution.py
@@ -478,11 +478,11 @@
     return list(lax.optimization_barrier(outs))
 
 
-def sum_everywhere(value, collective_id):
+def exchange_everywhere(value, combine, collective_id):
     sizes = (("dp", lax.axis_size("dp")), ("seq", lax.axis_size("seq")))
     steps = [(axis, 1 << bit) for axis, size in reversed(sizes) for bit in range(size.bit_length() - 1)]
 
-    def kernel(in_ref, out_ref, land, send, recv):
+    def kernel(in_ref, out_ref, leave, land, send, recv):
         dp, seq = lax.axis_index("dp"), lax.axis_index("seq")
         partners = []
         for axis, step in steps:
@@ -490,12 +490,11 @@
             other = mine + step - 2 * step * lax.rem(mine // step, 2)
             partners.append((other, seq) if axis == "dp" else (dp, other))
         greet(partners, [])
-        out_ref[...] = in_ref[...]
+        leave[0] = in_ref[...]
         for k, partner in enumerate(partners):
-            land[0, k] = out_ref[...]
             copy = pltpu.make_async_remote_copy(
-                src_ref=land.at[0, k],
-                dst_ref=land.at[1, k],
+                src_ref=leave.at[k],
+                dst_ref=land.at[k],
                 send_sem=send.at[k],
                 recv_sem=recv.at[k],
                 device_id=partner,
@@ -503,25 +502,202 @@
             )
             copy.start()
             copy.wait()
-            out_ref[...] = out_ref[...] + land[1, k]
+            both = combine(leave[k], land[k])
+            if k + 1 < len(steps):
+                leave[k + 1] = both
+            else:
+                out_ref[...] = both
 
     n = len(steps)
-    out = pl.pallas_call(
+    return pl.pallas_call(
         kernel,
-        out_shape=jax.ShapeDtypeStruct((8, 128), jnp.float32),
+        out_shape=jax.ShapeDtypeStruct(value.shape, jnp.float32),
         in_specs=[pl.BlockSpec(memory_space=pltpu.VMEM)],
         out_specs=pl.BlockSpec(memory_space=pltpu.VMEM),
         scratch_shapes=[
-            pltpu.VMEM((2, n, 8, 128), jnp.float32),
+            pltpu.VMEM((n,) + value.shape, jnp.float32),
+            pltpu.VMEM((n,) + value.shape, jnp.float32),
             pltpu.SemaphoreType.DMA((n,)),
             pltpu.SemaphoreType.DMA((n,)),
         ],
         compiler_params=pltpu.CompilerParams(collective_id=collective_id, has_side_effects=True),
-    )(jnp.broadcast_to(value, (8, 128)))
-    return out[0, 0]
+    )(value)
+
+
+def add_logs(left, right):
+    return jnp.maximum(left, right) + jnp.log(1.0 + jnp.exp(-jnp.abs(left - right)))
+
+
+def head_forward(rows_all, head_cols, local_ids, tile, sub):
+    tokens, features = rows_all.shape
+    width = head_cols.shape[1]
+
+    def kernel(rows_ref, head_ref, ids_ref, p_ref, stats_ref):
+        ids = jnp.transpose(jnp.broadcast_to(ids_ref[...], (128, tile)))[:, :1]
+        lane = lax.broadcasted_iota(jnp.int32, (sub, 128), 1)
+        column = lax.broadcasted_iota(jnp.int32, (sub, width), 1)
+        for part in range(tile // sub):
+            here = slice(part * sub, (part + 1) * sub)
+            logits = jnp.dot(rows_ref[here, :], head_ref[...], preferred_element_type=jnp.float32)
+            top = jnp.max(logits, axis=1, keepdims=True)
+            picked = jnp.sum(jnp.where(column == ids[here], logits, 0.0), axis=1, keepdims=True)
+            lifted = jnp.exp(logits - top)
+            spread = jnp.sum(lifted, axis=1, keepdims=True)
+            p_ref[here, :] = lifted.astype(jnp.bfloat16)
+            table = jnp.where(lane == 0, top, jnp.where(lane == 1, spread, picked))
+            stats_ref[:, here] = jnp.transpose(table)[:8]
+
+    return pl.pallas_call(
+        kernel,
+        grid=(tokens // tile,),
+        out_shape=[
+            jax.ShapeDtypeStruct((tokens, width), jnp.bfloat16),
+            jax.ShapeDtypeStruct((8, tokens), jnp.float32),
+        ],
+        in_specs=[
+            pl.BlockSpec((tile, features), lambda i: (i, 0)),
+            pl.BlockSpec((features, width), lambda i: (0, 0)),
+            pl.BlockSpec((1, tile), lambda i: (0, i)),
+        ],
+        out_specs=[
+            pl.BlockSpec((tile, width), lambda i: (i, 0)),
+            pl.BlockSpec((8, tile), lambda i: (0, i)),
+        ],
+        compiler_params=pltpu.CompilerParams(vmem_limit_bytes=50 << 20),
+    )(rows_all, head_cols, local_ids[None])
+
+
+def head_backward(lifted, rows_all, head_cols, local_ids, factors, tile, sub):
+    tokens, width = lifted.shape
+    features = rows_all.shape[1]
+    steps = tokens // tile
+
+    def kernel(p_ref, rows_ref, head_ref, ids_ref, factor_ref, d_rows_ref, d_head_ref, squares_ref, d_logits, total):
+        step = pl.program_id(0)
+        ids = jnp.transpose(jnp.broadcast_to(ids_ref[...], (128, tile)))[:, :1]
+        scales = jnp.transpose(jnp.concatenate([factor_ref[...]] * 16, axis=0))
+        scale, hit = scales[:, :1], scales[:, 1:2]
+        column = lax.broadcasted_iota(jnp.int32, (sub, width), 1)
+        for part in range(tile // sub):
+            here = slice(part * sub, (part + 1) * sub)
+            d_logits[here, :] = jnp.where(
+                column == ids[here], hit[here], p_ref[here, :].astype(jnp.float32) * scale[here]
+            ).astype(jnp.bfloat16)
+            d_rows_ref[here, :] = lax.dot_general(
+                d_logits[here, :], head_ref[...], (((1,), (1,)), ((), ())), preferred_element_type=jnp.float32
+            ).astype(jnp.bfloat16)
+        term = lax.dot_general(
+            rows_ref[...], d_logits[...], (((0,), (0,)), ((), ())), preferred_element_type=jnp.float32
+        )
+
+        @pl.when(step == 0)
+        def _():
+            total[...] = term
+
+        @pl.when(step > 0)
+        def _():
+            total[...] += term
+
+        @pl.when(step == steps - 1)
+        def _():
+            low = total[...].astype(jnp.bfloat16)
+            d_head_ref[...] = low
+            wide = low.astype(jnp.float32)
+            squares_ref[...] = jnp.sum((wide * wide).reshape(features // 8, 8, width), axis=0)
+
+    return pl.pallas_call(
+        kernel,
+        grid=(steps,),
+        out_shape=[
+            jax.ShapeDtypeStruct((tokens, features), jnp.bfloat16),
+            jax.ShapeDtypeStruct((features, width), jnp.bfloat16),
+            jax.ShapeDtypeStruct((8, width), jnp.float32),
+        ],
+        in_specs=[
+            pl.BlockSpec((tile, width), lambda i: (i, 0)),
+            pl.BlockSpec((tile, features), lambda i: (i, 0)),
+            pl.BlockSpec((features, width), lambda i: (0, 0)),
+            pl.BlockSpec((1, tile), lambda i: (0, i)),
+            pl.BlockSpec((8, tile), lambda i: (0, i)),
+        ],
+        out_specs=[
+            pl.BlockSpec((tile, features), lambda i: (i, 0)),
+            pl.BlockSpec((features, width), lambda i: (0, 0)),
+            pl.BlockSpec((8, width), lambda i: (0, 0)),
+        ],
+        scratch_shapes=[pltpu.VMEM((tile, width), jnp.bfloat16), pltpu.VMEM((features, width), jnp.float32)],
+        compiler_params=pltpu.CompilerParams(vmem_limit_bytes=56 << 20),
+    )(lifted, rows_all, head_cols, local_ids[None], factors)
+
+
+def embed_gradient(columns, token_ids, vocab, block):
+    features, tokens = columns.shape
+    lanes = 128
+    high_rows = -(-vocab // (8 * lanes)) * 8
+    group = 2
+    steps = tokens // block
+
+    def kernel(columns_ref, ids_ref, out_ref, squares_ref):
+        step = pl.program_id(0)
+        ids = ids_ref[...]
+        high = lax.broadcasted_iota(jnp.int32, (high_rows, block), 0) == lax.shift_right_logical(ids, 7)
+        high = jnp.where(high, 1.0, 0.0).astype(jnp.bfloat16)
+        low = lax.broadcasted_iota(jnp.int32, (lanes, block), 0) == jnp.bitwise_and(ids, lanes - 1)
+        values = columns_ref[...].astype(jnp.float32)
+
+        @pl.when(step == 0)
+        def _():
+            out_ref[...] = jnp.zeros_like(out_ref)
+
+        for first in range(0, features, group):
+            spread = jnp.concatenate(
+                [jnp.where(low, values[f : f + 1], 0.0).astype(jnp.bfloat16) for f in range(first, first + group)], axis=0
+            )
+            term = lax.dot_general(high, spread, (((1,), (1,)), ((), ())), preferred_element_type=jnp.float32)
+            for k in range(group):
+                out_ref[first + k] += term[:, k * lanes : (k + 1) * lanes]
+
+        @pl.when(step == steps - 1)
+        def _():
+            def turn(f, total):
+                one = out_ref[f]
+                return total + jnp.sum((one * one).reshape(high_rows // 8, 8, lanes), axis=0)
+            squares_ref[...] = lax.fori_loop(0, features, turn, jnp.zeros((8, lanes), jnp.float32))
+
+    sums, squares = pl.pallas_call(
+        kernel,
+        grid=(steps,),
+        out_shape=[
+            jax.ShapeDtypeStruct((features, high_rows, lanes), jnp.float32),
+            jax.ShapeDtypeStruct((8, lanes), jnp.float32),
+        ],
+        in_specs=[pl.BlockSpec((features, block), lambda i: (0, i)), pl.BlockSpec((1, block), lambda i: (0, i))],
+        out_specs=[
+            pl.BlockSpec((features, high_rows, lanes), lambda i: (0, 0, 0)),
+            pl.BlockSpec((8, lanes), lambda i: (0, 0)),
+        ],
+        compiler_params=pltpu.CompilerParams(vmem_limit_bytes=50 << 20),
+    )(columns, token_ids[None])
+    return sums[:, : vocab // lanes].reshape(features, vocab), squares
 
 
 BOTH = ("dp", "seq")
+mark_height = 8
+
+
+def mark_rows(targets, loss_mask):
+    own = targets.shape[0] // lax.axis_size("seq")
+    first = lax.axis_index("seq") * own
+    own_targets = lax.dynamic_slice_in_dim(targets, first, own)
+    own_mask = lax.dynamic_slice_in_dim(loss_mask, first, own)
+    rows = jnp.stack([own_targets // 256, own_targets % 256, own_mask]).astype(jnp.float32)
+    return jnp.pad(rows, ((0, mark_height - 3), (0, 0)))[None]
+
+
+def marks_of(gathered):
+    rows = gathered[0].reshape(-1, mark_height, gathered.shape[2]).astype(jnp.float32)
+    numbers = rows[:, :3].transpose(1, 0, 2).reshape(3, -1).astype(jnp.int32)
+    return (numbers[0] * 256 + numbers[1], numbers[2])
 
 
 def on_box():
@@ -531,6 +707,10 @@
 def gather_rows(tensors, portions, collective_id):
     if on_box():
         return gather_blocks(tensors, portions, collective_id)
+    return gather_plain(tensors)
+
+
+def gather_plain(tensors):
     return [lax.all_gather(t.astype(jnp.bfloat16), BOTH, axis=1, tiled=True) for t in tensors]
 
 
@@ -539,16 +719,37 @@
         devices = lax.axis_size("dp") * lax.axis_size("seq")
         rows = [t.shape[1] // devices for t in tensors]
         return scatter_blocks(tensors, portions, rows, collective_id)
+    return scatter_plain(tensors)
+
+
+def scatter_plain(tensors):
     return [
         lax.psum_scatter(t, BOTH, scatter_dimension=1, tiled=True).astype(jnp.float32) for t in tensors
     ]
 
 
-def weight_portions(square, expand, shrink, vectors):
+def scatter_joined(tensors):
+    square, expand, shrink = tensors
+    width = square.shape[2]
+    cut = [expand[:, :, k : k + width] for k in range(0, expand.shape[2], width)]
+    both = lax.psum_scatter(
+        jnp.concatenate([square] + cut), BOTH, scatter_dimension=1, tiled=True
+    ).astype(jnp.float32)
+    count = square.shape[0]
+    return [
+        both[:count],
+        jnp.concatenate([both[k : k + 1] for k in range(count, both.shape[0])], axis=2),
+        lax.psum_scatter(shrink, BOTH, scatter_dimension=1, tiled=True).astype(jnp.float32),
+    ]
+
+
+def weight_portions(square, expand, shrink, vectors, marks=0):
     first = [(1, 0, 1, 0, 2 * expand), (0, 0, 3, 0, 2 * square)]
     second = [(2, 0, 1, 0, 2 * shrink), (0, 3, 5, 0, 2 * square)]
     if vectors:
         second.append((3, 0, 1, 0, 2 * vectors))
+    if marks:
+        first.append((4, 0, 1, 0, 2 * marks))
     return [first, second]
 
 
@@ -568,7 +769,8 @@
 LEARN_RATES = (0.03, 0.03, 0.015, 0.5, 2.0, 0.05)
 DECAY_FLAGS = (True, True, True, False, True, True)
 param_stride = 11
-logit_block = 512
+head_tile = 1024
+embed_block = 1024
 scan_block = 256
 
 
@@ -943,9 +1145,18 @@
         ]
         if with_vectors:
             shards.append(as_rows(vector_params))
+            shards.append(mark_rows(targets, loss_mask))
+        else:
+            return gather_plain(shards)
         return gather_rows(
             shards,
-            weight_portions(square_own, expand_own, shrink_own, with_vectors * square_own),
+            weight_portions(
+                square_own,
+                expand_own,
+                shrink_own,
+                with_vectors * square_own,
+                with_vectors * mark_height,
+            ),
             layer_id,
         )
 
@@ -981,57 +1192,34 @@
     ).reshape(dp_count * features, vocab_part)
     own_rows = normed.shape[0]
     rows_all = gather_rows([normed[None]], row_portions(own_rows), 10)[0][0]
-    marks = lax.all_gather(jnp.stack([targets, loss_mask]), "dp", axis=1, tiled=True)
+    all_targets, all_mask = marks_of(fetched[0][4])
     first_column = lax.axis_index("seq") * vocab_own + lax.axis_index("dp") * vocab_part
-    local_ids = marks[0] - first_column
-    rows_per_block = min(logit_block, total_tokens)
-    block_count = total_tokens // rows_per_block
-    row_blocks = rows_all.reshape(block_count, rows_per_block, rows_all.shape[1])
-    id_blocks = local_ids.reshape(block_count, rows_per_block)
-    column_ids = jnp.arange(vocab_part, dtype=jnp.int32)[None, :]
-
-    def block_stats(step_item):
-        rows_now, ids_now = step_item
-        logits = matmul(rows_now, head_cols)
-        row_top = jnp.max(logits, axis=1)
-        spread = jnp.sum(jnp.exp(logits - row_top[:, None]), axis=1)
-        picked = jnp.sum(jnp.where(column_ids == ids_now[:, None], logits, 0.0), axis=1)
-        return (row_top, spread, picked)
-
-    stats = jnp.stack(lax.map(block_stats, (row_blocks, id_blocks))).reshape(3, total_tokens)
-    stats_all = lax.all_gather(stats, ("dp", "seq"))
-    row_top = jnp.max(stats_all[:, 0], axis=0)
-    spread = jnp.sum(stats_all[:, 1] * jnp.exp(stats_all[:, 0] - row_top), axis=0)
-    log_total = row_top + jnp.log(spread)
-    counted = marks[1].astype(jnp.float32)
-    losses = counted * (log_total - jnp.sum(stats_all[:, 2], axis=0))
-    loss_all = jnp.sum(losses)
+    local_ids = all_targets - first_column
+    tile = min(head_tile, total_tokens)
+    lifted, stats = head_forward(rows_all, head_cols, local_ids, tile, tile // 4)
+    own_log = stats[0] + jnp.log(stats[1])
+    log_total = exchange_everywhere(own_log.reshape(-1, 128), add_logs, 13).reshape(-1)
+    counted = all_mask.astype(jnp.float32)
+    picked_part = jnp.sum(counted * stats[2])
     weight_rows = counted / total_tokens
-
-    def block_back(grad_head, step_item):
-        rows_now, ids_now, log_now, weight_now = step_item
-        logits = matmul(rows_now, head_cols)
-        softmax_rows = jnp.exp(logits - log_now[:, None])
-        hits = (column_ids == ids_now[:, None]).astype(jnp.float32)
-        d_logits = ((softmax_rows - hits) * weight_now[:, None]).astype(jnp.bfloat16)
-        return (grad_head + matmul_tn(rows_now, d_logits), matmul_nt(d_logits, head_cols).astype(jnp.bfloat16))
-
-    grad_head, d_rows = lax.scan(
-        block_back,
-        jnp.zeros(head_cols.shape, jnp.float32),
-        (
-            row_blocks,
-            id_blocks,
-            log_total.reshape(block_count, rows_per_block),
-            weight_rows.reshape(block_count, rows_per_block),
+    factors = jnp.pad(
+        jnp.stack(
+            [
+                jnp.exp(stats[0] - log_total) * weight_rows,
+                (jnp.exp(stats[2] - log_total) - 1.0) * weight_rows,
+            ]
         ),
+        ((0, 6), (0, 0)),
+    )
+    d_rows, grad_head, head_squares = head_backward(
+        lifted, rows_all, head_cols, local_ids, factors, tile, tile // 2
     )
     d_normed = scatter_rows(
-        [d_rows.reshape(1, total_tokens, rows_all.shape[1])], row_portions(own_rows), 11
+        [d_rows[None]], row_portions(own_rows), 11
     )[0][0]
     g_head = (
         lax.all_to_all(
-            grad_head.astype(jnp.bfloat16).reshape(dp_count, features, vocab_part),
+            grad_head.reshape(dp_count, features, vocab_part),
             "dp",
             split_axis=0,
             concat_axis=0,
@@ -1061,27 +1249,30 @@
                 axis=0,
             )
             low_grads.append(as_rows(all_vectors).astype(jnp.bfloat16))
-        layer_grads[layer_id] = scatter_rows(
-            low_grads,
-            weight_portions(square_own, expand_own, shrink_own, (layer_id == 0) * square_own),
-            layers + layer_id,
-        )
+        if layer_id > 0:
+            layer_grads[layer_id] = scatter_joined(low_grads)
+        else:
+            layer_grads[layer_id] = scatter_rows(
+                low_grads, weight_portions(square_own, expand_own, shrink_own, square_own), layers
+            )
     back_columns = lax.all_to_all(
         d_embedded.T.astype(jnp.bfloat16), ("dp", "seq"), split_axis=0, concat_axis=1, tiled=True
     )
-    g_embed = jax.ops.segment_sum(
-        back_columns.T.astype(jnp.float32), token_ids, num_segments=embed_table.shape[1]
-    ).T
+    g_embed, embed_squares = embed_gradient(
+        back_columns, token_ids, embed_table.shape[1], min(embed_block, total_tokens)
+    )
     g_square = jnp.stack([layer_grads[layer_id][0] for layer_id in range(layers)])
     g_expand = jnp.concatenate([layer_grads[layer_id][1] for layer_id in range(layers)])
     g_shrink = jnp.concatenate([layer_grads[layer_id][2] for layer_id in range(layers)])
     g_vector = layer_grads[0][3][0, :, :vector_rows].T
     gradients = (g_square, g_expand, g_shrink, g_vector, g_embed, g_head)
-    square_part = jnp.zeros((), jnp.float32)
-    for gradient in gradients:
+    square_part = jnp.sum(embed_squares) + jnp.sum(head_squares)
+    for gradient in gradients[:4]:
         square_part = square_part + jnp.sum(gradient * gradient)
-    loss_sum = loss_all
-    square_sum = sum_everywhere(square_part, 12)
+    parts = jnp.stack([square_part, picked_part])
+    parts = exchange_everywhere(jnp.broadcast_to(jnp.pad(parts, (0, 6))[:, None], (8, 128)), jnp.add, 12)
+    square_sum = parts[0, 0]
+    loss_sum = jnp.sum(counted * log_total) - parts[1, 0]
     grad_norm = jnp.sqrt(square_sum)
     scale = jnp.minimum(1.0, 0.5 / math.sqrt(total_tokens) / (grad_norm + 1e-06))
     weights = (

time: 1480 us -> 1030 us (0.70)
  matrix products: 350 us -> 87.6 us
  waiting for transfers between devices: 76.2 us -> 8.48 us
  other arithmetic: 161 us -> 105 us
  local copies, waits for them, and re-layouts: 172 us -> 121 us
  blocking collectives: 68 us -> 27.4 us
  Pallas kernels: 571 us -> 595 us
    pallas_call x1 -> x5, Pallas kernels: 23.3 us -> 178 us  [the longest x1 61.1 us: head_backward(): pl.pallas_call(kernel, grid=(steps,), out_shape=[jax.ShapeDtypeStruct((to...]
    dot_general x46 -> x14, matrix products: 141 us -> 39.1 us  [matmul(): return jnp.dot(left, right, preferred_element_type=jnp.float32)]
    dot_general x30 -> x14, matrix products: 122 us -> 23.3 us  [matmul_tn(): lax.dot_general(left, right, (((0,), (0,)), ((), ())), preferred_element_...]
    pallas_call x3 -> x2, Pallas kernels: 293 us -> 217 us  [scatter_blocks(): pl.pallas_call(kernel, out_shape=[jax.ShapeDtypeStruct((m, r, w), jnp.flo...]
    all_gather x1 -> x3, waiting for transfers between devices: 62.8 us -> 0.01 us  [gather_plain(): lax.all_gather(t.astype(jnp.bfloat16), BOTH, axis=1, tiled=True)]
    dot_general x30 -> x14, matrix products: 82.6 us -> 21.1 us  [matmul_nt(): lax.dot_general(left, right, (((1,), (1,)), ((), ())), preferred_element_...]
    scatter-add x1 -> x0, other arithmetic: 54.7 us -> none  [per_device(): jax.ops.segment_sum(back_columns.T.astype(jnp.float32), token_ids, num_se...]
    pallas_call x3 -> x2, Pallas kernels: 254 us -> 200 us  [gather_blocks(): pl.pallas_call(kernel, out_shape=[jax.ShapeDtypeStruct((m, hops + 1, 2, 2...]
  transfers between devices with their start and end apart: 13 -> 17, of which waited for: 6 -> 5; matrix products, arithmetic and copies ran while one was open for 11% -> 23% of each run, Pallas kernels for 32% -> 39%
where the time goes in v2:
time: 1030 us; the launch traced here: 1020 us
  Pallas kernels  595 us (58%)
  local copies, waits for them, and re-layouts  121 us (12%)
  other arithmetic  105 us (10%)
  matrix products  87.6 us (9%)
  starting transfers between devices  47.7 us (5%)
  blocking collectives  27.4 us (3%)
  between operations  27.2 us (3%)
    pallas_call x2, Pallas kernels, scatter_blocks(): pl.pallas_call(kernel, out_shape=[jax.ShapeDtypeStruct((m, r, w), jnp.flo...  217 us
    pallas_call x2, Pallas kernels, gather_blocks(): pl.pallas_call(kernel, out_shape=[jax.ShapeDtypeStruct((m, hops + 1, 2, 2...  200 us
    pallas_call x1, Pallas kernels, head_backward(): pl.pallas_call(kernel, grid=(steps,), out_shape=[jax.ShapeDtypeStruct((to...  61.1 us
    pallas_call x2, Pallas kernels, exchange_everywhere(): pl.pallas_call(kernel, out_shape=jax.ShapeDtypeStruct(value.shape, jnp.fl...  51.9 us
    dot_general x14, matrix products, matmul(): return jnp.dot(left, right, preferred_element_type=jnp.float32)  39.1 us
    pallas_call x1, Pallas kernels, head_forward(): pl.pallas_call(kernel, grid=(tokens // tile,), out_shape=[jax.ShapeDtypeS...  36.7 us
    unnamed x584, local copies, waits for them, and re-layouts  33.6 us
    gather x2, local copies, waits for them, and re-layouts, per_device(): columns = jnp.take(embed_table.astype(jnp.bfloat16), token_ids, axis=1)  29.2 us
  transfers between devices with their start and end apart: 17, of which 5 were waited for; matrix products, arithmetic and copies ran while one was open for 23% of the time, Pallas kernels for 39%

profile of v2, /device:TPU:0, one launch (start us, length us, event | category | flops | bytes accessed | tf_op | source)
XLA Modules:
  0.0 1019.6 jit_solution(17572692883588044698)
XLA Ops:
  13.3 8.6 copy.68
  21.9 28.4 %gather_fusion = bf16[8192,24]{1,0:T(8,128)(2,1)S(1)} fusion(bf16[24,50688]{0,1:T(8,128)(2,1)} %copy.68, s32[8192]{0:T(1024)S(1)} %fusion.97), kind=kCustom, calls=%fused_computation | custom fusion | bytes 819200 | tf_op jit(solution)/shard_map/jit(_take)/gather | solution.py:1176
  52.0 7.2 all-to-all-start
  64.6 125.8 %shard_map.356 = (bf16[5,4,2,2,48,768]{5,4,3,2,1,0:T(8,128)(2,1)}, bf16[1,4,2,2,48,3072]{5,4,3,2,1,0:T(8,128)(2,1)S(1)}, bf16[1,4,2,2,192,768]{5,4,3,2,1,0:T(8,1...) custom-call(f32[5,24,768]{2,1,0:T(8,128)S(1)} %slice_bitcast_fusion.16.refs_0_, ...), custom_call_target="tpu_custom_call" | custom-call | tf_op jit(solution)/shard_map/pallas_call | solution.py:244
  208.2 5.4 fusion.165
  235.0 6.4 all-gather.5
  273.4 7.7 all-gather.6
  298.3 5.5 fusion.13
  312.8 74.3 %shard_map.357 = bf16[1,4,2,2,512,768]{5,4,3,2,1,0:T(8,128)(2,1)S(1)} custom-call(f32[1,256,768]{2,1,0:T(8,128)S(1)} %add_bitcast_fusion.refs_0_), custom_call_target="tpu_custom_call" | custom-call | tf_op jit(solution)/shard_map/pallas_call | solution.py:244
  391.6 36.7 %shard_map.358 = (bf16[8192,1584]{1,0:T(8,128)(2,1)}, f32[8,8192]{1,0:T(8,128)S(1)}) custom-call(bf16[8192,768]{1,0:T(8,128)(2,1)} %bitcast.518, bf16[768,1584]{1,0:T(8,128)(2,1)S(1)} %bitcast.520, s32[1,8192]{1,0:T(1,128)S(1)} %bitcast.530), custom_call_target="tpu_custom_call" | custom-call | tf_op jit(solution)/shard_map/pallas_call | solution.py:550
  428.9 16.9 %shard_map.359 = f32[64,128]{1,0:T(8,128)} custom-call(f32[64,128]{1,0:T(8,128)} %bitcast.592), custom_call_target="tpu_custom_call" | custom-call | tf_op jit(solution)/shard_map/pallas_call | solution.py:512
  448.0 61.1 %shard_map.360 = (bf16[8192,768]{1,0:T(8,128)(2,1)}, bf16[768,1584]{1,0:T(8,128)(2,1)}, f32[8,1584]{1,0:T(8,128)}) custom-call(bf16[8192,1584]{1,0:T(8,128)(2,1)} %get-tuple-element.472.p_ref, bf16[8192,768]{1,0:T(8,128)(2,1)} %bitcast.519, bf16[768,1584]{1,0:T(8,128)(2,1)} %bitcast.521, s32[1,8192]{1,0:T(1,128)} %bitcast.531, ...), custom_call_target="tpu_custom_call" | custom-call | tf_op jit(solution)/shard_map/pallas_call | solution.py:608
  509.2 80.2 %shard_map.361 = f32[1,256,768]{2,1,0:T(8,128)S(1)} custom-call(bf16[1,4,2,2,512,768]{5,4,3,2,1,0:T(8,128)(2,1)} %bitcast.563), custom_call_target="tpu_custom_call" | custom-call | tf_op jit(solution)/shard_map/pallas_call | solution.py:465
  624.9 6.2 all-gather.7
  675.4 7.1 all-gather.8
  696.0 15.4 %all-to-all-start.2 = ((bf16[32,24,256]{2,1,0:T(8,128)(2,1)}), bf16[32,24,256]{2,1,0:T(8,128)(2,1)}, u32[]{:S(2)}, u32[]{:S(2)}) async-start(bf16[32,24,256]{2,1,0:T(8,128)(2,1)} %bitcast.587), calls=%async_computation.2 | async-start | bytes 786432 | tf_op jit(solution)/shard_map/all_to_all | solution.py:1258
  720.3 5.8 all-to-all-done.2
  743.1 137.3 %shard_map.363 = (f32[5,24,768]{2,1,0:T(8,128)S(1)}, f32[1,24,3072]{2,1,0:T(8,128)S(1)}, f32[1,96,768]{2,1,0:T(8,128)S(1)}, f32[1,24,256]{2,1,0:T(8,128)S(1)}) custom-call(bf16[5,4,2,2,48,768]{5,4,3,2,1,0:T(8,128)(2,1)} %constant_dynamic-update-slice_fusion.refs_0_, bf16[1,4,2,2,48,3072]{5,4,3,2,1,0:T(8,128)(2,1)} %bitcast.541, ...), custom_call_target="tpu_custom_call" | custom-call | tf_op jit(solution)/shard_map/pallas_call | solution.py:465
  882.1 28.1 %shard_map.362 = (f32[24,400,128]{2,1,0:T(8,128)}, f32[8,128]{1,0:T(8,128)S(1)}) custom-call(bf16[24,8192]{1,0:T(8,128)(2,1)S(1)} %bitcast.526, s32[1,8192]{1,0:T(1,128)S(1)} %bitcast.532), custom_call_target="tpu_custom_call" | custom-call | tf_op jit(solution)/shard_map/pallas_call | solution.py:667
  926.5 35.0 %shard_map.364 = f32[8,128]{1,0:T(8,128)} custom-call(f32[8,128]{1,0:T(8,128)} %broadcast_in_dim.304.in_ref), custom_call_target="tpu_custom_call" | custom-call | tf_op jit(solution)/shard_map/pallas_call | solution.py:512
  968.8 5.2 copy.76
  974.0 5.8 mul.2694
  989.8 12.2 %multiply_subtract_fusion.1 = (f32[24,50688]{1,0:T(8,128)}, f32[24,50688]{1,0:T(8,128)}, f32[24,50688]{1,0:T(8,128)}) fusion(f32[24,50688]{1,0:T(8,128)} %param.36, f32[3,8,396,128]{3,2,1,0:T(8,128)S(1)} %bitcast.544, f32[24,50688]{1,0:T(8,128)} %param.42, f32[24,50688]{1,0:T(8,128)} %param.48), kind=kLoop, calls=%fused_computation.15 | loop fusion | flops 18247680 | bytes 34062336 | tf_op jit(solution)/shard_map/sub | solution.py:1102
  1002.1 8.2 multiply_subtract_fusion
  (904 shorter events, 261.6 us)
Async XLA Ops:
  7.2 261.3 %all-gather.17.cloned.1.call-start = ((), (), s32[]{:S(2)}) async-start(), calls=%async_computation.9 | async-start | bytes 6082560 | tf_op jit(solution)/shard_map/all_gather | solution.py:714
  8.9 289.4 %all-gather.13.cloned.1.call-start = ((), (), s32[]{:S(2)}) async-start(), calls=%async_computation.6 | async-start | bytes 4866048 | tf_op jit(solution)/shard_map/all_gather | solution.py:714
  52.0 161.6 %all-to-all-start = ((bf16[24,32,256]{2,0,1:T(8,128)(2,1)}), bf16[24,32,256]{2,0,1:T(8,128)(2,1)S(1)}, u32[]{:S(2)}, u32[]{:S(2)}) async-start(bf16[24,32,256]{2,0,1:T(8,128)(2,1)} %broadcast_select_fusion), calls=%async_computation | async-start | bytes 786432 | tf_op jit(solution)/shard_map/all_to_all | solution.py:1177
  59.2 244.6 %all-gather.15.cloned.1.call-start = ((), (), s32[]{:S(2)}) async-start(), calls=%async_computation.7 | async-start | bytes 4866048 | tf_op jit(solution)/shard_map/all_gather | solution.py:714
  213.6 177.9 %all-to-all-start.1 = ((bf16[8,96,1584]{2,1,0:T(8,128)(2,1)}), bf16[8,96,1584]{2,1,0:T(8,128)(2,1)S(1)}, u32[]{:S(2)}, u32[]{:S(2)}) async-start(bf16[8,96,1584]{2,1,0:T(8,128)(2,1)} %bitcast.571), calls=%async_computation.1 | async-start | bytes 5111808 | tf_op jit(solution)/shard_map/all_to_all | solution.py:1190
  217.3 694.7 %reduce-scatter.5.cloned.1.call-start = ((), (), s32[]{:S(2)}) async-start(), calls=%async_computation.8 | async-start | bytes 4866048 | tf_op jit(solution)/shard_map/reduce_scatter | solution.py:742
  224.4 3.5 collective-permute-start
  247.9 3.4 collective-permute-start.1
  262.5 4.3 collective-permute-start.2
  290.7 5.1 collective-permute-start.3
  295.7 95.9 %copy-start.3 = (s32[1,1,32,256]{3,1,2,0:T(1,128)}, s32[1,1,32,256]{3,1,2,0:T(1,128)S(1)}, u32[]{:S(2)}) copy-start(s32[1,1,32,256]{3,1,2,0:T(1,128)S(1)} %copy.83) | copy-start | bytes 98308
  509.2 81.7 %slice-start.10 = ((s8[4718592]{0:T(1024)(128)(4,1)}), s8[4194304]{0:T(1024)(128)(4,1)S(1)}, s32[]{:S(2)}) async-start(s8[4718592]{0:T(1024)(128)(4,1)} %bitcast.549), calls=%async_computation.21 | async-start | bytes 8388608
  509.2 80.2 %copy-start.30 = (f32[256,768]{1,0:T(8,128)S(1)}, f32[256,768]{1,0:T(8,128)}, u32[]{:S(2)}) copy-start(f32[256,768]{1,0:T(8,128)} %copy-done.29) | copy-start | bytes 2359300
  509.2 81.4 %copy-start.77 = (f32[256,768]{1,0:T(8,128)S(1)}, f32[256,768]{1,0:T(8,128)}, u32[]{:S(2)}) copy-start(f32[256,768]{1,0:T(8,128)} %copy-done.76) | copy-start | bytes 2359300
  509.2 81.4 %copy-start.104 = (f32[256,768]{1,0:T(8,128)S(1)}, f32[256,768]{1,0:T(8,128)}, u32[]{:S(2)}) copy-start(f32[256,768]{1,0:T(8,128)} %get-tuple-element.822) | copy-start | bytes 2359300
  509.2 81.7 %slice-start.11 = ((s8[4718592]{0:T(1024)(128)(4,1)}), s8[524288]{0:T(1024)(128)(4,1)S(1)}, s32[]{:S(2)}) async-start(s8[4718592]{0:T(1024)(128)(4,1)} %bitcast.549), calls=%async_computation.22 | async-start | bytes 1048576
  607.8 5.7 collective-permute-start.4
  611.0 303.4 %reduce-scatter.7.cloned.1.call-start = ((), (), s32[]{:S(2)}) async-start(), calls=%async_computation.10 | async-start | bytes 10948608
  636.3 13.6 %collective-permute-start.5 = (f32[1,768]{1,0:T(1,128)}, f32[1,768]{1,0:T(1,128)}, u32[]{:S(2)}, u32[]{:S(2)}) collective-permute-start(f32[1,768]{1,0:T(1,128)} %split.57), channel_id=1, source_target_pairs={{1,0},{2,1},{3,2},{5,4},{6,5},{7,6},{9,8},{10,9},{11,10},{13,12},{... | collective-permute-start | bytes 9224 | tf_op jit(solution)/shard_map/ppermute | solution.py:780
  662.0 3.7 collective-permute-start.6
  688.8 3.1 collective-permute-start.7
  696.0 30.2 %all-to-all-start.2 = ((bf16[32,24,256]{2,1,0:T(8,128)(2,1)}), bf16[32,24,256]{2,1,0:T(8,128)(2,1)}, u32[]{:S(2)}, u32[]{:S(2)}) async-start(bf16[32,24,256]{2,1,0:T(8,128)(2,1)} %bitcast.587), calls=%async_computation.2 | async-start | bytes 786432 | tf_op jit(solution)/shard_map/all_to_all | solution.py:1258
  726.1 242.3 %all-to-all-start.3 = ((bf16[8,96,1584]{2,1,0:T(8,128)(2,1)}), bf16[8,96,1584]{2,1,0:T(8,128)(2,1)S(1)}, u32[]{:S(2)}, u32[]{:S(2)}) async-start(bf16[8,96,1584]{2,1,0:T(8,128)(2,1)} %bitcast.585), calls=%async_computation.4 | async-start | bytes 5111808 | tf_op jit(solution)/shard_map/all_to_all | solution.py:1221
  743.1 139.0 %copy-start.5 = (s32[8192]{0:T(1024)S(1)}, s32[8192]{0:T(1024)}, u32[]{:S(2)}) copy-start(s32[8192]{0:T(1024)} %param.29) | copy-start | bytes 98308
  (278 other events, 1819.2 us)
Sparse Core Ops, SparseCore 0:
  11.5 80.9 all-gather.16
  95.5 74.1 all-gather.12
  173.1 80.3 all-gather.14
  611.2 118.8 reduce-scatter.4
  737.0 174.0 reduce-scatter.6

commit v3 on v2

--- a/solution.py
+++ b/solution.py
@@ -1,3 +1,4 @@
+import functools
 import math
 
 import jax
@@ -49,7 +50,7 @@
     dims = [t.shape for t in tensors]
     hops = 3
     pieces_total = sum(len(p) for p in portions)
-    n_send = count + count + pieces_total * (1 + 2 * hops + 7)
+    n_send = count + count + pieces_total * (7 + 2 * hops + 7)
 
     def kernel(*refs):
         ins, outs = refs[:count], refs[count : 2 * count]
@@ -129,111 +130,124 @@
             return half[t].at[m0:m1, r0:r1, :]
 
         both = slice(0, 2)
-        a_way, b_way = (yway, xway), (xway, yway)
-        a_msgs = []
-        for p in range(2):
-            msg = message(p, (z, y, x), a_way[p], from_half)
-            start(msg)
-            a_msgs.append(msg)
+        a_way, b_way = (yway, xway) * 2, (xway, yway) * 2
+        ways = range(len(portions))
+
+        def one_of(p, zz):
+            return (zz, y, x)
+
+        def pair_of(p, zz):
+            return (zz, both, x) if p % 2 == 0 else (zz, y, both)
+
+        def other_of(p, zz):
+            return (zz, 1 - y, x) if p % 2 == 0 else (zz, y, 1 - x)
+
+        def far_of(p, zz):
+            return (zz, both, 1 - x) if p % 2 == 0 else (zz, 1 - y, both)
+
+        def late(p):
+            return p >= 2
+
+        def event_z(e):
+            return z if e == 0 else z - e if e <= hops else z + e - hops
+
+        def happens(e):
+            return z - e >= 0 if e <= hops else z + e - hops <= hops
+
+        def when(e, what):
+            if e == 0:
+                what()
+            else:
+                pl.when(happens(e))(what)
+
+        events = range(1 + 2 * hops)
+        a_msgs, z_msgs, b_msgs = {}, {}, {}
+        for p in ways:
+            held = one_of if late(p) else pair_of
+            for e in events if late(p) else (0,):
+                a_msgs[p, e] = message(p, one_of(p, event_z(e)), a_way[p], from_half if e == 0 else None)
+            for k in range(hops):
+                source = from_half if late(p) and k == 0 else None
+                z_msgs[p, 1 + k] = message(p, held(p, z - k), up, source)
+                z_msgs[p, 1 + hops + k] = message(p, held(p, z + k), down, source)
+            for e in events:
+                b_msgs[p, e] = message(p, pair_of(p, event_z(e)), b_way[p])
+
+        def start_z(p, e):
+            @pl.when(has_up if e <= hops else has_down)
+            def _():
+                start(z_msgs[p, e])
+
+        for p in ways:
+            if late(p):
+                start_z(p, 1)
+                start_z(p, 1 + hops)
+            start(a_msgs[p, 0])
         for own in stay:
             own.wait()
-        for p in range(2):
+        for p in ways:
             to_core(p, z, y, x, from_half)
-
-        def pair_of(p, zz):
-            return (zz, both, x) if p == 0 else (zz, y, both)
-
-        def other_of(p, zz):
-            return (zz, 1 - y, x) if p == 0 else (zz, y, 1 - x)
-
-        def far_of(p, zz):
-            return (zz, both, 1 - x) if p == 0 else (zz, 1 - y, both)
-
-        zmsg = [[[message(p, pair_of(p, z - k), up) for k in range(hops)],
-                 [message(p, pair_of(p, z + k), down) for k in range(hops)]] for p in range(2)]
-        b_msgs = []
-        for p in range(2):
-            own = message(p, pair_of(p, z), b_way[p])
-            ups = [message(p, pair_of(p, z - 1 - k), b_way[p]) for k in range(hops)]
-            downs = [message(p, pair_of(p, z + 1 + k), b_way[p]) for k in range(hops)]
-            b_msgs.append((own, ups, downs))
-
-        for p in range(2):
-            arrive(a_msgs[p])
-
-            @pl.when(has_up)
-            def _():
-                start(zmsg[p][0][0])
-
-            @pl.when(has_down)
-            def _():
-                start(zmsg[p][1][0])
-            start(b_msgs[p][0])
-            to_core(p, *other_of(p, z))
-
-        def far_own(p):
-            arrive(b_msgs[p][0])
-            to_core(p, *far_of(p, z))
-
-        def far_hop(p, k):
-            @pl.when(z - 1 - k >= 0)
-            def _():
-                arrive(b_msgs[p][1][k])
-                to_core(p, *far_of(p, z - 1 - k))
-
-            @pl.when(z + 1 + k <= hops)
-            def _():
-                arrive(b_msgs[p][2][k])
-                to_core(p, *far_of(p, z + 1 + k))
-
-        for k in range(hops):
-            for p in range(2):
-                @pl.when(z - 1 - k >= 0)
-                def _():
-                    arrive(zmsg[p][0][k])
-                    if k + 1 < hops:
-                        @pl.when(has_up)
-                        def _():
-                            start(zmsg[p][0][k + 1])
-                    start(b_msgs[p][1][k])
-                    to_core(p, *pair_of(p, z - 1 - k))
-
-                @pl.when(z + 1 + k <= hops)
-                def _():
-                    arrive(zmsg[p][1][k])
-                    if k + 1 < hops:
-                        @pl.when(has_down)
-                        def _():
-                            start(zmsg[p][1][k + 1])
-                    start(b_msgs[p][2][k])
-                    to_core(p, *pair_of(p, z + 1 + k))
-            for p in range(2):
-                if k == 0:
-                    far_own(p)
+        for p in ways:
+            if not late(p):
+                arrive(a_msgs[p, 0])
+                start_z(p, 1)
+                start_z(p, 1 + hops)
+                start(b_msgs[p, 0])
+                to_core(p, *other_of(p, z))
+
+        def z_event(p, e):
+            def turn():
+                arrive(z_msgs[p, e])
+                if e % hops:
+                    start_z(p, e + 1)
+                if late(p):
+                    start(a_msgs[p, e])
+                    to_core(p, *one_of(p, event_z(e)))
                 else:
-                    far_hop(p, k - 1)
-        for p in range(2):
-            far_hop(p, hops - 1)
-
-        for p in range(2):
-            sent(a_msgs[p])
-            sent(b_msgs[p][0])
-            for k in range(hops):
-                @pl.when((z - k >= 0) & has_up)
-                def _():
-                    sent(zmsg[p][0][k])
-
-                @pl.when((z + k <= hops) & has_down)
-                def _():
-                    sent(zmsg[p][1][k])
-
-                @pl.when(z - 1 - k >= 0)
-                def _():
-                    sent(b_msgs[p][1][k])
-
-                @pl.when(z + 1 + k <= hops)
-                def _():
-                    sent(b_msgs[p][2][k])
+                    start(b_msgs[p, e])
+                    to_core(p, *pair_of(p, event_z(e)))
+            when(e, turn)
+
+        def a_event(p, e):
+            def turn():
+                arrive(a_msgs[p, e])
+                start(b_msgs[p, e])
+                to_core(p, *other_of(p, event_z(e)))
+            when(e, turn)
+
+        def b_event(p, e):
+            def turn():
+                arrive(b_msgs[p, e])
+                to_core(p, *far_of(p, event_z(e)))
+            when(e, turn)
+
+        def at(hop):
+            return (0,) if hop == 0 else (hop, hops + hop)
+
+        for hop in range(hops + 3):
+            if 1 <= hop <= hops:
+                for p in ways:
+                    for e in at(hop):
+                        z_event(p, e)
+            if hop - 1 in range(hops + 1):
+                for p in ways:
+                    for e in at(hop - 1):
+                        if late(p):
+                            a_event(p, e)
+                        else:
+                            b_event(p, e)
+            if hop - 2 in range(hops + 1):
+                for p in ways:
+                    for e in at(hop - 2):
+                        if late(p):
+                            b_event(p, e)
+
+        for (p, e), msg in list(a_msgs.items()) + list(b_msgs.items()):
+            when(e, functools.partial(sent, msg))
+        for (p, e), msg in z_msgs.items():
+            k = (e - 1) % hops
+            going = (z - k >= 0) & has_up if e <= hops else (z + k <= hops) & has_down
+            pl.when(going)(functools.partial(sent, msg))
         for t in range(count):
             whole = pltpu.make_async_remote_copy(
                 src_ref=outs[t].at[:, :, :, :, :, cols(t, c)], dst_ref=outs[t].at[:, :, :, :, :, cols(t, 1 - c)],
@@ -260,9 +274,10 @@
     dims = [(t.shape[0], r, t.shape[2]) for t, r in zip(tensors, rows_own)]
     views = [t.reshape(m, hops + 1, 2, 2, 2 * r, w) for t, (m, r, w) in zip(tensors, dims)]
     pieces_total = sum(len(p) for p in portions)
-    n_send = pieces_total * (2 + 4 + 2 * hops + 1) + count
+    n_send = pieces_total * (2 + 4 + 2 * hops + 4) + count
     n_local = pieces_total * 2 + count
-    flat = [(p, piece) for p in range(2) for piece in portions[p]]
+    ways = range(len(portions))
+    flat = [(p, piece) for p in ways for piece in portions[p]]
     flat_dims = [(piece[2] - piece[1], piece[4] - piece[3], dims[piece[0]][2] // 2) for _, piece in flat]
 
     def kernel(*refs):
@@ -286,7 +301,7 @@
         has_up, has_down = z < hops, z > 0
         greet([core, xway, yway], [(has_up, up), (has_down, down)])
         sems = Sems(send, recv, local)
-        a_way, b_way = (yway, xway), (xway, yway)
+        a_way, b_way = (yway, xway) * 2, (xway, yway) * 2
 
         def cols(t, side):
             width = dims[t][2] // 2
@@ -298,9 +313,13 @@
                                                 device_id=device, device_id_type=ON_MESH)
 
         def place_of(p, zz, a, b):
-            return (zz, a, b) if p == 0 else (zz, b, a)
-
-        own_a, own_b = (y, x), (x, y)
+            return (zz, a, b) if p % 2 == 0 else (zz, b, a)
+
+        own_a, own_b = (y, x) * 2, (x, y) * 2
+
+        def late(p):
+            return p >= 2
+
 
         def add(dst, src, lead):
             def turn(i, _):
@@ -319,7 +338,7 @@
         everyz, both = slice(0, hops + 1), slice(0, 2)
         chunks = {}
         for far in (1, 0):
-            for p in range(2):
+            for p in ways:
                 b = own_b[p] if far == 0 else 1 - own_b[p]
                 made = []
                 for i, piece in index[p]:
@@ -341,7 +360,7 @@
 
         zorder = (3, 0, 2, 1)
         b_msgs = {}
-        for p in range(2):
+        for p in ways:
             core_add(1, p)
             for zz in zorder:
                 msgs = []
@@ -351,7 +370,7 @@
                 for msg in msgs:
                     msg.start()
                 b_msgs[p, zz] = msgs
-        for p in range(2):
+        for p in ways:
             core_add(0, p)
 
         def b_add(p, zz):
@@ -363,19 +382,41 @@
 
         def mine(p, i, piece, zz):
             t, m0, m1, r0, r1 = piece
-            return acc[t].at[(slice(m0, m1),) + place_of(p, zz, both, own_b[p]) + (slice(r0, r1),)]
+            a = own_a[p] if late(p) else both
+            return acc[t].at[(slice(m0, m1),) + place_of(p, zz, a, own_b[p]) + (slice(r0, r1),)]
+
+        def landing(p, land, i, zz):
+            return land[i].at[:, zz, 0] if late(p) else land[i].at[:, zz]
+
+        a_msgs = {}
+
+        def a_start(p, zz):
+            msgs = []
+            for i, (t, m0, m1, r0, r1) in index[p]:
+                src = acc[t].at[(slice(m0, m1),) + place_of(p, zz, 1 - own_a[p], own_b[p]) + (slice(r0, r1),)]
+                msgs.append(remote(src, a_all[i].at[:, zz if late(p) else 0], a_way[p]))
+            for msg in msgs:
+                msg.start()
+            a_msgs[p, zz if late(p) else 0] = msgs
+
+        def a_add(p, zz):
+            for msg in a_msgs[p, zz]:
+                msg.wait_recv()
+            for i, piece in index[p]:
+                add(mine(p, i, piece, zz), a_all[i].at[:, zz], (piece[2] - piece[1],))
 
         up_msgs, down_msgs = {}, {}
-        for p in range(2):
+        for p in ways:
             for zz in range(hops + 1):
-                up_msgs[p, zz] = [remote(mine(p, i, piece, zz), u_all[i].at[:, zz], up) for i, piece in index[p]] if zz > 0 else None
-                down_msgs[p, zz] = [remote(mine(p, i, piece, zz), d_all[i].at[:, zz], down) for i, piece in index[p]] if zz < hops else None
+                up_msgs[p, zz] = [remote(mine(p, i, piece, zz), landing(p, u_all, i, zz), up) for i, piece in index[p]] if zz > 0 else None
+                down_msgs[p, zz] = [remote(mine(p, i, piece, zz), landing(p, d_all, i, zz), down) for i, piece in index[p]] if zz < hops else None
 
         def z_add(p, zz, msgs, land):
             for msg in msgs[p, zz]:
                 msg.wait_recv()
             for i, piece in index[p]:
-                add(mine(p, i, piece, zz), land[i].at[:, zz], (piece[2] - piece[1], 2))
+                lead = (piece[2] - piece[1],) if late(p) else (piece[2] - piece[1], 2)
+                add(mine(p, i, piece, zz), landing(p, land, i, zz), lead)
 
         def up_send(p, zz):
             @pl.when(z < zz)
@@ -395,21 +436,42 @@
                 for msg in down_msgs[p, zz]:
                     msg.start()
 
-        for p in range(2):
-            b_add(p, 3)
+        early_ways, late_ways = [p for p in ways if not late(p)], [p for p in ways if late(p)]
+        for zz in zorder[:2]:
+            for p in ways:
+                b_add(p, zz)
+                if late(p):
+                    a_start(p, zz)
+                elif zz == 3:
+                    up_send(p, 3)
+                else:
+                    down_send(p, 0)
+        for zz in zorder[2:]:
+            for p in ways:
+                b_add(p, zz)
+                if late(p):
+                    a_start(p, zz)
+                elif zz == 2:
+                    up_send(p, 2)
+                else:
+                    down_send(p, 1)
+        for p in late_ways:
+            a_add(p, 3)
             up_send(p, 3)
-            b_add(p, 0)
+            a_add(p, 0)
             down_send(p, 0)
-        for p in range(2):
-            b_add(p, 2)
-            up_send(p, 2)
-            b_add(p, 1)
-            down_send(p, 1)
-        for p in range(2):
+        for p in early_ways:
             up_send(p, 1)
             down_send(p, 2)
-        a_msgs = {}
-        for p in range(2):
+        for p in late_ways:
+            a_add(p, 2)
+            up_send(p, 2)
+            a_add(p, 1)
+            down_send(p, 1)
+        for p in late_ways:
+            up_send(p, 1)
+            down_send(p, 2)
+        for p in ways:
             for zz in range(hops + 1):
                 @pl.when(z == zz)
                 def _():
@@ -417,20 +479,19 @@
                         z_add(p, zz, up_msgs, u_all)
                     if zz < hops:
                         z_add(p, zz, down_msgs, d_all)
-            msgs = []
+            if not late(p):
+                a_start(p, z)
+        for p in late_ways:
             for i, (t, m0, m1, r0, r1) in index[p]:
-                src = acc[t].at[(slice(m0, m1),) + place_of(p, z, 1 - own_a[p], own_b[p]) + (slice(r0, r1),)]
-                msgs.append(remote(src, a_all[i], a_way[p]))
-            for msg in msgs:
-                msg.start()
-            a_msgs[p] = msgs
-        for p in range(2):
-            for msg in a_msgs[p]:
+                for m in range(m0, m1):
+                    fin[t][m, r0:r1, :] = acc[t][(m,) + place_of(p, z, own_a[p], own_b[p]) + (slice(r0, r1),)].astype(jnp.float32)
+        for p in early_ways:
+            for msg in a_msgs[p, 0]:
                 msg.wait_recv()
             for i, (t, m0, m1, r0, r1) in index[p]:
                 for m in range(m0, m1):
                     part = acc[t][(m,) + place_of(p, z, own_a[p], own_b[p]) + (slice(r0, r1),)]
-                    fin[t][m, r0:r1, :] = part.astype(jnp.float32) + a_all[i][m - m0].astype(jnp.float32)
+                    fin[t][m, r0:r1, :] = part.astype(jnp.float32) + a_all[i][m - m0, 0].astype(jnp.float32)
         last = []
         for t in range(count):
             r = dims[t][1]
@@ -445,7 +506,7 @@
         for msgs in list(b_msgs.values()) + list(a_msgs.values()):
             for msg in msgs:
                 msg.wait_send()
-        for p in range(2):
+        for p in ways:
             for zz in range(hops + 1):
                 if zz > 0:
                     @pl.when(z < zz)
@@ -471,7 +532,7 @@
         + [pltpu.VMEM((m, hops + 1, 2, 2, 2 * r, w // 2), bf) for m, r, w in dims]
         + [pltpu.VMEM((m, 2 * r, w // 2), jnp.float32) for m, r, w in dims]
         + [pltpu.VMEM((m, hops + 1, 2, r, w), bf) for m, r, w in flat_dims] * 3
-        + [pltpu.VMEM((m, r, w), bf) for m, r, w in flat_dims]
+        + [pltpu.VMEM((m, hops + 1, r, w), bf) for m, r, w in flat_dims]
         + [pltpu.SemaphoreType.DMA((n_send,)), pltpu.SemaphoreType.DMA((n_send,)), pltpu.SemaphoreType.DMA((n_local,))],
         compiler_params=pltpu.CompilerParams(collective_id=collective_id, has_side_effects=True, vmem_limit_bytes=50 << 20),
     )(*views)
@@ -630,6 +691,267 @@
     )(lifted, rows_all, head_cols, local_ids[None], factors)
 
 
+def head_backward_scattered(lifted, rows_all, head_cols, local_ids, factors, collective_id):
+    tokens, width = lifted.shape
+    features = rows_all.shape[1]
+    hops, block = 3, tokens // 16
+    rows, wing = block // 2, features // 2
+    zorder = (3, 0, 2, 1)
+    cuts = [slice(k, min(k + 512, width)) for k in range(0, width - 256, 512)]
+    cuts[-1] = slice(cuts[-1].start, width)
+    parts = (slice(0, rows), slice(rows, block))
+
+    def kernel(p_hbm, rows_hbm, head_ref, ids_ref, factor_ref, out, d_head_ref, squares_ref,
+               p_buf, r_buf, d_logits, total, acc, give, crecv, b_all, u_all, d_all, a_all, fin,
+               in_sem, core_send, core_recv, send, recv, local):
+        dp, seq, z, y, x, c = place()
+        core = (dp, seq + 1 - 2 * c)
+        xway = (dp, seq + 2 - 4 * x)
+        yway = (dp + 1 - 2 * y, seq)
+        up, down = (dp + 2, seq), (dp - 2, seq)
+        has_up, has_down = z < hops, z > 0
+        groups = ((1 - y, 1 - x), (y, 1 - x), (1 - y, x), (y, x))
+
+        def fetch(slot, zz, yy, xx):
+            return (
+                pltpu.make_async_copy(p_hbm.at[zz, yy, xx], p_buf.at[slot], in_sem.at[slot, 0]),
+                pltpu.make_async_copy(rows_hbm.at[zz, yy, xx], r_buf.at[slot], in_sem.at[slot, 1]),
+            )
+
+        for copy in fetch(0, zorder[0], *groups[0]):
+            copy.start()
+        greet([core, xway, yway], [(has_up, up), (has_down, down)])
+        sems = Sems(send, recv, local)
+
+        def remote(src, dst, device):
+            ss, rs = sems.pair()
+            return pltpu.make_async_remote_copy(src_ref=src, dst_ref=dst, send_sem=ss, recv_sem=rs,
+                                                device_id=device, device_id_type=ON_MESH)
+
+        def to_core(g, k, zz):
+            yy, xx = groups[g]
+            return pltpu.make_async_remote_copy(
+                src_ref=give.at[k], dst_ref=crecv.at[zz, yy, xx], send_sem=core_send.at[g * 4 + k],
+                recv_sem=core_recv.at[g * 4 + k], device_id=core, device_id_type=ON_MESH)
+
+        total[...] = jnp.zeros_like(total)
+        column = lax.broadcasted_iota(jnp.int32, (rows, width), 1)
+
+        def zz_of(k):
+            return jnp.where(k == 0, 3, jnp.where(k == 1, 0, jnp.where(k == 2, 2, 1)))
+
+        def compute(g, k):
+            yy, xx = groups[g]
+            zz = zz_of(k)
+            slot = lax.rem(k, 2)
+            for copy in fetch(slot, zz, yy, xx):
+                copy.wait()
+            if g < 3:
+                more = k < 4
+            else:
+                more = k < 3
+            nyy, nxx = groups[min(g + 1, 3)]
+            last = k == 3
+
+            @pl.when(more)
+            def _():
+                for copy in fetch(1 - slot, jnp.where(last, 3, zz_of(k + 1)), jnp.where(last, nyy, yy), jnp.where(last, nxx, xx)):
+                    copy.start()
+            first = pl.multiple_of(((zz * 2 + yy) * 2 + xx) * block, block)
+            here = pl.ds(first, block)
+            ids = jnp.transpose(jnp.broadcast_to(ids_ref[:, here], (128, block)))[:, :1]
+            scales = jnp.transpose(jnp.concatenate([factor_ref[:, here]] * 16, axis=0))
+            if g > 0:
+                to_core(g - 1, k, zz).wait_send()
+            for part in parts:
+                d_logits[part, :] = jnp.where(
+                    column == ids[part], scales[part, 1:2], p_buf[slot, part, :].astype(jnp.float32) * scales[part, :1]
+                ).astype(jnp.bfloat16)
+                d_rows = lax.dot_general(
+                    d_logits[part, :], head_ref[...], (((1,), (1,)), ((), ())), preferred_element_type=jnp.float32)
+                left, right = d_rows[:, :wing], d_rows[:, wing:]
+                acc[zz, yy, xx, part, :] = jnp.where(c == 0, left, right).astype(jnp.bfloat16)
+                give[k, part, :] = jnp.where(c == 0, right, left).astype(jnp.bfloat16)
+            to_core(g, k, zz).start()
+            for cut in cuts:
+                total[:, cut] += lax.dot_general(
+                    r_buf[slot], d_logits[:, cut], (((0,), (0,)), ((), ())), preferred_element_type=jnp.float32)
+
+        def add(dst, src):
+            dst[...] = (dst[...].astype(jnp.float32) + src[...].astype(jnp.float32)).astype(dst.dtype)
+
+        own_b = (x, y)
+        own_a = (y, x)
+        b_way, a_way = (xway, yway), (yway, xway)
+
+        def spot(p, zz, a, b):
+            yy, xx = (a, b) if p == 0 else (b, a)
+            return acc.at[zz, yy, xx, parts[p]]
+
+        b_msgs, z_up, z_down = {}, {}, {}
+        for p in range(2):
+            for zz in range(hops + 1):
+                for near in range(2):
+                    a = own_a[p] if near else 1 - own_a[p]
+                    b_msgs[p, zz, near] = remote(spot(p, zz, a, 1 - own_b[p]), b_all.at[p, zz, a], b_way[p])
+                    mine = spot(p, zz, a, own_b[p])
+                    if zz > 0:
+                        z_up[p, zz, near] = remote(mine, u_all.at[p, zz - 1, a], up)
+                    if zz < hops:
+                        z_down[p, zz, near] = remote(mine, d_all.at[p, zz, a], down)
+
+        def core_add(g):
+            yy, xx = groups[g]
+            for k, zz in enumerate(zorder):
+                to_core(g, k, zz).wait_recv()
+                for part in parts:
+                    add(acc.at[zz, yy, xx, part], crecv.at[zz, yy, xx, part])
+                for p, near in (((0, 0), (1, 0)), ((0, 1),), ((1, 1),), ())[g]:
+                    b_msgs[p, zz, near].start()
+
+        def b_add(p, near):
+            a = own_a[p] if near else 1 - own_a[p]
+            for zz in zorder:
+                b_msgs[p, zz, near].wait_recv()
+                add(spot(p, zz, a, own_b[p]), b_all.at[p, zz, a])
+
+        def z_take(p, zz, near, msgs, land):
+            a = own_a[p] if near else 1 - own_a[p]
+            msgs[p, zz, near].wait_recv()
+            add(spot(p, zz, a, own_b[p]), land.at[p, zz - 1 if msgs is z_up else zz, a])
+
+        def z_hop(p, near, hop):
+            @pl.when(z == hop)
+            def _():
+                for zz in range(hops, hop, -1):
+                    if hop > 0:
+                        z_take(p, zz, near, z_up, u_all)
+                    z_up[p, zz, near].start()
+
+            @pl.when(z == hops - hop)
+            def _():
+                for zz in range(0, hops - hop):
+                    if hop > 0:
+                        z_take(p, zz, near, z_down, d_all)
+                    z_down[p, zz, near].start()
+
+        def run(g):
+            def turn(k, _):
+                compute(g, k)
+                return 0
+            lax.fori_loop(0, 4, turn, 0)
+
+        run(0)
+        core_add(0)
+        run(1)
+        core_add(1)
+        b_add(1, 0)
+        z_hop(1, 0, 0)
+        run(2)
+        core_add(2)
+        b_add(0, 0)
+        z_hop(0, 0, 0)
+        z_hop(1, 0, 1)
+        run(3)
+        core_add(3)
+        for p in range(2):
+            b_add(p, 1)
+            z_hop(p, 1, 0)
+        z_hop(0, 0, 1)
+        z_hop(1, 0, 2)
+        for p in range(2):
+            z_hop(p, 1, 1)
+        z_hop(0, 0, 2)
+        for p in range(2):
+            z_hop(p, 1, 2)
+        low = total[...].astype(jnp.bfloat16)
+        d_head_ref[...] = low
+        wide = low.astype(jnp.float32)
+        squares_ref[...] = jnp.sum((wide * wide).reshape(features // 8, 8, width), axis=0)
+        a_msgs = []
+        for p in range(2):
+            for zz in range(hops + 1):
+                @pl.when(z == zz)
+                def _():
+                    for near in range(2):
+                        if zz > 0:
+                            z_take(p, zz, near, z_up, u_all)
+                        if zz < hops:
+                            z_take(p, zz, near, z_down, d_all)
+            msg = remote(spot(p, z, 1 - own_a[p], own_b[p]), a_all.at[p], a_way[p])
+            msg.start()
+            a_msgs.append(msg)
+        for p in range(2):
+            a_msgs[p].wait_recv()
+            fin[parts[p], :] = spot(p, z, own_a[p], own_b[p])[...].astype(jnp.float32) + a_all[p].astype(jnp.float32)
+        side = pl.ds(pl.multiple_of(c * wing, 128), wing)
+        other = remote(fin.at[pl.ds(pl.multiple_of((1 - c) * rows, 8), rows), :], out.at[:, side], core)
+        keep = pltpu.make_async_copy(fin.at[pl.ds(pl.multiple_of(c * rows, 8), rows), :], out.at[:, side], sems.own())
+        other.start()
+        keep.start()
+        for k in range(4):
+            to_core(3, k, zorder[k]).wait_send()
+        for msg in list(b_msgs.values()) + a_msgs:
+            msg.wait_send()
+        for zz in range(hops + 1):
+            @pl.when(z < zz)
+            def _():
+                for p in range(2):
+                    for near in range(2):
+                        if zz > 0:
+                            z_up[p, zz, near].wait_send()
+
+            @pl.when(z > zz)
+            def _():
+                for p in range(2):
+                    for near in range(2):
+                        if zz < hops:
+                            z_down[p, zz, near].wait_send()
+        keep.wait()
+        other.wait()
+
+    bf = jnp.bfloat16
+    n_send = 2 * 8 + 2 * 2 * 2 * hops + 2 + 1
+    whole = pl.BlockSpec(memory_space=pltpu.VMEM)
+    return pl.pallas_call(
+        kernel,
+        out_shape=[
+            jax.ShapeDtypeStruct((rows, features), jnp.float32),
+            jax.ShapeDtypeStruct((features, width), bf),
+            jax.ShapeDtypeStruct((8, width), jnp.float32),
+        ],
+        in_specs=[pl.BlockSpec(memory_space=pl.ANY)] * 2 + [whole] * 3,
+        out_specs=[pl.BlockSpec(memory_space=pl.ANY), whole, whole],
+        scratch_shapes=[
+            pltpu.VMEM((2, block, width), bf),
+            pltpu.VMEM((2, block, features), bf),
+            pltpu.VMEM((block, width), bf),
+            pltpu.VMEM((features, width), jnp.float32),
+            pltpu.VMEM((hops + 1, 2, 2, block, wing), bf),
+            pltpu.VMEM((4, block, wing), bf),
+            pltpu.VMEM((hops + 1, 2, 2, block, wing), bf),
+            pltpu.VMEM((2, hops + 1, 2, rows, wing), bf),
+            pltpu.VMEM((2, hops, 2, rows, wing), bf),
+            pltpu.VMEM((2, hops, 2, rows, wing), bf),
+            pltpu.VMEM((2, rows, wing), bf),
+            pltpu.VMEM((block, wing), jnp.float32),
+            pltpu.SemaphoreType.DMA((2, 2)),
+            pltpu.SemaphoreType.DMA((16,)),
+            pltpu.SemaphoreType.DMA((16,)),
+            pltpu.SemaphoreType.DMA((n_send,)),
+            pltpu.SemaphoreType.DMA((n_send,)),
+            pltpu.SemaphoreType.DMA((1,)),
+        ],
+        compiler_params=pltpu.CompilerParams(collective_id=collective_id, has_side_effects=True, vmem_limit_bytes=60 << 20),
+    )(
+        lifted.reshape(hops + 1, 2, 2, block, width),
+        rows_all.reshape(hops + 1, 2, 2, block, features),
+        head_cols,
+        local_ids[None],
+        factors,
+    )
+
+
 def embed_gradient(columns, token_ids, vocab, block):
     features, tokens = columns.shape
     lanes = 128
@@ -744,17 +1066,21 @@
 
 
 def weight_portions(square, expand, shrink, vectors, marks=0):
-    first = [(1, 0, 1, 0, 2 * expand), (0, 0, 3, 0, 2 * square)]
-    second = [(2, 0, 1, 0, 2 * shrink), (0, 3, 5, 0, 2 * square)]
+    split = 2 * square * 2 // 3
+    first = [(1, 0, 1, 0, 2 * expand)]
+    second = [(2, 0, 1, 0, 2 * shrink)]
+    third = [(0, 0, 2, 0, 2 * square), (0, 2, 3, 0, split)]
+    fourth = [(0, 3, 5, 0, 2 * square), (0, 2, 3, split, 2 * square)]
     if vectors:
-        second.append((3, 0, 1, 0, 2 * vectors))
+        fourth.append((3, 0, 1, 0, 2 * vectors))
     if marks:
-        first.append((4, 0, 1, 0, 2 * marks))
-    return [first, second]
+        fourth.append((4, 0, 1, 0, 2 * marks))
+    return [first, second, third, fourth]
 
 
 def row_portions(rows):
-    return [[(0, 0, 1, 0, rows)], [(0, 0, 1, rows, 2 * rows)]]
+    ends = [0, rows * 5 // 8, rows * 10 // 8, rows * 13 // 8, 2 * rows]
+    return [[(0, 0, 1, first, last)] for first, last in zip(ends, ends[1:])]
 
 
 def as_rows(vectors):
@@ -1211,12 +1537,15 @@
         ),
         ((0, 6), (0, 0)),
     )
-    d_rows, grad_head, head_squares = head_backward(
-        lifted, rows_all, head_cols, local_ids, factors, tile, tile // 2
-    )
-    d_normed = scatter_rows(
-        [d_rows[None]], row_portions(own_rows), 11
-    )[0][0]
+    if on_box():
+        d_normed, grad_head, head_squares = head_backward_scattered(
+            lifted, rows_all, head_cols, local_ids, factors, 11
+        )
+    else:
+        d_rows, grad_head, head_squares = head_backward(
+            lifted, rows_all, head_cols, local_ids, factors, tile, tile // 2
+        )
+        d_normed = scatter_plain([d_rows[None]])[0][0]
     g_head = (
         lax.all_to_all(
             grad_head.reshape(dp_count, features, vocab_part),

time: 1030 us -> 943 us (0.916)
  Pallas kernels: 595 us -> 517 us
  starting transfers between devices: 47.7 us -> 36.6 us
    pallas_call x2 -> x1, Pallas kernels: 217 us -> 135 us  [scatter_blocks(): pl.pallas_call(kernel, out_shape=[jax.ShapeDtypeStruct((m, r, w), jnp.flo...]
    pallas_call x1, Pallas kernels: 61.1 us -> 112 us  [head_backward_scattered(): pl.pallas_call(kernel, out_shape=[jax.ShapeDtypeStruct((rows, features),...]
    pallas_call x2, Pallas kernels: 200 us -> 169 us  [gather_blocks(): pl.pallas_call(kernel, out_shape=[jax.ShapeDtypeStruct((m, hops + 1, 2, 2...]
    pallas_call x2, Pallas kernels: 51.9 us -> 35.9 us  [exchange_everywhere(): pl.pallas_call(kernel, out_shape=jax.ShapeDtypeStruct(value.shape, jnp.fl...]
    all_to_all x1, starting transfers between devices: 15.4 us -> 3.97 us  [per_device(): lax.all_to_all(d_embedded.T.astype(jnp.bfloat16), ('dp', 'seq'), split_ax...]
    unnamed x584 -> x572, local copies, waits for them, and re-layouts: 33.6 us -> 32.9 us
  transfers between devices with their start and end apart: 17 -> 17, of which waited for: 5 -> 5; matrix products, arithmetic and copies ran while one was open for 23% -> 25% of each run, Pallas kernels for 39% -> 38%
where the time goes in v3:
time: 943 us; the launch traced here: 932 us
  Pallas kernels  517 us (55%)
  local copies, waits for them, and re-layouts  119 us (13%)
  other arithmetic  108 us (11%)
  matrix products  89.2 us (9%)
  starting transfers between devices  36.6 us (4%)
  between operations  26.9 us (3%)
  blocking collectives  26.7 us (3%)
    pallas_call x2, Pallas kernels, gather_blocks(): pl.pallas_call(kernel, out_shape=[jax.ShapeDtypeStruct((m, hops + 1, 2, 2...  169 us
    pallas_call x1, Pallas kernels, scatter_blocks(): pl.pallas_call(kernel, out_shape=[jax.ShapeDtypeStruct((m, r, w), jnp.flo...  135 us
    pallas_call x1, Pallas kernels, head_backward_scattered(): pl.pallas_call(kernel, out_shape=[jax.ShapeDtypeStruct((rows, features),...  112 us
    dot_general x14, matrix products, matmul(): return jnp.dot(left, right, preferred_element_type=jnp.float32)  39.1 us
    pallas_call x1, Pallas kernels, head_forward(): pl.pallas_call(kernel, grid=(tokens // tile,), out_shape=[jax.ShapeDtypeS...  36.7 us
    pallas_call x2, Pallas kernels, exchange_everywhere(): pl.pallas_call(kernel, out_shape=jax.ShapeDtypeStruct(value.shape, jnp.fl...  35.9 us
    unnamed x572, local copies, waits for them, and re-layouts  32.9 us
    gather x2, local copies, waits for them, and re-layouts, per_device(): columns = jnp.take(embed_table.astype(jnp.bfloat16), token_ids, axis=1)  29.2 us
  transfers between devices with their start and end apart: 17, of which 5 were waited for; matrix products, arithmetic and copies ran while one was open for 25% of the time, Pallas kernels for 38%

profile of v3, /device:TPU:0, one launch (start us, length us, event | category | flops | bytes accessed | tf_op | source)
XLA Modules:
  0.0 931.9 jit_solution(12144526114052266900)
XLA Ops:
  13.3 8.6 copy.68
  21.9 28.4 %gather_fusion = bf16[8192,24]{1,0:T(8,128)(2,1)S(1)} fusion(bf16[24,50688]{0,1:T(8,128)(2,1)} %copy.68, s32[8192]{0:T(1024)S(1)} %fusion.96), kind=kCustom, calls=%fused_computation | custom fusion | bytes 819200 | tf_op jit(solution)/shard_map/jit(_take)/gather | solution.py:1502
  52.0 7.2 all-to-all-start
  64.6 105.5 %shard_map.356 = (bf16[5,4,2,2,48,768]{5,4,3,2,1,0:T(8,128)(2,1)}, bf16[1,4,2,2,48,3072]{5,4,3,2,1,0:T(8,128)(2,1)S(1)}, bf16[1,4,2,2,192,768]{5,4,3,2,1,0:T(8,1...) custom-call(f32[5,24,768]{2,1,0:T(8,128)S(1)} %slice_bitcast_fusion.16.refs_0_, ...), custom_call_target="tpu_custom_call" | custom-call | tf_op jit(solution)/shard_map/pallas_call | solution.py:258
  187.9 5.3 fusion.164
  214.7 5.5 all-gather.5
  252.1 8.2 all-gather.6
  277.6 5.5 fusion.13
  292.0 63.7 %shard_map.357 = bf16[1,4,2,2,512,768]{5,4,3,2,1,0:T(8,128)(2,1)S(1)} custom-call(f32[1,256,768]{2,1,0:T(8,128)S(1)} %add_bitcast_fusion.refs_0_), custom_call_target="tpu_custom_call" | custom-call | tf_op jit(solution)/shard_map/pallas_call | solution.py:258
  360.2 36.7 %shard_map.358 = (bf16[8192,1584]{1,0:T(8,128)(2,1)}, f32[8,8192]{1,0:T(8,128)S(1)}) custom-call(bf16[8192,768]{1,0:T(8,128)(2,1)} %bitcast.509, bf16[768,1584]{1,0:T(8,128)(2,1)S(1)} %bitcast.511, s32[1,8192]{1,0:T(1,128)S(1)} %bitcast.521), custom_call_target="tpu_custom_call" | custom-call | tf_op jit(solution)/shard_map/pallas_call | solution.py:611
  397.6 16.7 %shard_map.359 = f32[64,128]{1,0:T(8,128)} custom-call(f32[64,128]{1,0:T(8,128)} %bitcast.581), custom_call_target="tpu_custom_call" | custom-call | tf_op jit(solution)/shard_map/pallas_call | solution.py:573
  416.5 111.8 %shard_map.360 = (f32[256,768]{1,0:T(8,128)}, bf16[768,1584]{1,0:T(8,128)(2,1)}, f32[8,1584]{1,0:T(8,128)}) custom-call(bf16[4,2,2,512,1584]{4,3,2,1,0:T(8,128)(2,1)} %bitcast.532, bf16[4,2,2,512,768]{4,3,2,1,0:T(8,128)(2,1)} %bitcast.510, bf16[768,1584]{1,0:T(8,128)(2,1)} %bitcast.512, s32[1,8192]{1,0:T(1,128)} %bitcast.522, ...), custom_call_target="tpu_custom_call" | custom-call | tf_op jit(solution)/shard_map/pallas_call | solution.py:916
  567.1 6.2 all-gather.7
  617.3 6.8 all-gather.8
  641.5 5.1 convolution_convert_fusion.3
  650.4 6.5 all-to-all-done.2
  674.0 134.9 %shard_map.362 = (f32[5,24,768]{2,1,0:T(8,128)S(1)}, f32[1,24,3072]{2,1,0:T(8,128)S(1)}, f32[1,96,768]{2,1,0:T(8,128)S(1)}, f32[1,24,256]{2,1,0:T(8,128)S(1)}) custom-call(bf16[5,4,2,2,48,768]{5,4,3,2,1,0:T(8,128)(2,1)} %constant_dynamic-update-slice_fusion.refs_0_, bf16[1,4,2,2,48,3072]{5,4,3,2,1,0:T(8,128)(2,1)} %bitcast.533, ...), custom_call_target="tpu_custom_call" | custom-call | tf_op jit(solution)/shard_map/pallas_call | solution.py:526
  810.6 28.1 %shard_map.361 = (f32[24,400,128]{2,1,0:T(8,128)}, f32[8,128]{1,0:T(8,128)S(1)}) custom-call(bf16[24,8192]{1,0:T(8,128)(2,1)S(1)} %bitcast.517, s32[1,8192]{1,0:T(1,128)S(1)} %bitcast.523), custom_call_target="tpu_custom_call" | custom-call | tf_op jit(solution)/shard_map/pallas_call | solution.py:989
  855.0 19.2 %shard_map.363 = f32[8,128]{1,0:T(8,128)} custom-call(f32[8,128]{1,0:T(8,128)} %broadcast_in_dim.304.in_ref), custom_call_target="tpu_custom_call" | custom-call | tf_op jit(solution)/shard_map/pallas_call | solution.py:573
  876.2 5.0 slice_multiply_fusion
  881.5 5.2 copy.76
  886.7 5.8 mul.2694
  902.5 12.1 %multiply_subtract_fusion.1 = (f32[24,50688]{1,0:T(8,128)}, f32[24,50688]{1,0:T(8,128)}, f32[24,50688]{1,0:T(8,128)}) fusion(f32[24,50688]{1,0:T(8,128)} %param.36, f32[3,8,396,128]{3,2,1,0:T(8,128)S(1)} %bitcast.536, f32[24,50688]{1,0:T(8,128)} %param.42, f32[24,50688]{1,0:T(8,128)} %param.48), kind=kLoop, calls=%fused_computation.15 | loop fusion | flops 18247680 | bytes 34062336 | tf_op jit(solution)/shard_map/sub | solution.py:1428
  914.7 8.2 multiply_subtract_fusion
  (889 shorter events, 258.7 us)
Async XLA Ops:
  7.2 240.0 %all-gather.17.cloned.1.call-start = ((), (), s32[]{:S(2)}) async-start(), calls=%async_computation.9 | async-start | bytes 6082560 | tf_op jit(solution)/shard_map/all_gather | solution.py:1036
  8.9 268.6 %all-gather.13.cloned.1.call-start = ((), (), s32[]{:S(2)}) async-start(), calls=%async_computation.6 | async-start | bytes 4866048 | tf_op jit(solution)/shard_map/all_gather | solution.py:1036
  21.9 40.1 %copy-start.86 = (f32[2,24,3072]{2,1,0:T(8,128)S(1)}, f32[2,24,3072]{2,1,0:T(8,128)}, u32[]{:S(2)}) copy-start(f32[2,24,3072]{2,1,0:T(8,128)} %param.33) | copy-start | bytes 1769476
  21.9 41.1 %copy-start.139 = (f32[26,24]{0,1:T(8,128)S(1)}, f32[26,24]{0,1:T(8,128)}, u32[]{:S(2)}) copy-start(f32[26,24]{0,1:T(8,128)} %param.35) | copy-start | bytes 7492
  52.0 141.2 %all-to-all-start = ((bf16[24,32,256]{2,0,1:T(8,128)(2,1)}), bf16[24,32,256]{2,0,1:T(8,128)(2,1)S(1)}, u32[]{:S(2)}, u32[]{:S(2)}) async-start(bf16[24,32,256]{2,0,1:T(8,128)(2,1)} %broadcast_select_fusion), calls=%async_computation | async-start | bytes 786432 | tf_op jit(solution)/shard_map/all_to_all | solution.py:1503
  59.2 223.9 %all-gather.15.cloned.1.call-start = ((), (), s32[]{:S(2)}) async-start(), calls=%async_computation.7 | async-start | bytes 4866048 | tf_op jit(solution)/shard_map/all_gather | solution.py:1036
  193.2 167.0 %all-to-all-start.1 = ((bf16[8,96,1584]{2,1,0:T(8,128)(2,1)}), bf16[8,96,1584]{2,1,0:T(8,128)(2,1)S(1)}, u32[]{:S(2)}, u32[]{:S(2)}) async-start(bf16[8,96,1584]{2,1,0:T(8,128)(2,1)} %bitcast.560), calls=%async_computation.1 | async-start | bytes 5111808 | tf_op jit(solution)/shard_map/all_to_all | solution.py:1516
  196.8 643.7 %reduce-scatter.5.cloned.1.call-start = ((), (), s32[]{:S(2)}) async-start(), calls=%async_computation.8 | async-start | bytes 4866048 | tf_op jit(solution)/shard_map/reduce_scatter | solution.py:1064
  203.9 3.7 collective-permute-start
  226.7 3.4 collective-permute-start.1
  241.2 4.2 collective-permute-start.2
  269.9 5.2 collective-permute-start.3
  275.0 85.2 %copy-start.3 = (s32[1,1,32,256]{3,1,2,0:T(1,128)}, s32[1,1,32,256]{3,1,2,0:T(1,128)S(1)}, u32[]{:S(2)}) copy-start(s32[1,1,32,256]{3,1,2,0:T(1,128)S(1)} %copy.83) | copy-start | bytes 98308
  416.5 111.8 %copy-start.30 = (f32[256,768]{1,0:T(8,128)S(1)}, f32[256,768]{1,0:T(8,128)}, u32[]{:S(2)}) copy-start(f32[256,768]{1,0:T(8,128)} %copy-done.29) | copy-start | bytes 2359300
  416.5 115.5 %copy-start.77 = (f32[256,768]{1,0:T(8,128)S(1)}, f32[256,768]{1,0:T(8,128)}, u32[]{:S(2)}) copy-start(f32[256,768]{1,0:T(8,128)} %copy-done.76) | copy-start | bytes 2359300
  416.5 115.5 %copy-start.104 = (f32[256,768]{1,0:T(8,128)S(1)}, f32[256,768]{1,0:T(8,128)}, u32[]{:S(2)}) copy-start(f32[256,768]{1,0:T(8,128)} %get-tuple-element.823) | copy-start | bytes 2359300
  549.5 6.3 collective-permute-start.4
  552.1 290.9 %reduce-scatter.7.cloned.1.call-start = ((), (), s32[]{:S(2)}) async-start(), calls=%async_computation.10 | async-start | bytes 10948608
  578.5 13.6 %collective-permute-start.5 = (f32[1,768]{1,0:T(1,128)}, f32[1,768]{1,0:T(1,128)}, u32[]{:S(2)}, u32[]{:S(2)}) collective-permute-start(f32[1,768]{1,0:T(1,128)} %split.57), channel_id=1, source_target_pairs={{1,0},{2,1},{3,2},{5,4},{6,5},{7,6},{9,8},{10,9},{11,10},{13,12},{... | collective-permute-start | bytes 9224 | tf_op jit(solution)/shard_map/ppermute | solution.py:1106
  604.0 3.7 collective-permute-start.6
  630.4 3.1 collective-permute-start.7
  637.5 19.4 %all-to-all-start.2 = ((bf16[32,24,256]{2,1,0:T(8,128)(2,1)}), bf16[32,24,256]{2,1,0:T(8,128)(2,1)}, u32[]{:S(2)}, u32[]{:S(2)}) async-start(bf16[32,24,256]{2,1,0:T(8,128)(2,1)} %bitcast.576), calls=%async_computation.2 | async-start | bytes 786432 | tf_op jit(solution)/shard_map/all_to_all | solution.py:1587
  656.9 224.3 %all-to-all-start.3 = ((bf16[8,96,1584]{2,1,0:T(8,128)(2,1)}), bf16[8,96,1584]{2,1,0:T(8,128)(2,1)S(1)}, u32[]{:S(2)}, u32[]{:S(2)}) async-start(bf16[8,96,1584]{2,1,0:T(8,128)(2,1)} %bitcast.574), calls=%async_computation.4 | async-start | bytes 5111808 | tf_op jit(solution)/shard_map/all_to_all | solution.py:1550
  674.0 136.5 %copy-start.5 = (s32[8192]{0:T(1024)S(1)}, s32[8192]{0:T(1024)}, u32[]{:S(2)}) copy-start(s32[8192]{0:T(1024)} %param.29) | copy-start | bytes 98308
  (272 other events, 1696.1 us)
Sparse Core Ops, SparseCore 0:
  11.5 81.6 all-gather.16
  96.1 76.2 all-gather.12
  175.3 94.8 all-gather.14
  552.2 106.8 reduce-scatter.4
  666.0 175.5 reduce-scatter.6

commit v4 on v3

--- a/solution.py
+++ b/solution.py
@@ -534,7 +534,7 @@
         + [pltpu.VMEM((m, hops + 1, 2, r, w), bf) for m, r, w in flat_dims] * 3
         + [pltpu.VMEM((m, hops + 1, r, w), bf) for m, r, w in flat_dims]
         + [pltpu.SemaphoreType.DMA((n_send,)), pltpu.SemaphoreType.DMA((n_send,)), pltpu.SemaphoreType.DMA((n_local,))],
-        compiler_params=pltpu.CompilerParams(collective_id=collective_id, has_side_effects=True, vmem_limit_bytes=50 << 20),
+        compiler_params=pltpu.CompilerParams(collective_id=collective_id, has_side_effects=True, vmem_limit_bytes=60 << 20),
     )(*views)
     return list(lax.optimization_barrier(outs))
 
@@ -589,17 +589,18 @@
     return jnp.maximum(left, right) + jnp.log(1.0 + jnp.exp(-jnp.abs(left - right)))
 
 
-def head_forward(rows_all, head_cols, local_ids, tile, sub):
+def head_forward(rows_all, head_cols, masked, local_ids, tile, sub):
     tokens, features = rows_all.shape
     width = head_cols.shape[1]
 
-    def kernel(rows_ref, head_ref, ids_ref, p_ref, stats_ref):
+    def kernel(rows_ref, head_ref, masked_ref, ids_ref, p_ref, stats_ref):
         ids = jnp.transpose(jnp.broadcast_to(ids_ref[...], (128, tile)))[:, :1]
         lane = lax.broadcasted_iota(jnp.int32, (sub, 128), 1)
         column = lax.broadcasted_iota(jnp.int32, (sub, width), 1)
         for part in range(tile // sub):
             here = slice(part * sub, (part + 1) * sub)
             logits = jnp.dot(rows_ref[here, :], head_ref[...], preferred_element_type=jnp.float32)
+            logits = logits + masked_ref[...]
             top = jnp.max(logits, axis=1, keepdims=True)
             picked = jnp.sum(jnp.where(column == ids[here], logits, 0.0), axis=1, keepdims=True)
             lifted = jnp.exp(logits - top)
@@ -618,6 +619,7 @@
         in_specs=[
             pl.BlockSpec((tile, features), lambda i: (i, 0)),
             pl.BlockSpec((features, width), lambda i: (0, 0)),
+            pl.BlockSpec((1, width), lambda i: (0, 0)),
             pl.BlockSpec((1, tile), lambda i: (0, i)),
         ],
         out_specs=[
@@ -625,7 +627,7 @@
             pl.BlockSpec((8, tile), lambda i: (0, i)),
         ],
         compiler_params=pltpu.CompilerParams(vmem_limit_bytes=50 << 20),
-    )(rows_all, head_cols, local_ids[None])
+    )(rows_all, head_cols, masked, local_ids[None])
 
 
 def head_backward(lifted, rows_all, head_cols, local_ids, factors, tile, sub):
@@ -1050,18 +1052,12 @@
     ]
 
 
-def scatter_joined(tensors):
-    square, expand, shrink = tensors
-    width = square.shape[2]
-    cut = [expand[:, :, k : k + width] for k in range(0, expand.shape[2], width)]
-    both = lax.psum_scatter(
-        jnp.concatenate([square] + cut), BOTH, scatter_dimension=1, tiled=True
-    ).astype(jnp.float32)
-    count = square.shape[0]
+def gradient_portions(square, expand, shrink):
     return [
-        both[:count],
-        jnp.concatenate([both[k : k + 1] for k in range(count, both.shape[0])], axis=2),
-        lax.psum_scatter(shrink, BOTH, scatter_dimension=1, tiled=True).astype(jnp.float32),
+        [(1, 0, 1, 0, 2 * expand), (0, 0, 1, 0, 2 * square)],
+        [(2, 0, 1, 0, 2 * shrink), (4, 0, 1, 0, 2 * square)],
+        [(0, 1, 5, 0, 2 * square)],
+        [(4, 1, 5, 0, 2 * square), (3, 0, 1, 0, 2 * square)],
     ]
 
 
@@ -1097,6 +1093,7 @@
 param_stride = 11
 head_tile = 1024
 embed_block = 1024
+far_below = -1e30
 scan_block = 256
 
 
@@ -1428,6 +1425,33 @@
     return (weights - step_rate * moved, first_new, second_new)
 
 
+def adam_columns(weights, pieces, first, second, scale, slot):
+    rows, columns = weights.shape
+    width = pieces.shape[2]
+
+    def kernel(w_ref, g_ref, first_ref, second_ref, scale_ref, w_out, first_out, second_out):
+        gradient = g_ref[0].astype(jnp.float32) * scale_ref[0]
+        w_out[...], first_out[...], second_out[...] = adam_update(
+            w_ref[...], gradient, first_ref[...], second_ref[...], LEARN_RATES[slot], DECAY_FLAGS[slot]
+        )
+
+    block = pl.BlockSpec((rows, width), lambda i: (0, i))
+    return pl.pallas_call(
+        kernel,
+        grid=(-(-columns // width),),
+        out_shape=[jax.ShapeDtypeStruct(weights.shape, jnp.float32)] * 3,
+        in_specs=[
+            block,
+            pl.BlockSpec((1, rows, width), lambda i: (i, 0, 0)),
+            block,
+            block,
+            pl.BlockSpec(memory_space=pltpu.SMEM),
+        ],
+        out_specs=[block] * 3,
+        compiler_params=pltpu.CompilerParams(vmem_limit_bytes=40 << 20),
+    )(weights, pieces, first, second, scale[None])
+
+
 def per_device(
     token_ids,
     targets,
@@ -1511,18 +1535,23 @@
     normed, norm_pull_last = jax.vjp(layer_norm, stream, global_params[2], global_params[3])
     dp_count = lax.axis_size("dp")
     features, vocab_own = head_table.shape
-    vocab_part = vocab_own // dp_count
-    head_cut = head_table.astype(jnp.bfloat16).reshape(features, dp_count, vocab_part)
+    vocab_part = -(-vocab_own // (dp_count * 128)) * 128
+    head_cut = jnp.pad(
+        head_table.astype(jnp.bfloat16), ((0, 0), (0, dp_count * vocab_part - vocab_own))
+    ).reshape(features, dp_count, vocab_part)
     head_cols = lax.all_to_all(
         head_cut.transpose(1, 0, 2), "dp", split_axis=0, concat_axis=0, tiled=True
     ).reshape(dp_count * features, vocab_part)
+    valid = jnp.clip(vocab_own - lax.axis_index("dp") * vocab_part, 0, vocab_part)
+    masked = jnp.where(jnp.arange(vocab_part) < valid, 0.0, far_below)[None]
     own_rows = normed.shape[0]
     rows_all = gather_rows([normed[None]], row_portions(own_rows), 10)[0][0]
     all_targets, all_mask = marks_of(fetched[0][4])
     first_column = lax.axis_index("seq") * vocab_own + lax.axis_index("dp") * vocab_part
     local_ids = all_targets - first_column
+    local_ids = jnp.where(local_ids < valid, local_ids, -1)
     tile = min(head_tile, total_tokens)
-    lifted, stats = head_forward(rows_all, head_cols, local_ids, tile, tile // 4)
+    lifted, stats = head_forward(rows_all, head_cols, masked, local_ids, tile, tile // 4)
     own_log = stats[0] + jnp.log(stats[1])
     log_total = exchange_everywhere(own_log.reshape(-1, 128), add_logs, 13).reshape(-1)
     counted = all_mask.astype(jnp.float32)
@@ -1546,21 +1575,13 @@
             lifted, rows_all, head_cols, local_ids, factors, tile, tile // 2
         )
         d_normed = scatter_plain([d_rows[None]])[0][0]
-    g_head = (
-        lax.all_to_all(
-            grad_head.reshape(dp_count, features, vocab_part),
-            "dp",
-            split_axis=0,
-            concat_axis=0,
-            tiled=True,
-        )
-        .transpose(1, 0, 2)
-        .reshape(features, vocab_own)
-        .astype(jnp.float32)
+    g_head = lax.all_to_all(
+        grad_head.reshape(dp_count, features, vocab_part), "dp", split_axis=0, concat_axis=0, tiled=True
     )
     d_stream, d_gain_last, d_bias_last = norm_pull_last(d_normed)
     layer_grads = [None] * layers
     vector_grads = [None] * layers
+    later_squares = []
     d_embedded = d_stream
     for layer_id in reversed(range(layers)):
         d_stream, grads = layer_backward(d_stream, saved_layers[layer_id], blocks[layer_id])
@@ -1579,11 +1600,16 @@
             )
             low_grads.append(as_rows(all_vectors).astype(jnp.bfloat16))
         if layer_id > 0:
-            layer_grads[layer_id] = scatter_joined(low_grads)
-        else:
-            layer_grads[layer_id] = scatter_rows(
-                low_grads, weight_portions(square_own, expand_own, shrink_own, square_own), layers
-            )
+            layer_grads[layer_id] = [None] + scatter_plain(low_grads[1:])
+            later_squares.append(low_grads[0])
+    summed = scatter_rows(
+        low_grads + later_squares,
+        gradient_portions(square_own, expand_own, shrink_own),
+        layers,
+    )
+    layer_grads[0] = summed[:4]
+    for layer_id, square_sum in zip(reversed(range(1, layers)), summed[4:]):
+        layer_grads[layer_id][0] = square_sum
     back_columns = lax.all_to_all(
         d_embedded.T.astype(jnp.bfloat16), ("dp", "seq"), split_axis=0, concat_axis=1, tiled=True
     )
@@ -1630,8 +1656,9 @@
             LEARN_RATES[slot],
             DECAY_FLAGS[slot],
         )
-        for slot in range(6)
+        for slot in range(5)
     ]
+    updated.append(adam_columns(head_table, g_head, head_first, head_second, scale, 5))
     return (
         loss_sum,
         grad_norm,

time: 943 us -> 911 us (0.966)
  other arithmetic: 108 us -> 77.5 us
  Pallas kernels: 517 us -> 533 us
  local copies, waits for them, and re-layouts: 119 us -> 106 us
    pallas_call x0 -> x1, Pallas kernels: none -> 11.2 us  [adam_columns(): pl.pallas_call(kernel, grid=(-(-columns // width),), out_shape=[jax.Shape...]
    mul x2 -> x0, local copies, waits for them, and re-layouts: 11 us -> none  [per_device(): gradients[slot] * scale]
    sub x6 -> x5, other arithmetic: 28.6 us -> 18.7 us  [adam_update(): return (weights - step_rate * moved, first_new, second_new)]
    unnamed x572 -> x503, local copies, waits for them, and re-layouts: 32.9 us -> 39.7 us
  transfers between devices with their start and end apart: 17 -> 17, of which waited for: 5 -> 5; matrix products, arithmetic and copies ran while one was open for 25% -> 24% of each run, Pallas kernels for 38% -> 39%
where the time goes in v4:
time: 911 us; the launch traced here: 901 us
  Pallas kernels  533 us (59%)
  local copies, waits for them, and re-layouts  106 us (12%)
  matrix products  81.6 us (9%)
  other arithmetic  77.5 us (9%)
  starting transfers between devices  42.7 us (5%)
  between operations  26.5 us (3%)
  blocking collectives  26.2 us (3%)
    pallas_call x2, Pallas kernels, gather_blocks(): pl.pallas_call(kernel, out_shape=[jax.ShapeDtypeStruct((m, hops + 1, 2, 2...  169 us
    pallas_call x1, Pallas kernels, scatter_blocks(): pl.pallas_call(kernel, out_shape=[jax.ShapeDtypeStruct((m, r, w), jnp.flo...  137 us
    pallas_call x1, Pallas kernels, head_backward_scattered(): pl.pallas_call(kernel, out_shape=[jax.ShapeDtypeStruct((rows, features),...  111 us
    unnamed x503, local copies, waits for them, and re-layouts  39.7 us
    pallas_call x1, Pallas kernels, head_forward(): pl.pallas_call(kernel, grid=(tokens // tile,), out_shape=[jax.ShapeDtypeS...  38.6 us
    pallas_call x2, Pallas kernels, exchange_everywhere(): pl.pallas_call(kernel, out_shape=jax.ShapeDtypeStruct(value.shape, jnp.fl...  37.8 us
    dot_general x14, matrix products, matmul(): return jnp.dot(left, right, preferred_element_type=jnp.float32)  34.9 us
    gather x2, local copies, waits for them, and re-layouts, per_device(): columns = jnp.take(embed_table.astype(jnp.bfloat16), token_ids, axis=1)  29.2 us
  transfers between devices with their start and end apart: 17, of which 5 were waited for; matrix products, arithmetic and copies ran while one was open for 24% of the time, Pallas kernels for 39%

profile of v4, /device:TPU:0, one launch (start us, length us, event | category | flops | bytes accessed | tf_op | source)
XLA Modules:
  0.0 901.4 jit_solution(3726607487366330172)
XLA Ops:
  13.3 8.6 copy.65
  21.9 28.4 %gather_fusion = bf16[8192,24]{1,0:T(8,128)(2,1)S(1)} fusion(bf16[24,50688]{0,1:T(8,128)(2,1)} %copy.65, s32[8192]{0:T(1024)S(1)} %fusion.85), kind=kCustom, calls=%fused_computation | custom fusion | bytes 819200 | tf_op jit(solution)/shard_map/jit(_take)/gather | solution.py:1526
  52.0 7.2 all-to-all-start
  63.6 106.1 %shard_map.356 = (bf16[5,4,2,2,48,768]{5,4,3,2,1,0:T(8,128)(2,1)}, bf16[1,4,2,2,48,3072]{5,4,3,2,1,0:T(8,128)(2,1)S(1)}, bf16[1,4,2,2,192,768]{5,4,3,2,1,0:T(8,1...) custom-call(f32[5,24,768]{2,1,0:T(8,128)S(1)} %slice_bitcast_fusion.15.refs_0_, ...), custom_call_target="tpu_custom_call" | custom-call | tf_op jit(solution)/shard_map/pallas_call | solution.py:258
  182.2 5.3 fusion.152
  207.7 5.4 all-gather.5
  240.1 8.0 all-gather.6
  249.3 4.6 multiply_convert_fusion.8
  262.5 5.5 fusion.12
  271.6 4.7 fusion.4
  280.4 62.4 %shard_map.357 = bf16[1,4,2,2,512,768]{5,4,3,2,1,0:T(8,128)(2,1)S(1)} custom-call(f32[1,256,768]{2,1,0:T(8,128)S(1)} %add_bitcast_fusion.refs_0_), custom_call_target="tpu_custom_call" | custom-call | tf_op jit(solution)/shard_map/pallas_call | solution.py:258
  342.8 4.5 copy-done
  347.3 38.6 %shard_map.358 = (bf16[8192,1664]{1,0:T(8,128)(2,1)}, f32[8,8192]{1,0:T(8,128)S(1)}) custom-call(bf16[8192,768]{1,0:T(8,128)(2,1)} %bitcast.491, bf16[768,1664]{1,0:T(8,128)(2,1)S(1)} %bitcast.493, f32[1,1664]{1,0:T(1,128)S(1)} %compare_select_fusion.2.masked_ref, s32[1,8192]{1,0:T(1,128)S(1)} %compare_select_fusion.ids_ref), custom_call_target="tpu_custom_call" | custom-call | tf_op jit(solution)/shard_map/pallas_call | solution.py:612
  386.6 16.7 %shard_map.359 = f32[64,128]{1,0:T(8,128)} custom-call(f32[64,128]{1,0:T(8,128)} %bitcast.562), custom_call_target="tpu_custom_call" | custom-call | tf_op jit(solution)/shard_map/pallas_call | solution.py:573
  405.5 111.2 %shard_map.360 = (f32[256,768]{1,0:T(8,128)}, bf16[768,1664]{1,0:T(8,128)(2,1)}, f32[8,1664]{1,0:T(8,128)}) custom-call(bf16[4,2,2,512,1664]{4,3,2,1,0:T(8,128)(2,1)} %bitcast.512, bf16[4,2,2,512,768]{4,3,2,1,0:T(8,128)(2,1)} %bitcast.492, bf16[768,1664]{1,0:T(8,128)(2,1)} %bitcast.494, s32[1,8192]{1,0:T(1,128)} %copy-done.5, ...), custom_call_target="tpu_custom_call" | custom-call | tf_op jit(solution)/shard_map/pallas_call | solution.py:918
  533.1 4.4 fusion.6
  561.0 6.0 all-gather.7
  607.2 6.8 all-gather.8
  638.7 137.3 %shard_map.362 = (f32[5,24,768]{2,1,0:T(8,128)}, f32[1,24,3072]{2,1,0:T(8,128)}, f32[1,96,768]{2,1,0:T(8,128)}, f32[1,24,256]{2,1,0:T(8,128)}, f32[5,24,768]{2,1,0:T(8,128)}) custom-call(bf16[5,4,2,2,48,768]{5,4,3,2,1,0:T(8,128)(2,1)} %constant_dynamic-update-slice_fusion.refs_0_, bf16[1,4,2,2,48,3072]{5,4,3,2,1,0:T(8,128)(2,1)} %bitcast.513, ...), custom_call_target="tpu_custom_call" | custom-call | tf_op jit(solution)/shard_map/pallas_call | solution.py:526
  779.3 11.1 %all-to-all-start.3 = ((bf16[8,96,1664]{2,1,0:T(8,128)(2,1)}), bf16[8,96,1664]{2,1,0:T(8,128)(2,1)S(1)}, u32[]{:S(2)}, u32[]{:S(2)}) async-start(bf16[8,96,1664]{2,1,0:T(8,128)(2,1)} %bitcast.551), calls=%async_computation.5 | async-start | bytes 5111808 | tf_op jit(solution)/shard_map/all_to_all | solution.py:1578
  790.4 28.1 %shard_map.361 = (f32[24,400,128]{2,1,0:T(8,128)}, f32[8,128]{1,0:T(8,128)S(1)}) custom-call(bf16[24,8192]{1,0:T(8,128)(2,1)S(1)} %bitcast.501, s32[1,8192]{1,0:T(1,128)S(1)} %bitcast.502), custom_call_target="tpu_custom_call" | custom-call | tf_op jit(solution)/shard_map/pallas_call | solution.py:991
  828.8 21.1 %shard_map.363 = f32[8,128]{1,0:T(8,128)} custom-call(f32[8,128]{1,0:T(8,128)} %broadcast_in_dim.323.in_ref), custom_call_target="tpu_custom_call" | custom-call | tf_op jit(solution)/shard_map/pallas_call | solution.py:573
  855.7 10.9 %multiply_subtract_fusion = (f32[24,50688]{1,0:T(8,128)}, f32[24,50688]{1,0:T(8,128)}, f32[24,50688]{1,0:T(8,128)}) fusion(f32[24,50688]{1,0:T(8,128)S(1)} %bitcast.516, f32[3,8,396,128]{3,2,1,0:T(8,128)S(1)} %bitcast.514, f32[24,50688]{1,0:T(8,128)} %param.42, f32[24,50688]{1,0:T(8,128)} %param.48), kind=kLoop, calls=%fused_computation.10 | loop fusion | flops 18247680 | bytes 34062336 | tf_op jit(solution)/shard_map/sub | solution.py:1425
  881.0 11.2 %shard_map.364 = (f32[96,12672]{1,0:T(8,128)}, f32[96,12672]{1,0:T(8,128)}, f32[96,12672]{1,0:T(8,128)}) custom-call(f32[96,12672]{1,0:T(8,128)S(1)} %copy-done.2, bf16[8,96,1664]{2,1,0:T(8,128)(2,1)S(1)} %all-to-all-done.3.g_ref, f32[96,12672]{1,0:T(8,128)S(1)} %copy-done.4, f32[96,12672]{1,0:T(8,128)} %second_ref.1, f32[1]{0:T(128)} %bitcast.106.scale_ref), custom_call_target="tpu_custom_call" | custom-call | tf_op jit(solution)/shard_map/pallas_call | solution.py:1439
  (814 shorter events, 220.7 us)
Async XLA Ops:
  7.2 228.0 %all-gather.17.cloned.1.call-start = ((), (), s32[]{:S(2)}) async-start(), calls=%async_computation.10 | async-start | bytes 6082560 | tf_op jit(solution)/shard_map/all_gather | solution.py:1038
  8.9 252.8 %all-gather.13.cloned.1.call-start = ((), (), s32[]{:S(2)}) async-start(), calls=%async_computation.6 | async-start | bytes 4866048 | tf_op jit(solution)/shard_map/all_gather | solution.py:1038
  21.9 37.4 %copy-start.79 = (f32[2,96,768]{2,1,0:T(8,128)S(1)}, f32[2,96,768]{2,1,0:T(8,128)}, u32[]{:S(2)}) copy-start(f32[2,96,768]{2,1,0:T(8,128)} %param.34) | copy-start | bytes 1769476
  52.0 135.6 %all-to-all-start = ((bf16[24,32,256]{2,0,1:T(8,128)(2,1)}), bf16[24,32,256]{2,0,1:T(8,128)(2,1)S(1)}, u32[]{:S(2)}, u32[]{:S(2)}) async-start(bf16[24,32,256]{2,0,1:T(8,128)(2,1)} %broadcast_select_fusion), calls=%async_computation | async-start | bytes 786432 | tf_op jit(solution)/shard_map/all_to_all | solution.py:1527
  59.2 212.4 %all-gather.15.cloned.1.call-start = ((), (), s32[]{:S(2)}) async-start(), calls=%async_computation.7 | async-start | bytes 4866048 | tf_op jit(solution)/shard_map/all_gather | solution.py:1038
  181.6 40.2 %copy-start.116 = (f32[768]{0:T(1024)}, f32[768]{0:T(1024)S(1)}, u32[]{:S(2)}) copy-start(f32[768]{0:T(1024)S(1)} %get-tuple-element.644) | copy-start | bytes 9220
  181.6 51.3 %copy-start.118 = (f32[768]{0:T(1024)}, f32[768]{0:T(1024)S(1)}, u32[]{:S(2)}) copy-start(f32[768]{0:T(1024)S(1)} %get-tuple-element.640) | copy-start | bytes 9220
  187.6 159.7 %all-to-all-start.1 = ((bf16[8,96,1664]{2,1,0:T(8,128)(2,1)}), bf16[8,96,1664]{2,1,0:T(8,128)(2,1)S(1)}, u32[]{:S(2)}, u32[]{:S(2)}) async-start(bf16[8,96,1664]{2,1,0:T(8,128)(2,1)} %bitcast.534), calls=%async_computation.1 | async-start | bytes 5111808 | tf_op jit(solution)/shard_map/all_to_all | solution.py:1542
  191.2 629.8 %reduce-scatter.3.cloned.1.call-start = ((), (), s32[]{:S(2)}) async-start(), calls=%async_computation.8 | async-start | bytes 4866048 | tf_op jit(solution)/shard_map/reduce_scatter | solution.py:1051
  198.3 3.7 collective-permute-start
  218.7 3.1 collective-permute-start.1
  221.0 126.3 %copy-start.5 = (s32[1,8192]{1,0:T(1,128)}, s32[1,8192]{1,0:T(1,128)S(1)}, u32[]{:S(2)}) copy-start(s32[1,8192]{1,0:T(1,128)S(1)} %compare_select_fusion.ids_ref) | copy-start | bytes 98308
  228.5 4.4 collective-permute-start.2
  256.9 3.0 collective-permute-start.3
  347.3 38.6 %copy-start.1 = (bf16[8,96,1664]{2,1,0:T(8,128)(2,1)}, bf16[8,96,1664]{2,1,0:T(8,128)(2,1)S(1)}, u32[]{:S(2)}) copy-start(bf16[8,96,1664]{2,1,0:T(8,128)(2,1)S(1)} %all-to-all-done.1) | copy-start | bytes 7667716
  405.5 111.2 %copy-start.30 = (f32[256,768]{1,0:T(8,128)S(1)}, f32[256,768]{1,0:T(8,128)}, u32[]{:S(2)}) copy-start(f32[256,768]{1,0:T(8,128)} %copy-done.29) | copy-start | bytes 2359300
  531.3 292.2 %reduce-scatter.5.cloned.1.call-start = ((), (), s32[]{:S(2)}) async-start(), calls=%async_computation.9 | async-start | bytes 4866048 | tf_op jit(solution)/shard_map/reduce_scatter | solution.py:1051
  540.3 14.2 %collective-permute-start.4 = (f32[1,768]{1,0:T(1,128)}, f32[1,768]{1,0:T(1,128)}, u32[]{:S(2)}, u32[]{:S(2)}) collective-permute-start(f32[1,768]{1,0:T(1,128)} %split.53), channel_id=1, source_target_pairs={{1,0},{2,1},{3,2},{5,4},{6,5},{7,6},{9,8},{10,9},{11,10},{13,12},{... | collective-permute-start | bytes 9224 | tf_op jit(solution)/shard_map/ppermute | solution.py:1103
  573.6 8.1 collective-permute-start.5
  598.6 3.9 collective-permute-start.6
  619.6 8.4 collective-permute-start.7
  631.0 148.2 %all-to-all-start.2 = ((bf16[32,24,256]{2,1,0:T(8,128)(2,1)}), bf16[32,24,256]{2,1,0:T(8,128)(2,1)S(1)}, u32[]{:S(2)}, u32[]{:S(2)}) async-start(bf16[32,24,256]{2,1,0:T(8,128)(2,1)} %bitcast.45), calls=%async_computation.2 | async-start | bytes 786432 | tf_op jit(solution)/shard_map/all_to_all | solution.py:1613
  779.3 42.7 %copy-start.95 = (f32[1,24,3072]{2,1,0:T(8,128)S(1)}, f32[1,24,3072]{2,1,0:T(8,128)}, u32[]{:S(2)}) copy-start(f32[1,24,3072]{2,1,0:T(8,128)} %get-tuple-element.482) | copy-start | bytes 884740
  779.3 97.0 %all-to-all-start.3 = ((bf16[8,96,1664]{2,1,0:T(8,128)(2,1)}), bf16[8,96,1664]{2,1,0:T(8,128)(2,1)S(1)}, u32[]{:S(2)}, u32[]{:S(2)}) async-start(bf16[8,96,1664]{2,1,0:T(8,128)(2,1)} %bitcast.551), calls=%async_computation.5 | async-start | bytes 5111808 | tf_op jit(solution)/shard_map/all_to_all | solution.py:1578
  (238 other events, 1079.0 us)
Sparse Core Ops, SparseCore 0:
  11.5 82.4 all-gather.16
  96.9 75.5 all-gather.12
  176.0 95.5 all-gather.14
  531.4 104.6 reduce-scatter.2
  642.9 125.7 reduce-scatter.4

commit v5 on v4

--- a/solution.py
+++ b/solution.py
@@ -1052,12 +1052,20 @@
     ]
 
 
+def scatter_joined(square, expand, shrink):
+    width, count = square.shape[2], square.shape[0]
+    cut = [expand[:, :, k : k + width] for k in range(0, expand.shape[2], width)]
+    shrink_sum, both = scatter_plain([shrink, jnp.concatenate([square] + cut)])
+    wide = jnp.concatenate([both[k : k + 1] for k in range(count, both.shape[0])], axis=2)
+    return [both[:count], wide, shrink_sum]
+
+
 def gradient_portions(square, expand, shrink):
     return [
         [(1, 0, 1, 0, 2 * expand), (0, 0, 1, 0, 2 * square)],
         [(2, 0, 1, 0, 2 * shrink), (4, 0, 1, 0, 2 * square)],
-        [(0, 1, 5, 0, 2 * square)],
-        [(4, 1, 5, 0, 2 * square), (3, 0, 1, 0, 2 * square)],
+        [(0, 1, 4, 0, 2 * square)],
+        [(0, 4, 5, 0, 2 * square), (4, 1, 3, 0, 2 * square), (3, 0, 1, 0, 2 * square)],
     ]
 
 
@@ -1094,6 +1102,7 @@
 head_tile = 1024
 embed_block = 1024
 far_below = -1e30
+joined = 2
 scan_block = 256
 
 
@@ -1600,8 +1609,9 @@
             )
             low_grads.append(as_rows(all_vectors).astype(jnp.bfloat16))
         if layer_id > 0:
-            layer_grads[layer_id] = [None] + scatter_plain(low_grads[1:])
-            later_squares.append(low_grads[0])
+            layer_grads[layer_id] = scatter_joined(low_grads[0][:joined], *low_grads[1:])
+            later_squares.append(low_grads[0][joined:])
+    low_grads, g_head = lax.optimization_barrier((low_grads, g_head))
     summed = scatter_rows(
         low_grads + later_squares,
         gradient_portions(square_own, expand_own, shrink_own),
@@ -1609,7 +1619,7 @@
     )
     layer_grads[0] = summed[:4]
     for layer_id, square_sum in zip(reversed(range(1, layers)), summed[4:]):
-        layer_grads[layer_id][0] = square_sum
+        layer_grads[layer_id][0] = jnp.concatenate([layer_grads[layer_id][0], square_sum])
     back_columns = lax.all_to_all(
         d_embedded.T.astype(jnp.bfloat16), ("dp", "seq"), split_axis=0, concat_axis=1, tiled=True
     )

time: 911 us -> 926 us (1.016)
  blocking collectives: 26.2 us -> 47.6 us
  local copies, waits for them, and re-layouts: 106 us -> 92.3 us
  starting transfers between devices: 42.7 us -> 33.1 us
    all_to_all x0 -> x1, blocking collectives: none -> 20.5 us  [per_device(): lax.all_to_all(d_embedded.T.astype(jnp.bfloat16), ('dp', 'seq'), split_ax...]
    pallas_call x1, Pallas kernels: 137 us -> 148 us  [scatter_blocks(): pl.pallas_call(kernel, out_shape=[jax.ShapeDtypeStruct((m, r, w), jnp.flo...]
    unnamed x503 -> x555, local copies, waits for them, and re-layouts: 39.7 us -> 28.9 us
  transfers between devices with their start and end apart: 17 -> 16, of which waited for: 5 -> 7; matrix products, arithmetic and copies ran while one was open for 24% -> 21% of each run, Pallas kernels for 39% -> 38%
where the time goes in v5:
time: 926 us; the launch traced here: 915 us
  Pallas kernels  538 us (58%)
  local copies, waits for them, and re-layouts  92.3 us (10%)
  matrix products  86.6 us (9%)
  other arithmetic  81.5 us (9%)
  blocking collectives  47.6 us (5%)
  starting transfers between devices  33.1 us (4%)
  between operations  26.6 us (3%)
  waiting for transfers between devices  9.78 us (1%)
    pallas_call x2, Pallas kernels, gather_blocks(): pl.pallas_call(kernel, out_shape=[jax.ShapeDtypeStruct((m, hops + 1, 2, 2...  168 us
    pallas_call x1, Pallas kernels, scatter_blocks(): pl.pallas_call(kernel, out_shape=[jax.ShapeDtypeStruct((m, r, w), jnp.flo...  148 us
    pallas_call x1, Pallas kernels, head_backward_scattered(): pl.pallas_call(kernel, out_shape=[jax.ShapeDtypeStruct((rows, features),...  111 us
    pallas_call x1, Pallas kernels, head_forward(): pl.pallas_call(kernel, grid=(tokens // tile,), out_shape=[jax.ShapeDtypeS...  38.6 us
    dot_general x14, matrix products, matmul(): return jnp.dot(left, right, preferred_element_type=jnp.float32)  34.9 us
    pallas_call x2, Pallas kernels, exchange_everywhere(): pl.pallas_call(kernel, out_shape=jax.ShapeDtypeStruct(value.shape, jnp.fl...  32 us
    gather x2, local copies, waits for them, and re-layouts, per_device(): columns = jnp.take(embed_table.astype(jnp.bfloat16), token_ids, axis=1)  29.2 us
    unnamed x555, local copies, waits for them, and re-layouts  28.9 us
  transfers between devices with their start and end apart: 16, of which 7 were waited for; matrix products, arithmetic and copies ran while one was open for 21% of the time, Pallas kernels for 38%

profile of v5, /device:TPU:0, one launch (start us, length us, event | category | flops | bytes accessed | tf_op | source)
XLA Modules:
  0.0 915.3 jit_solution(1070239477130269193)
XLA Ops:
  13.3 8.6 copy.65
  21.9 28.4 %gather_fusion = bf16[8192,24]{1,0:T(8,128)(2,1)S(1)} fusion(bf16[24,50688]{0,1:T(8,128)(2,1)} %copy.65, s32[8192]{0:T(1024)S(1)} %fusion.104), kind=kCustom, calls=%fused_computation | custom fusion | bytes 819200 | tf_op jit(solution)/shard_map/jit(_take)/gather | solution.py:1535
  51.9 7.2 all-to-all-start
  65.5 104.8 %shard_map.356 = (bf16[5,4,2,2,48,768]{5,4,3,2,1,0:T(8,128)(2,1)}, bf16[1,4,2,2,48,3072]{5,4,3,2,1,0:T(8,128)(2,1)S(1)}, bf16[1,4,2,2,192,768]{5,4,3,2,1,0:T(8,1...) custom-call(f32[5,24,768]{2,1,0:T(8,128)S(1)} %slice_bitcast_fusion.15.refs_0_, ...), custom_call_target="tpu_custom_call" | custom-call | tf_op jit(solution)/shard_map/pallas_call | solution.py:258
  182.9 5.4 fusion.171
  208.2 5.7 all-gather.5
  241.2 7.8 all-gather.6
  250.2 4.6 multiply_convert_fusion.8
  264.9 5.6 fusion.14
  272.2 4.7 fusion.4
  281.0 62.9 %shard_map.357 = bf16[1,4,2,2,512,768]{5,4,3,2,1,0:T(8,128)(2,1)S(1)} custom-call(f32[1,256,768]{2,1,0:T(8,128)S(1)} %add_bitcast_fusion.refs_0_), custom_call_target="tpu_custom_call" | custom-call | tf_op jit(solution)/shard_map/pallas_call | solution.py:258
  343.9 4.5 copy-done
  348.4 38.6 %shard_map.358 = (bf16[8192,1664]{1,0:T(8,128)(2,1)}, f32[8,8192]{1,0:T(8,128)S(1)}) custom-call(bf16[8192,768]{1,0:T(8,128)(2,1)} %bitcast.529, bf16[768,1664]{1,0:T(8,128)(2,1)S(1)} %bitcast.531, f32[1,1664]{1,0:T(1,128)S(1)} %compare_select_fusion.2.masked_ref, s32[1,8192]{1,0:T(1,128)S(1)} %compare_select_fusion.ids_ref), custom_call_target="tpu_custom_call" | custom-call | tf_op jit(solution)/shard_map/pallas_call | solution.py:612
  387.7 16.8 %shard_map.359 = f32[64,128]{1,0:T(8,128)} custom-call(f32[64,128]{1,0:T(8,128)} %bitcast.599), custom_call_target="tpu_custom_call" | custom-call | tf_op jit(solution)/shard_map/pallas_call | solution.py:573
  406.8 111.3 %shard_map.360 = (f32[256,768]{1,0:T(8,128)}, bf16[768,1664]{1,0:T(8,128)(2,1)}, f32[8,1664]{1,0:T(8,128)}) custom-call(bf16[4,2,2,512,1664]{4,3,2,1,0:T(8,128)(2,1)} %bitcast.554, bf16[4,2,2,512,768]{4,3,2,1,0:T(8,128)(2,1)} %bitcast.530, bf16[768,1664]{1,0:T(8,128)(2,1)} %bitcast.532, s32[1,8192]{1,0:T(1,128)} %copy-done.3, ...), custom_call_target="tpu_custom_call" | custom-call | tf_op jit(solution)/shard_map/pallas_call | solution.py:918
  548.6 6.7 all-gather.7
  587.6 6.9 all-gather.8
  608.0 20.5 %all_to_all.39 = bf16[32,24,256]{2,1,0:T(8,128)(2,1)S(1)} all-to-all(bf16[32,24,256]{2,1,0:T(8,128)(2,1)S(1)} %bitcast.590), channel_id=1, replica_groups=mesh['dp'=8,'seq'=4] {'dp','seq'}, dimensions={0} | all-to-all | bytes 786432 | tf_op jit(solution)/shard_map/all_to_all | solution.py:1623
  628.5 4.7 all-to-all-start.3
  662.1 28.0 %shard_map.361 = (f32[24,400,128]{2,1,0:T(8,128)}, f32[8,128]{1,0:T(8,128)S(1)}) custom-call(bf16[24,8192]{1,0:T(8,128)(2,1)S(1)} %bitcast.543, s32[1,8192]{1,0:T(1,128)S(1)} %bitcast.544), custom_call_target="tpu_custom_call" | custom-call | tf_op jit(solution)/shard_map/pallas_call | solution.py:991
  696.1 148.3 %shard_map.362 = (f32[5,24,768]{2,1,0:T(8,128)}, f32[1,24,3072]{2,1,0:T(8,128)}, f32[1,96,768]{2,1,0:T(8,128)}, f32[1,24,256]{2,1,0:T(8,128)}, f32[3,24,768]{2,1,0:T(8,128)}) custom-call(bf16[5,4,2,2,48,768]{5,4,3,2,1,0:T(8,128)(2,1)} %bitcast.90.refs_0_, bf16[1,4,2,2,48,3072]{5,4,3,2,1,0:T(8,128)(2,1)} %bitcast.560, ...), custom_call_target="tpu_custom_call" | custom-call | tf_op jit(solution)/shard_map/pallas_call | solution.py:526
  855.4 15.2 %shard_map.363 = f32[8,128]{1,0:T(8,128)} custom-call(f32[8,128]{1,0:T(8,128)} %broadcast_in_dim.331.in_ref), custom_call_target="tpu_custom_call" | custom-call | tf_op jit(solution)/shard_map/pallas_call | solution.py:573
  883.2 11.0 %multiply_subtract_fusion = (f32[24,50688]{1,0:T(8,128)}, f32[24,50688]{1,0:T(8,128)}, f32[24,50688]{1,0:T(8,128)}) fusion(f32[24,50688]{1,0:T(8,128)S(1)} %bitcast.557, f32[3,8,396,128]{3,2,1,0:T(8,128)S(1)} %bitcast.555, f32[24,50688]{1,0:T(8,128)} %param.42, f32[24,50688]{1,0:T(8,128)} %param.48), kind=kLoop, calls=%fused_computation.10 | loop fusion | flops 18247680 | bytes 34062336 | tf_op jit(solution)/shard_map/sub | solution.py:1434
  894.2 11.8 %shard_map.364 = (f32[96,12672]{1,0:T(8,128)}, f32[96,12672]{1,0:T(8,128)}, f32[96,12672]{1,0:T(8,128)}) custom-call(f32[96,12672]{1,0:T(8,128)S(1)} %bitcast.534, bf16[8,96,1664]{2,1,0:T(8,128)(2,1)} %all-to-all-done.3.g_ref, f32[96,12672]{1,0:T(8,128)S(1)} %bitcast.542, f32[96,12672]{1,0:T(8,128)} %second_ref.1, f32[1]{0:T(128)} %bitcast.111.scale_ref), custom_call_target="tpu_custom_call" | custom-call | tf_op jit(solution)/shard_map/pallas_call | solution.py:1448
  (873 shorter events, 218.6 us)
Async XLA Ops:
  7.2 229.1 %all-gather.17.cloned.1.call-start = ((), (), s32[]{:S(2)}) async-start(), calls=%async_computation.9 | async-start | bytes 6082560 | tf_op jit(solution)/shard_map/all_gather | solution.py:1038
  8.9 255.9 %all-gather.13.cloned.1.call-start = ((), (), s32[]{:S(2)}) async-start(), calls=%async_computation.6 | async-start | bytes 4866048 | tf_op jit(solution)/shard_map/all_gather | solution.py:1038
  51.9 136.3 %all-to-all-start = ((bf16[24,32,256]{2,0,1:T(8,128)(2,1)}), bf16[24,32,256]{2,0,1:T(8,128)(2,1)S(1)}, u32[]{:S(2)}, u32[]{:S(2)}) async-start(bf16[24,32,256]{2,0,1:T(8,128)(2,1)} %broadcast_select_fusion), calls=%async_computation | async-start | bytes 786432 | tf_op jit(solution)/shard_map/all_to_all | solution.py:1536
  59.2 213.0 %all-gather.15.cloned.1.call-start = ((), (), s32[]{:S(2)}) async-start(), calls=%async_computation.7 | async-start | bytes 4866048 | tf_op jit(solution)/shard_map/all_gather | solution.py:1038
  188.2 160.2 %all-to-all-start.1 = ((bf16[8,96,1664]{2,1,0:T(8,128)(2,1)}), bf16[8,96,1664]{2,1,0:T(8,128)(2,1)S(1)}, u32[]{:S(2)}, u32[]{:S(2)}) async-start(bf16[8,96,1664]{2,1,0:T(8,128)(2,1)} %bitcast.580), calls=%async_computation.1 | async-start | bytes 5111808 | tf_op jit(solution)/shard_map/all_to_all | solution.py:1551
  192.0 653.8 %reduce-scatter.5.cloned.1.call-start = ((), (), s32[]{:S(2)}) async-start(), calls=%async_computation.8 | async-start | bytes 4866048 | tf_op jit(solution)/shard_map/reduce_scatter | solution.py:1051
  199.1 3.5 collective-permute-start
  219.7 3.0 collective-permute-start.1
  222.0 126.5 %copy-start.3 = (s32[1,8192]{1,0:T(1,128)}, s32[1,8192]{1,0:T(1,128)S(1)}, u32[]{:S(2)}) copy-start(s32[1,8192]{1,0:T(1,128)S(1)} %compare_select_fusion.ids_ref) | copy-start | bytes 98308
  228.6 26.3 %copy-start.14 = (f32[256,768]{1,0:T(8,128)}, f32[256,768]{1,0:T(8,128)S(1)}, u32[]{:S(2)}) copy-start(f32[256,768]{1,0:T(8,128)S(1)} %get-tuple-element.741) | copy-start | bytes 2359300
  229.6 4.4 collective-permute-start.2
  258.1 4.3 collective-permute-start.3
  348.4 38.6 %copy-start.1 = (bf16[8,96,1664]{2,1,0:T(8,128)(2,1)}, bf16[8,96,1664]{2,1,0:T(8,128)(2,1)S(1)}, u32[]{:S(2)}) copy-start(bf16[8,96,1664]{2,1,0:T(8,128)(2,1)S(1)} %all-to-all-done.1) | copy-start | bytes 7667716
  348.4 56.1 %copy-start.121 = (f32[1,1,32,256]{3,1,2,0:T(1,128)S(1)}, f32[1,1,32,256]{3,1,2,0:T(1,128)}, u32[]{:S(2)}) copy-start(f32[1,1,32,256]{3,1,2,0:T(1,128)} %copy.82) | copy-start | bytes 98308
  406.8 111.4 %copy-start.28 = (f32[256,768]{1,0:T(8,128)S(1)}, f32[256,768]{1,0:T(8,128)}, u32[]{:S(2)}) copy-start(f32[256,768]{1,0:T(8,128)} %copy-done.27) | copy-start | bytes 2359300
  539.2 3.2 collective-permute-start.4
  540.7 307.8 %reduce-scatter.7.cloned.1.call-start = ((), (), s32[]{:S(2)}) async-start(), calls=%async_computation.10 | async-start | bytes 7299072
  560.5 7.1 collective-permute-start.5
  578.4 3.8 collective-permute-start.6
  601.4 3.2 collective-permute-start.7
  608.0 26.7 %copy-start.132 = (f32[8,1664]{1,0:T(8,128)S(1)}, f32[8,1664]{1,0:T(8,128)}, u32[]{:S(2)}) copy-start(f32[8,1664]{1,0:T(8,128)} %get-tuple-element.484) | copy-start | bytes 159748
  608.0 27.3 %copy-start.117 = (f32[64,128]{1,0:T(8,128)S(1)}, f32[64,128]{1,0:T(8,128)}, u32[]{:S(2)}) copy-start(f32[64,128]{1,0:T(8,128)} %shard_map.359) | copy-start | bytes 98308
  608.0 27.9 %copy-start.61 = (bf16[256,768]{1,0:T(8,128)(2,1)S(1)}, bf16[256,768]{1,0:T(8,128)(2,1)}, u32[]{:S(2)}) copy-start(bf16[256,768]{1,0:T(8,128)(2,1)} %copy-done.60) | copy-start | bytes 1179652
  628.5 66.7 %all-to-all-start.3 = ((bf16[8,96,1664]{2,1,0:T(8,128)(2,1)}), bf16[8,96,1664]{2,1,0:T(8,128)(2,1)}, u32[]{:S(2)}, u32[]{:S(2)}) async-start(bf16[8,96,1664]{2,1,0:T(8,128)(2,1)} %bitcast.588), calls=%async_computation.3 | async-start | bytes 5111808 | tf_op jit(solution)/shard_map/all_to_all | solution.py:1587
  (265 other events, 1238.6 us)
Sparse Core Ops, SparseCore 0:
  11.5 81.0 all-gather.16
  95.5 76.8 all-gather.12
  175.3 96.7 all-gather.14
  540.8 117.2 reduce-scatter.4
  664.5 173.8 reduce-scatter.6
